TPU v7x, 32 devices: a whole 2x2x4 slice. The times are simulated.
32 devices in a mesh: gx: 8 (over z, y), yz: 4 (over x, core).
Axes of the slice: x: 2, y: 2, z: 4, core: 2. Of those that a mesh axis runs over, the one named last changes fastest.
Arguments:
- right_side: float32 [32, 128, 512], P('gx', 'yz'), may hold values from -5 to 5
- phase: int32 [32, 128, 512], P('gx', 'yz'), may hold values 0 or 1
- pressure_guess: float32 [32, 128, 512], P('gx', 'yz'), may hold values from -6 to 6
Outputs:
- pressure: float32 [32, 128, 512], P('gx', 'yz')
- residual: float32 [32, 128, 512], P('gx', 'yz')
All inputs are finite; a program needn't handle non-finite values. No bound on the sum of `phase` on one device may be relied on, other than what follows from the above.
Results may differ from a plain program's by a relative error of at most 0.0003.
Values sent between devices are 32-bit elements; how exact they have to be, the bound alone decides.
No kernel may reach another device: no remote copies, remote signals or barrier semaphores. Data moves between devices by JAX's collectives and lax.ppermute only.
A program may use at most 128 MiB of HBM per device.

v0:
```python
import jax
import jax.numpy as jnp
from jax import lax
from jax.sharding import PartitionSpec as P

SWEEPS = 2
BOTTOM_SWEEPS = 4


def with_halo(x, sides, width):
    for axis, dim in sides:
        size, length = (lax.axis_size(axis), x.shape[dim])
        up = [(i, (i + 1) % size) for i in range(size - 1)]
        down = [(j, i) for i, j in up]
        last = lax.slice_in_dim(x, length - width, length, axis=dim)
        first = lax.slice_in_dim(x, 0, width, axis=dim)
        before = lax.ppermute(last, axis, up)
        after = lax.ppermute(first, axis, down)
        x = jnp.concatenate([before, x, after], axis=dim)
    return x


def harmonic(left, right):
    total = left + right
    safe = jnp.where(total > 0, total, 1.0)
    return jnp.where(total > 0, 2.0 * left * right / safe, 0.0)


def coefficients(padded):
    faces_x = harmonic(padded[1:], padded[:-1])
    faces_y = harmonic(padded[:, 1:], padded[:, :-1])
    centre = padded[1:-1, 1:-1]
    faces_z = harmonic(centre[:, :, 1:], centre[:, :, :-1])
    zero_plane = jnp.zeros_like(centre[:, :, :1])
    x_lower = faces_x[:-1, 1:-1]
    x_upper = faces_x[1:, 1:-1]
    y_lower = faces_y[1:-1, :-1]
    y_upper = faces_y[1:-1, 1:]
    z_lower = jnp.concatenate([zero_plane, faces_z], axis=2)
    z_upper = jnp.concatenate([faces_z, 2.0 * centre[:, :, -1:]], axis=2)
    diagonal = x_lower + x_upper + y_lower + y_upper + z_lower + z_upper
    diagonal = jnp.where(diagonal > 0, diagonal, 1.0)
    return (x_lower, x_upper, y_lower, y_upper, z_lower, z_upper, diagonal)


def shrink(coeffs):
    return tuple((item[1:-1, 1:-1] for item in coeffs))


def parity_of(extent, start_x, start_y):
    index_x = lax.broadcasted_iota(jnp.int32, extent, 0) + start_x
    index_y = lax.broadcasted_iota(jnp.int32, extent, 1) + start_y
    index_z = lax.broadcasted_iota(jnp.int32, extent, 2)
    return (index_x + index_y + index_z) % 2


def neighbours(padded, coeffs):
    centre = padded[1:-1, 1:-1]
    zero_plane = jnp.zeros_like(centre[:, :, :1])
    lower_z = jnp.concatenate([zero_plane, centre[:, :, :-1]], axis=2)
    upper_z = jnp.concatenate([centre[:, :, 1:], zero_plane], axis=2)
    beside_all = coeffs[0] * padded[:-2, 1:-1] + coeffs[1] * padded[2:, 1:-1]
    beside_all = beside_all + coeffs[2] * padded[1:-1, :-2] + coeffs[3] * padded[1:-1, 2:]
    beside_all = beside_all + coeffs[4] * lower_z + coeffs[5] * upper_z
    return (beside_all, centre)


def colour_pass(padded, source, coeffs, parity, colour):
    beside_all, centre = neighbours(padded, coeffs)
    updated = (source + beside_all) / coeffs[6]
    return jnp.where(parity == colour, updated, centre)


def residual_of(padded, source, coeffs):
    beside_all, centre = neighbours(padded, coeffs)
    return source - (coeffs[6] * centre - beside_all)


def restrict_sum(field):
    size_x, size_y, size_z = field.shape
    return 0.5 * field.reshape(size_x // 2, 2, size_y // 2, 2, size_z // 2, 2).sum(axis=(1, 3, 5))


def restrict_mean(field):
    size_x, size_y, size_z = field.shape
    return 0.125 * field.reshape(size_x // 2, 2, size_y // 2, 2, size_z // 2, 2).sum(axis=(1, 3, 5))


def inject(field):
    return jnp.repeat(jnp.repeat(jnp.repeat(field, 2, axis=0), 2, axis=1), 2, axis=2)


def rim_one(field):
    return with_halo(field, (("gx", 0), ("yz", 1)), 1)


def rim_two(field):
    return with_halo(field, (("gx", 0), ("yz", 1)), 2)


def offsets(field):
    return (lax.axis_index("gx") * field.shape[0], lax.axis_index("yz") * field.shape[1])


def prepare_plain(mobility):
    start_x, start_y = offsets(mobility)
    return (coefficients(rim_one(mobility)), parity_of(mobility.shape, start_x, start_y))


def prepare(mobility):
    start_x, start_y = offsets(mobility)
    size_x, size_y, size_z = mobility.shape
    region = coefficients(rim_two(mobility))
    loop_parity = parity_of((size_x + 2, size_y + 2, size_z), start_x - 1, start_y - 1)
    operator_set = (
        shrink(region),
        parity_of(mobility.shape, start_x, start_y),
        region,
        loop_parity,
    )
    return operator_set


def smooth_plain(field, source, operator_set, sweeps, rim):
    coeffs = operator_set[0]
    parity = operator_set[1]
    for _ in range(sweeps):
        field = colour_pass(rim(field), source, coeffs, parity, 0)
        field = colour_pass(rim(field), source, coeffs, parity, 1)
    return field


def smooth(field, source, operator_set, sweeps):
    interior, parity, region, loop_parity = operator_set
    source_loop = rim_one(source)
    for _ in range(sweeps):
        loop_field = colour_pass(rim_two(field), source_loop, region, loop_parity, 0)
        field = colour_pass(loop_field, source, interior, parity, 1)
    return field


def local(right_side, phase, pressure_guess):
    mobility = 1.0 + 999.0 * phase.astype(jnp.float32)
    level_zero = prepare(mobility)
    pressure = smooth(pressure_guess, right_side, level_zero, SWEEPS)
    fine_res = residual_of(rim_one(pressure), right_side, level_zero[0])
    source_one = restrict_sum(fine_res)
    mobility_one = restrict_mean(mobility)
    level_one = prepare(mobility_one)
    coarse_one = smooth(jnp.zeros_like(source_one), source_one, level_one, SWEEPS)
    res_one = residual_of(rim_one(coarse_one), source_one, level_one[0])
    source_two = restrict_sum(res_one)
    mobility_two = restrict_mean(mobility_one)
    level_two = prepare_plain(mobility_two)
    coarse_two = smooth_plain(
        jnp.zeros_like(source_two), source_two, level_two, BOTTOM_SWEEPS, rim_one
    )
    coarse_one = smooth(coarse_one + inject(coarse_two), source_one, level_one, SWEEPS)
    pressure = smooth(pressure + inject(coarse_one), right_side, level_zero, SWEEPS)
    residual = residual_of(rim_one(pressure), right_side, level_zero[0])
    return (pressure, residual)


def solution(mesh):
    in_specs = (P("gx", "yz", None), P("gx", "yz", None), P("gx", "yz", None))
    out_specs = (P("gx", "yz", None), P("gx", "yz", None))
    return jax.shard_map(local, mesh=mesh, in_specs=in_specs, out_specs=out_specs, check_vma=False)
```

profile of v0, /device:TPU:0, one launch (start us, length us, event | category | flops | bytes accessed | tf_op | source)
XLA Modules:
  0.0 682.0 jit_solution(3072846826854109648)
XLA Ops:
  1.6 18.1 %reshape.169 = f32[2,2,16,2,256,2]{5,4,3,2,1,0:T(8,128)} reshape(f32[4,32,512]{2,1,0:T(8,128)S(1)} %multiply_add_fusion) | data formatting | bytes 524288 | tf_op jit(solution)/shard_map/reshape | solution.py:86
  19.7 7.0 %reduce_sum.43 = f32[2,16,256]{2,1,0:T(8,128)S(1)} reduce(f32[2,2,16,2,256,2]{5,4,3,2,1,0:T(8,128)} %reshape.169, f32[]{:T(128)} %constant.45.clone.1), dimensions={1,3,5}, to_apply=%region_1.2 | reduce | flops 57344 | bytes 294916 | tf_op jit(solution)/shard_map/reduce_sum | solution.py:86
  26.7 5.0 collective-permute-start.20
  40.1 5.0 collective-permute-start.44
  54.8 5.5 collective-permute-start.28
  62.2 5.5 collective-permute-start
  69.6 5.4 collective-permute-start.8
  77.7 4.8 collective-permute-start.4
  100.1 4.9 collective-permute-start.42
  161.3 5.2 collective-permute-start.12
  169.0 20.7 %collective-permute-done.12 = f32[2,32,512]{1,2,0:T(8,128)S(1)} collective-permute-done((f32[2,32,512]{1,2,0:T(8,128)S(1)}, f32[2,32,512]{1,2,0:T(8,128)S(1)}, u32[]{:S(2)}, u32[]{:S(2)}) %collective-permute-start.12) | collective-permute-done | bytes 131104 | tf_op jit(solution)/shard_map/ppermute | solution.py:17
  228.6 4.8 collective-permute-start.16
  259.8 7.4 %fusion.74 = f32[4,32,512]{1,2,0:T(8,128)} fusion(f32[4,32,512]{1,2,0:T(8,128)} %copy.205, f32[1,32,512]{1,2,0:T(8,128)} %collective-permute-done.17, f32[4,32,512]{1,2,0:T(8,128)} %copy-done.8, f32[1,32,512]{1,2,0:T(8,128)} %collective-permute-done.16, f32[4,32,512]{1,2,0:T(8,128)} %get-tuple-element.13, f32[4,32,511]{1,2,0:T(8,128)} %get-tuple-element.45, ...), kind=kLoop, calls=%fused_computation.144 | loop fusion | flops 1048576 | bytes 3954896 | tf_op jit(solution)/shard_map/sub | solution.py:76
  269.5 18.8 %reshape.168 = f32[2,2,16,2,256,2]{5,4,3,2,1,0:T(8,128)} reshape(f32[4,32,512]{2,1,0:T(8,128)} %copy.185) | data formatting | bytes 524288 | tf_op jit(solution)/shard_map/reshape | solution.py:81
  288.3 7.6 %reduce_sum.39 = f32[2,16,256]{2,1,0:T(8,128)} reduce(f32[2,2,16,2,256,2]{5,4,3,2,1,0:T(8,128)} %reshape.168, f32[]{:T(128)} %constant.45.clone.1), dimensions={1,3,5}, to_apply=%region_0.1 | reduce | flops 57344 | bytes 294916 | tf_op jit(solution)/shard_map/reduce_sum | solution.py:81
  296.8 5.0 collective-permute-start.24
  304.0 5.2 collective-permute-done.25
  319.2 4.8 collective-permute-start.32
  361.0 4.6 collective-permute-start.48
  523.9 20.7 %collective-permute-done.84 = f32[2,32,512]{1,2,0:T(8,128)S(1)} collective-permute-done((f32[2,32,512]{1,2,0:T(8,128)S(1)}, f32[2,32,512]{1,2,0:T(8,128)S(1)}, u32[]{:S(2)}, u32[]{:S(2)}) %collective-permute-start.84) | collective-permute-done | bytes 131104 | tf_op jit(solution)/shard_map/ppermute | solution.py:17
  583.9 21.2 %collective-permute-done.88 = f32[2,32,512]{1,2,0:T(8,128)S(1)} collective-permute-done((f32[2,32,512]{1,2,0:T(8,128)S(1)}, f32[2,32,512]{1,2,0:T(8,128)S(1)}, u32[]{:S(2)}, u32[]{:S(2)}) %collective-permute-start.88) | collective-permute-done | bytes 131104 | tf_op jit(solution)/shard_map/ppermute | solution.py:17
  639.7 4.8 collective-permute-start.92
  648.0 7.3 %collective-permute-done.92 = f32[1,32,512]{1,2,0:T(8,128)} collective-permute-done((f32[1,32,512]{1,2,0:T(8,128)}, f32[1,32,512]{1,2,0:T(8,128)}, u32[]{:S(2)}, u32[]{:S(2)}) %collective-permute-start.92) | collective-permute-done | bytes 65568 | tf_op jit(solution)/shard_map/ppermute | solution.py:17
  671.6 7.7 %fusion.51 = f32[4,32,512]{1,2,0:T(8,128)} fusion(f32[4,32,512]{1,2,0:T(8,128)} %copy.205, f32[1,32,512]{1,2,0:T(8,128)} %collective-permute-done.93, f32[4,32,512]{1,2,0:T(8,128)} %copy-done.21, f32[1,32,512]{1,2,0:T(8,128)} %collective-permute-done.92, f32[4,32,512]{1,2,0:T(8,128)} %get-tuple-element.13, f32[4,32,511]{1,2,0:T(8,128)} %get-tuple-element.37, ...), kind=kLoop, calls=%fused_computation.109 | loop fusion | flops 1048576 | bytes 3954896 | tf_op jit(solution)/shard_map/sub | solution.py:76
  (608 shorter events, 471.3 us)
Async XLA Ops:
  26.7 41.6 %collective-permute-start.20 = (f32[2,16,256]{2,1,0:T(8,128)S(1)}, f32[2,16,256]{2,1,0:T(8,128)S(1)}, u32[]{:S(2)}, u32[]{:S(2)}) collective-permute-start(f32[2,16,256]{2,1,0:T(8,128)S(1)} %get-tuple-element.105), channel_id=1, source_target_pairs={{0,4},{4,8},{8,12},{12,16},{16,20},{20,24},{24,28},{1,5},{5,9},{9,... | collective-permute-start | bytes 98312 | tf_op jit(solution)/shard_map/ppermute | solution.py:17
  31.7 37.9 %collective-permute-start.21 = (f32[2,16,256]{2,1,0:T(8,128)S(1)}, f32[2,16,256]{2,1,0:T(8,128)S(1)}, u32[]{:S(2)}, u32[]{:S(2)}) collective-permute-start(f32[2,16,256]{2,1,0:T(8,128)S(1)} %get-tuple-element.105), channel_id=1, source_target_pairs={{4,0},{8,4},{12,8},{16,12},{20,16},{24,20},{28,24},{5,1},{9,5},{13... | collective-permute-start | bytes 98312 | tf_op jit(solution)/shard_map/ppermute | solution.py:18
  34.3 19.2 %collective-permute-start.40 = (f32[1,8,128]{2,1,0:T(8,128)S(1)}, f32[1,8,128]{2,1,0:T(8,128)S(1)}, u32[]{:S(2)}, u32[]{:S(2)}) collective-permute-start(f32[1,8,128]{2,1,0:T(8,128)S(1)} %multiply_bitcast_fusion), channel_id=1, source_target_pairs={{0,4},{4,8},{8,12},{12,16},{16,20},{20,24},{24,28},{1,5},{5,9},{9,... | collective-permute-start | bytes 12296 | tf_op jit(solution)/shard_map/ppermute | solution.py:17
  38.8 16.0 %collective-permute-start.41 = (f32[1,8,128]{2,1,0:T(8,128)S(1)}, f32[1,8,128]{2,1,0:T(8,128)S(1)}, u32[]{:S(2)}, u32[]{:S(2)}) collective-permute-start(f32[1,8,128]{2,1,0:T(8,128)S(1)} %multiply_bitcast_fusion), channel_id=1, source_target_pairs={{4,0},{8,4},{12,8},{16,12},{20,16},{24,20},{28,24},{5,1},{9,5},{13... | collective-permute-start | bytes 12296 | tf_op jit(solution)/shard_map/ppermute | solution.py:18
  40.1 20.7 %collective-permute-start.44 = (f32[1,8,128]{2,1,0:T(8,128)S(1)}, f32[1,8,128]{2,1,0:T(8,128)S(1)}, u32[]{:S(2)}, u32[]{:S(2)}) collective-permute-start(f32[1,8,128]{2,1,0:T(8,128)S(1)} %broadcast.360), channel_id=1, source_target_pairs={{0,4},{4,8},{8,12},{12,16},{16,20},{20,24},{24,28},{1,5},{5,9},{9,... | collective-permute-start | bytes 12296 | tf_op jit(solution)/shard_map/ppermute | solution.py:17
  54.8 20.2 %collective-permute-start.28 = (f32[2,16,256]{2,1,0:T(8,128)S(1)}, f32[2,16,256]{2,1,0:T(8,128)S(1)}, u32[]{:S(2)}, u32[]{:S(2)}) collective-permute-start(f32[2,16,256]{2,1,0:T(8,128)S(1)} %broadcast_in_dim.87), channel_id=1, source_target_pairs={{0,4},{4,8},{8,12},{12,16},{16,20},{20,24},{24,28},{1,5},{5,9},{9,... | collective-permute-start | bytes 98312 | tf_op jit(solution)/shard_map/ppermute | solution.py:17
  60.9 15.5 %collective-permute-start.29 = (f32[2,16,256]{2,1,0:T(8,128)S(1)}, f32[2,16,256]{2,1,0:T(8,128)S(1)}, u32[]{:S(2)}, u32[]{:S(2)}) collective-permute-start(f32[2,16,256]{2,1,0:T(8,128)S(1)} %broadcast_in_dim.87), channel_id=1, source_target_pairs={{4,0},{8,4},{12,8},{16,12},{20,16},{24,20},{28,24},{5,1},{9,5},{13... | collective-permute-start | bytes 98312 | tf_op jit(solution)/shard_map/ppermute | solution.py:18
  62.2 44.6 %collective-permute-start = (f32[2,32,512]{2,1,0:T(8,128)S(1)}, f32[2,32,512]{2,1,0:T(8,128)S(1)}, u32[]{:S(2)}, u32[]{:S(2)}) collective-permute-start(f32[2,32,512]{2,1,0:T(8,128)S(1)} %get-tuple-element.64), channel_id=1, source_target_pairs={{0,4},{4,8},{8,12},{12,16},{16,20},{20,24},{24,28},{1,5},{5,9},{9,... | collective-permute-start | bytes 393224 | tf_op jit(solution)/shard_map/ppermute | solution.py:17
  68.3 39.9 %collective-permute-start.1 = (f32[2,32,512]{2,1,0:T(8,128)S(1)}, f32[2,32,512]{2,1,0:T(8,128)S(1)}, u32[]{:S(2)}, u32[]{:S(2)}) collective-permute-start(f32[2,32,512]{2,1,0:T(8,128)S(1)} %get-tuple-element.65), channel_id=1, source_target_pairs={{4,0},{8,4},{12,8},{16,12},{20,16},{24,20},{28,24},{5,1},{9,5},{13... | collective-permute-start | bytes 393224 | tf_op jit(solution)/shard_map/ppermute | solution.py:18
  69.6 42.3 %collective-permute-start.8 = (f32[2,32,512]{2,1,0:T(8,128)S(1)}, f32[2,32,512]{2,1,0:T(8,128)S(1)}, u32[]{:S(2)}, u32[]{:S(2)}) collective-permute-start(f32[2,32,512]{2,1,0:T(8,128)S(1)} %get-tuple-element.69), channel_id=1, source_target_pairs={{0,4},{4,8},{8,12},{12,16},{16,20},{20,24},{24,28},{1,5},{5,9},{9,... | collective-permute-start | bytes 393224 | tf_op jit(solution)/shard_map/ppermute | solution.py:17
  97.2 16.9 %collective-permute-start.9 = (f32[2,32,512]{2,1,0:T(8,128)}, f32[2,32,512]{2,1,0:T(8,128)S(1)}, u32[]{:S(2)}, u32[]{:S(2)}) collective-permute-start(f32[2,32,512]{2,1,0:T(8,128)} %get-tuple-element.68), channel_id=1, source_target_pairs={{4,0},{8,4},{12,8},{16,12},{20,16},{24,20},{28,24},{5,1},{9,5},{13... | collective-permute-start | bytes 393224 | tf_op jit(solution)/shard_map/ppermute | solution.py:18
  100.1 224.0 %collective-permute-start.42 = (f32[3,1,128]{2,1,0:T(1,128)}, f32[3,1,128]{2,1,0:T(1,128)}, u32[]{:S(2)}, u32[]{:S(2)}) collective-permute-start(f32[3,1,128]{2,1,0:T(1,128)} %get-tuple-element.123), channel_id=1, source_target_pairs={{0,1},{1,2},{2,3},{4,5},{5,6},{6,7},{8,9},{9,10},{10,11},{12,13},{... | collective-permute-start | bytes 4616 | tf_op jit(solution)/shard_map/ppermute | solution.py:17
  106.9 218.5 %collective-permute-start.43 = (f32[3,1,128]{2,1,0:T(1,128)}, f32[3,1,128]{2,1,0:T(1,128)}, u32[]{:S(2)}, u32[]{:S(2)}) collective-permute-start(f32[3,1,128]{2,1,0:T(1,128)} %get-tuple-element.122), channel_id=1, source_target_pairs={{1,0},{2,1},{3,2},{5,4},{6,5},{7,6},{9,8},{10,9},{11,10},{13,12},{... | collective-permute-start | bytes 4616 | tf_op jit(solution)/shard_map/ppermute | solution.py:18
  108.2 251.8 %collective-permute-start.46 = (f32[3,1,128]{2,1,0:T(1,128)}, f32[3,1,128]{2,1,0:T(1,128)}, u32[]{:S(2)}, u32[]{:S(2)}) collective-permute-start(f32[3,1,128]{2,1,0:T(1,128)} %get-tuple-element.124), channel_id=1, source_target_pairs={{0,1},{1,2},{2,3},{4,5},{5,6},{6,7},{8,9},{9,10},{10,11},{12,13},{... | collective-permute-start | bytes 4616 | tf_op jit(solution)/shard_map/ppermute | solution.py:17
  119.2 18.1 %collective-permute-start.10 = (f32[8,2,512]{2,0,1:T(8,128)}, f32[8,2,512]{2,0,1:T(8,128)}, u32[]{:S(2)}, u32[]{:S(2)}) collective-permute-start(f32[8,2,512]{2,0,1:T(8,128)} %copy.216), channel_id=1, source_target_pairs={{0,1},{1,2},{2,3},{4,5},{5,6},{6,7},{8,9},{9,10},{10,11},{12,13},{... | collective-permute-start | bytes 98312 | tf_op jit(solution)/shard_map/ppermute | solution.py:17
  124.9 15.2 %collective-permute-start.11 = (f32[8,2,512]{2,0,1:T(8,128)}, f32[8,2,512]{2,0,1:T(8,128)}, u32[]{:S(2)}, u32[]{:S(2)}) collective-permute-start(f32[8,2,512]{2,0,1:T(8,128)} %copy.217), channel_id=1, source_target_pairs={{1,0},{2,1},{3,2},{5,4},{6,5},{7,6},{9,8},{10,9},{11,10},{13,12},{... | collective-permute-start | bytes 98312 | tf_op jit(solution)/shard_map/ppermute | solution.py:18
  161.3 28.4 %collective-permute-start.12 = (f32[2,32,512]{1,2,0:T(8,128)S(1)}, f32[2,32,512]{1,2,0:T(8,128)S(1)}, u32[]{:S(2)}, u32[]{:S(2)}) collective-permute-start(f32[2,32,512]{1,2,0:T(8,128)S(1)} %get-tuple-element.48), channel_id=1, source_target_pairs={{0,4},{4,8},{8,12},{12,16},{16,20},{20,24},{24,28},{1,5},{5,9},{9,... | collective-permute-start | bytes 393224 | tf_op jit(solution)/shard_map/ppermute | solution.py:17
  166.5 23.2 %collective-permute-start.13 = (f32[2,32,512]{1,2,0:T(8,128)S(1)}, f32[2,32,512]{1,2,0:T(8,128)S(1)}, u32[]{:S(2)}, u32[]{:S(2)}) collective-permute-start(f32[2,32,512]{1,2,0:T(8,128)S(1)} %get-tuple-element.49), channel_id=1, source_target_pairs={{4,0},{8,4},{12,8},{16,12},{20,16},{24,20},{28,24},{5,1},{9,5},{13... | collective-permute-start | bytes 393224 | tf_op jit(solution)/shard_map/ppermute | solution.py:18
  314.5 45.5 %collective-permute-start.47 = (f32[3,1,128]{2,1,0:T(1,128)}, f32[3,1,128]{2,1,0:T(1,128)}, u32[]{:S(2)}, u32[]{:S(2)}) collective-permute-start(f32[3,1,128]{2,1,0:T(1,128)} %get-tuple-element.125), channel_id=1, source_target_pairs={{1,0},{2,1},{3,2},{5,4},{6,5},{7,6},{9,8},{10,9},{11,10},{13,12},{... | collective-permute-start | bytes 4616 | tf_op jit(solution)/shard_map/ppermute | solution.py:18
  519.7 24.8 %collective-permute-start.84 = (f32[2,32,512]{1,2,0:T(8,128)S(1)}, f32[2,32,512]{1,2,0:T(8,128)S(1)}, u32[]{:S(2)}, u32[]{:S(2)}) collective-permute-start(f32[2,32,512]{1,2,0:T(8,128)S(1)} %get-tuple-element.42), channel_id=1, source_target_pairs={{0,4},{4,8},{8,12},{12,16},{16,20},{20,24},{24,28},{1,5},{5,9},{9,... | collective-permute-start | bytes 393224 | tf_op jit(solution)/shard_map/ppermute | solution.py:17
  522.6 22.0 %collective-permute-start.85 = (f32[2,32,512]{1,2,0:T(8,128)S(1)}, f32[2,32,512]{1,2,0:T(8,128)S(1)}, u32[]{:S(2)}, u32[]{:S(2)}) collective-permute-start(f32[2,32,512]{1,2,0:T(8,128)S(1)} %get-tuple-element.43), channel_id=1, source_target_pairs={{4,0},{8,4},{12,8},{16,12},{20,16},{24,20},{28,24},{5,1},{9,5},{13... | collective-permute-start | bytes 393224 | tf_op jit(solution)/shard_map/ppermute | solution.py:18
  578.5 26.7 %collective-permute-start.88 = (f32[2,32,512]{1,2,0:T(8,128)S(1)}, f32[2,32,512]{1,2,0:T(8,128)S(1)}, u32[]{:S(2)}, u32[]{:S(2)}) collective-permute-start(f32[2,32,512]{1,2,0:T(8,128)S(1)} %get-tuple-element.40), channel_id=1, source_target_pairs={{0,4},{4,8},{8,12},{12,16},{16,20},{20,24},{24,28},{1,5},{5,9},{9,... | collective-permute-start | bytes 393224 | tf_op jit(solution)/shard_map/ppermute | solution.py:17
  582.6 22.5 %collective-permute-start.89 = (f32[2,32,512]{1,2,0:T(8,128)S(1)}, f32[2,32,512]{1,2,0:T(8,128)S(1)}, u32[]{:S(2)}, u32[]{:S(2)}) collective-permute-start(f32[2,32,512]{1,2,0:T(8,128)S(1)} %get-tuple-element.41), channel_id=1, source_target_pairs={{4,0},{8,4},{12,8},{16,12},{20,16},{24,20},{28,24},{5,1},{9,5},{13... | collective-permute-start | bytes 393224 | tf_op jit(solution)/shard_map/ppermute | solution.py:18
  639.7 15.6 %collective-permute-start.92 = (f32[1,32,512]{1,2,0:T(8,128)}, f32[1,32,512]{1,2,0:T(8,128)}, u32[]{:S(2)}, u32[]{:S(2)}) collective-permute-start(f32[1,32,512]{1,2,0:T(8,128)} %get-tuple-element.38), channel_id=1, source_target_pairs={{0,4},{4,8},{8,12},{12,16},{16,20},{20,24},{24,28},{1,5},{5,9},{9,... | collective-permute-start | bytes 196616 | tf_op jit(solution)/shard_map/ppermute | solution.py:17
  (194 other events, 1931.8 us)
where the time goes:
time: 693 us; the launch traced here: 682 us
  starting transfers between devices  237 us (34%)
  local copies, waits for them, and re-layouts  163 us (24%)
  waiting for transfers between devices  160 us (23%)
  other arithmetic  119 us (17%)
    ppermute x48, starting transfers between devices, with_halo(): before = lax.ppermute(last, axis, up)  173 us
    ppermute x48, waiting for transfers between devices, with_halo(): after = lax.ppermute(first, axis, down)  87.7 us
    ppermute x48, waiting for transfers between devices, with_halo(): before = lax.ppermute(last, axis, up)  72.1 us
    ppermute x48, starting transfers between devices, with_halo(): after = lax.ppermute(first, axis, down)  63.5 us
    select_n x24, other arithmetic, colour_pass(): return jnp.where(parity == colour, updated, centre)  39.9 us
    unnamed x259, local copies, waits for them, and re-layouts  38.1 us
    concatenate x19, other arithmetic, with_halo(): x = jnp.concatenate([before, x, after], axis=dim)  23.6 us
    reshape x1, local copies, waits for them, and re-layouts, restrict_sum(): field.reshape(size_x // 2, 2, size_y // 2, 2, size_z // 2, 2)  18.8 us
  transfers between devices with their start and end apart: 96, of which 33 were waited for; matrix products, arithmetic and copies ran while one was open for 23% of the time, Pallas kernels for 0%

commit v1 on v0

--- a/solution.py
+++ b/solution.py
@@ -1,6 +1,10 @@
+import functools
+
 import jax
 import jax.numpy as jnp
 from jax import lax
+from jax.experimental import pallas as pl
+from jax.experimental.pallas import tpu as pltpu
 from jax.sharding import PartitionSpec as P
 
 SWEEPS = 2
@@ -161,7 +165,528 @@
     return (pressure, residual)
 
 
+ROWS = 8
+WIN = 3 * ROWS
+REACH = 3
+MIX = 2.0 / 1001.0
+
+
+def place_of(rows, columns):
+    slab = []
+    for g in range(rows):
+        a = (g // 2) * 2 + ((g % 2) ^ ((g // 2) % 2))
+        slab += [a * columns + (j if a % 2 == 0 else columns - 1 - j) for j in range(columns)]
+    return slab
+
+
+def slab_index(columns):
+    g, j = lax.axis_index("gx"), lax.axis_index("yz")
+    a = (g // 2) * 2 + (g + g // 2) % 2
+    return a * columns + jnp.where(a % 2 == 0, j, columns - 1 - j)
+
+
+def device_of(slab, columns):
+    a, b = slab // columns, slab % columns
+    g = (a // 2) * 2 + (a + a // 2) % 2
+    return g * columns + jnp.where(a % 2 == 0, b, columns - 1 - b)
+
+
+def lanes(shape):
+    return lax.broadcasted_iota(jnp.int32, shape, len(shape) - 1)
+
+
+def swap_lanes(v, step):
+    width = v.shape[-1]
+    up, down = pltpu.roll(v, step, 1), pltpu.roll(v, width - step, 1)
+    return jnp.where((lanes(v.shape) // step) % 2 == 0, down, up)
+
+
+def swap_blocks(tiles):
+    block = lanes(tiles[0].shape) // 32
+    low, even = block < 2, block % 2 == 0
+    t = [None] * 4
+    for a in (0, 1):
+        t[a] = jnp.where(low, tiles[a], pltpu.roll(tiles[a + 2], 64, 1))
+        t[a + 2] = jnp.where(low, pltpu.roll(tiles[a], 64, 1), tiles[a + 2])
+    out = [None] * 4
+    for a in (0, 2):
+        out[a] = jnp.where(even, t[a], pltpu.roll(t[a + 1], 32, 1))
+        out[a + 1] = jnp.where(even, pltpu.roll(t[a], 96, 1), t[a + 1])
+    return out
+
+
+def brick_parity(shape):
+    lane = lanes(shape)
+    return (lane // 32 + lane) % 2
+
+
+def pack_kernel(order, source_ref, phase_ref, guess_ref, out_ref, turned):
+    for a, ref in enumerate((source_ref, phase_ref, guess_ref)):
+        brick = ref[...].reshape(128, ref.shape[2])
+        if a == 1:
+            brick = 1.0 + 999.0 * brick.astype(jnp.float32)
+        turned[a] = brick.T
+    even = brick_parity((ROWS, 128)) == 0
+    for device, slab in enumerate(order):
+        base = 2 * ROWS * slab
+        for a, at in ((1, 0), (0, 2 * ROWS), (2, 3 * ROWS)):
+            low = turned[a, pl.ds(base, ROWS, stride=2), :]
+            high = turned[a, pl.ds(base + 1, ROWS, stride=2), :]
+            if a != 2:
+                out_ref[device, at : at + ROWS, :] = jnp.where(even, low, high)
+            out_ref[device, at + ROWS : at + 2 * ROWS, :] = jnp.where(even, high, low)
+
+
+def unpack_kernel(order, in_ref, pressure_ref, residual_ref, turned):
+    even = brick_parity((ROWS, 128)) == 0
+    for device, slab in enumerate(order):
+        base = 2 * ROWS * slab
+        p0, p1 = in_ref[device, 0:ROWS, :], in_ref[device, ROWS : 2 * ROWS, :]
+        r0 = in_ref[device, 2 * ROWS : 3 * ROWS, :]
+        turned[0, pl.ds(base, ROWS, stride=2), :] = jnp.where(even, p0, p1)
+        turned[0, pl.ds(base + 1, ROWS, stride=2), :] = jnp.where(even, p1, p0)
+        turned[1, pl.ds(base, ROWS, stride=2), :] = jnp.where(even, r0, 0.0)
+        turned[1, pl.ds(base + 1, ROWS, stride=2), :] = jnp.where(even, 0.0, r0)
+    for a, ref in enumerate((pressure_ref, residual_ref)):
+        ref[...] = turned[a].T.reshape(ref.shape)
+
+
+MID = slice(ROWS, ROWS + WIN)
+BELOW = slice(ROWS - 1, ROWS + WIN - 1)
+ABOVE = slice(ROWS + 1, ROWS + WIN + 1)
+
+
+def clear_edges(ref):
+    planes, _, width = ref.shape
+    zero = jnp.zeros((ref.shape[1], width), jnp.float32)
+    ref[0] = zero
+    ref[planes - 1] = zero
+
+    def one(x, _):
+        ref[x, 0:ROWS, :] = zero[:ROWS]
+        ref[x, ROWS + WIN :, :] = zero[:ROWS]
+        return 0
+
+    lax.fori_loop(1, planes - 1, one, 0)
+
+
+def around_fine(ref, x, low):
+    centre = ref[x + 1, MID, :]
+    width = centre.shape[1]
+    return (
+        ref[x, MID, :],
+        ref[x + 2, MID, :],
+        pltpu.roll(centre, 1, 1),
+        pltpu.roll(centre, width - 1, 1),
+        centre,
+        jnp.where(low, ref[x + 1, BELOW, :], ref[x + 1, ABOVE, :]),
+    )
+
+
+def around_coarse(ref, i, low):
+    centre = ref[i + 1, MID, :]
+    width = centre.shape[1]
+    return (
+        ref[i + 1, BELOW, :],
+        ref[i + 1, ABOVE, :],
+        pltpu.roll(centre, 2, 1),
+        pltpu.roll(centre, width - 2, 1),
+        centre,
+        jnp.where(low, ref[i, MID, :], ref[i + 2, MID, :]),
+    )
+
+
+def around_coarsest(planes, k, low):
+    centre = planes[k + 1]
+    rows, width = centre.shape
+    return (
+        pltpu.roll(centre, 1, 0),
+        pltpu.roll(centre, rows - 1, 0),
+        pltpu.roll(centre, 4, 1),
+        pltpu.roll(centre, width - 4, 1),
+        centre,
+        jnp.where(low, planes[k], planes[k + 2]),
+    )
+
+
+def walls(sides, first, last):
+    return sides[:2] + (jnp.where(first, 0.0, sides[2]), jnp.where(last, 0.0, sides[3])) + sides[4:]
+
+
+def mean_fine(u, w):
+    return jnp.where(u == w, u, u * w * MIX)
+
+
+def mean_any(u, w):
+    total = u + w
+    return 2.0 * u * w / jnp.where(total > 0, total, 1.0)
+
+
+def weights(mean, u, sides, top):
+    faces = [mean(u, w) for w in sides]
+    diagonal = (faces[0] + faces[1]) + (faces[2] + faces[3]) + (faces[4] + faces[5])
+    diagonal = diagonal + jnp.where(top, 2.0 * u, 0.0)
+    diagonal = jnp.where(diagonal > 0, diagonal, 1.0)
+    inverse = 1.0 / diagonal
+    return [face * inverse for face in faces], inverse, diagonal
+
+
+def relax(scaled, share, sides):
+    parts = [share[a] * sides[a] for a in range(6)]
+    return scaled + ((parts[0] + parts[1]) + (parts[2] + parts[3]) + (parts[4] + parts[5]))
+
+
+def fine_low(x_parity, colour, width):
+    return (lanes((WIN, width)) + (x_parity + colour)) % 2 == 0
+
+
+def coarse_low(colour, width):
+    row = lax.broadcasted_iota(jnp.int32, (WIN, width), 0)
+    return (row + lanes((WIN, width)) // 2 + colour) % 2 == 0
+
+
+def fine_pass(colour, target, other, share, scaled):
+    planes, width = share.shape[1], share.shape[3]
+
+    def two(i, _):
+        for parity in (0, 1):
+            x = 2 * i + parity
+            sides = around_fine(other, x, fine_low(parity, colour, width))
+            target[x + 1, MID, :] = relax(scaled[x], share[:, x], sides)
+        return 0
+
+    lax.fori_loop(0, planes // 2, two, 0)
+
+
+def coarse_pass(colour, target, other, share, scaled):
+    planes, width = share.shape[1], share.shape[3]
+
+    def one(i, _):
+        sides = around_coarse(other, i, coarse_low(colour, width))
+        target[i + 1, MID, :] = relax(scaled[i], share[:, i], sides)
+        return 0
+
+    lax.fori_loop(0, planes, one, 0)
+
+
+def down_kernel(
+    own, before, after,
+    share0, share1, scaled0, scaled1, diagonal0, field1,
+    cshare0, cshare1, cscaled0, cscaled1, cfield1, packed, message,
+    m0, m1, v0, v1, cm0, cm1, e0, e1, cdiagonal0, rest,
+):
+    planes, width = share0.shape[1], share0.shape[3]
+    for ref in (m0, m1, v0, v1, cm0, cm1, e0, e1):
+        clear_edges(ref)
+
+    def unfold(i, _):
+        for slab, ref in enumerate((before, own, after)):
+            at = slab * ROWS
+            for a, to in enumerate((m0, m1, scaled0, scaled1, v1)):
+                tiles = [ref[4 * i + j, a * ROWS : (a + 1) * ROWS, :] for j in range(4)]
+                shift = 1 if a in (0, 1, 4) else 0
+                for j, tile in enumerate(swap_blocks(tiles)):
+                    row = at + ROWS * shift
+                    to[4 * i + j + shift, row : row + ROWS, :] = tile
+        return 0
+
+    lax.fori_loop(0, planes // 4, unfold, 0)
+
+    lane = lanes((WIN, width))
+
+    def fine_weights(i, _):
+        for parity in (0, 1):
+            x = 2 * i + parity
+            for colour, mine, other, share, scaled in ((0, m0, m1, share0, scaled0), (1, m1, m0, share1, scaled1)):
+                low = fine_low(parity, colour, width)
+                u = mine[x + 1, MID, :]
+                sides = walls(around_fine(other, x, low), lane == 0, lane == width - 1)
+                top = jnp.logical_and(jnp.logical_not(low), sides[5] == 0)
+                shares, inverse, diagonal = weights(mean_fine, u, sides, top)
+                for a in range(6):
+                    share[a, x] = shares[a]
+                scaled[x] = scaled[x] * inverse
+                if colour == 0:
+                    diagonal0[x] = diagonal
+        return 0
+
+    lax.fori_loop(0, planes // 2, fine_weights, 0)
+
+    for _ in range(SWEEPS):
+        fine_pass(0, v0, v1, share0, scaled0)
+        fine_pass(1, v1, v0, share1, scaled1)
+
+    even = coarse_low(0, width)
+
+    def restrict(i, _):
+        fields, mobilities = [], []
+        for half in (0, 1):
+            total, mass = 0.0, 0.0
+            for parity in (0, 1):
+                x = 4 * i + 2 * half + parity
+                sides = around_fine(v1, x, fine_low(parity, 0, width))
+                total = total + diagonal0[x] * (relax(scaled0[x], share0[:, x], sides) - v0[x + 1, MID, :])
+                mass = mass + (m0[x + 1, MID, :] + m1[x + 1, MID, :])
+            fields.append(0.5 * (total + swap_lanes(total, 1)))
+            mobilities.append(0.125 * (mass + swap_lanes(mass, 1)))
+        cscaled0[i] = jnp.where(even, fields[0], fields[1])
+        cscaled1[i] = jnp.where(even, fields[1], fields[0])
+        cm0[i + 1, MID, :] = jnp.where(even, mobilities[0], mobilities[1])
+        cm1[i + 1, MID, :] = jnp.where(even, mobilities[1], mobilities[0])
+        return 0
+
+    lax.fori_loop(0, planes // 4, restrict, 0)
+
+    def copy_field(x, _):
+        field1[x] = v1[x + 1, MID, :]
+        return 0
+
+    lax.fori_loop(0, planes, copy_field, 0)
+
+    def coarse_weights(i, _):
+        for colour, mine, other, share, scaled in ((0, cm0, cm1, cshare0, cscaled0), (1, cm1, cm0, cshare1, cscaled1)):
+            u = mine[i + 1, MID, :]
+            sides = walls(around_coarse(other, i, coarse_low(colour, width)), lane < 2, lane >= width - 2)
+            shares, inverse, diagonal = weights(mean_any, u, sides, sides[1] == 0)
+            for a in range(6):
+                share[a, i] = shares[a]
+            scaled[i] = scaled[i] * inverse
+            if colour == 0:
+                cdiagonal0[i] = diagonal
+        e0[i + 1, MID, :] = cscaled0[i]
+        return 0
+
+    lax.fori_loop(0, planes // 4, coarse_weights, 0)
+
+    for sweep in range(SWEEPS):
+        if sweep:
+            coarse_pass(0, e0, e1, cshare0, cscaled0)
+        coarse_pass(1, e1, e0, cshare1, cscaled1)
+
+    here = slice(ROWS, 2 * ROWS)
+    part = lanes((ROWS, width)) % 4
+    row = lax.broadcasted_iota(jnp.int32, (ROWS, width), 0)
+    pick = jnp.logical_and(row % 2 == 0, part == row // 2)
+    first = lanes((ROWS, width)) % 2 == 0
+    low = coarse_low(0, width)
+    for i in range(planes // 4):
+        sides = around_coarse(e1, i, low)
+        rest[...] = cdiagonal0[i] * (relax(cscaled0[i], cshare0[:, i], sides) - e0[i + 1, MID, :])
+        pair = rest[ROWS : 2 * ROWS, :] + rest[ROWS + 1 : 2 * ROWS + 1, :]
+        pair = 0.5 * (pair + swap_lanes(pair, 2))
+        packed[0, i : i + 1, :] = jnp.sum(jnp.where(pick, pair, 0.0), axis=0, keepdims=True)
+        rest[...] = cm0[i + 1, MID, :] + cm1[i + 1, MID, :]
+        pair = rest[ROWS : 2 * ROWS, :] + rest[ROWS + 1 : 2 * ROWS + 1, :]
+        pair = 0.125 * (pair + swap_lanes(pair, 2))
+        at = planes // 4 + i
+        packed[0, at : at + 1, :] = jnp.sum(jnp.where(pick, pair, 0.0), axis=0, keepdims=True)
+        cfield1[i] = e1[i + 1, MID, :]
+        message[i] = jnp.where(first, cfield1[i, here, :], cscaled0[i, here, :])
+    tile = packed[0]
+    for device in range(1, packed.shape[0]):
+        packed[device] = tile
+
+
+def up_kernel(
+    columns,
+    gathered, before, after,
+    share0, share1, scaled0, scaled1, diagonal0, field1,
+    cshare0, cshare1, cscaled0, cscaled1, cfield1,
+    out,
+    v0, v1, e0, e1, wide0, bshare, coarsest, spread,
+):
+    planes, width = share0.shape[1], share0.shape[3]
+    count = gathered.shape[0]
+    rows = planes // 4
+    for ref in (v0, v1, e0, e1):
+        clear_edges(ref)
+
+    slab = slab_index(columns)
+    lane = lanes((rows, width))
+    part = lane % 4
+    sources, mobilities = [], []
+    for w in range(-REACH, REACH + 1):
+        near = slab + w
+        inside = jnp.logical_and(near >= 0, near < count)
+        device = device_of(jnp.clip(near, 0, count - 1), columns)
+        keep = jnp.where(inside, 1.0, 0.0)
+        for at, into in ((0, sources), (rows, mobilities)):
+            tile = gathered[device, at : at + rows, :] * keep
+            for z in range(4):
+                v = jnp.where(part == z, tile, 0.0)
+                v = v + swap_lanes(v, 1)
+                into.append(v + swap_lanes(v, 2))
+
+    parity = (lax.broadcasted_iota(jnp.int32, (rows, width), 0) + lane // 4) % 2
+    pairs = len(sources) // 2
+    zero = jnp.zeros((rows, width), jnp.float32)
+    low = (parity == 0, parity == 1)
+
+    def coloured(planes_of):
+        first = [jnp.where(low[0], planes_of[2 * k], planes_of[2 * k + 1]) for k in range(pairs)]
+        second = [jnp.where(low[0], planes_of[2 * k + 1], planes_of[2 * k]) for k in range(pairs)]
+        return [zero] + first + [zero], [zero] + second + [zero]
+
+    source, mobility = coloured(sources), coloured(mobilities)
+    row = lax.broadcasted_iota(jnp.int32, (rows, width), 0)
+    scaled = ([], [])
+    for k in range(pairs):
+        for colour in (0, 1):
+            sides = around_coarsest(mobility[1 - colour], k, low[colour])
+            sides = (jnp.where(row == 0, 0.0, sides[0]), jnp.where(row == rows - 1, 0.0, sides[1])) + sides[2:]
+            sides = walls(sides, lane < 4, lane >= width - 4)
+            top = jnp.logical_and(jnp.logical_not(low[colour]), sides[5] == 0)
+            shares, inverse, _ = weights(mean_any, mobility[colour][k + 1], sides, top)
+            for a in range(6):
+                bshare[colour, a, k] = shares[a]
+            scaled[colour].append(source[colour][k + 1] * inverse)
+
+    fields = [[zero] + scaled[0] + [zero], None]
+    for step in range(1, 2 * BOTTOM_SWEEPS):
+        colour = step % 2
+        new = []
+        for k in range(pairs):
+            sides = around_coarsest(fields[1 - colour], k, low[colour])
+            new.append(relax(scaled[colour][k], [bshare[colour, a, k] for a in range(6)], sides))
+        fields[colour] = [zero] + new + [zero]
+
+    start = 4 * REACH - ROWS // 2
+    for k in range(WIN // 4):
+        a, b = fields[0][start // 2 + k + 1], fields[1][start // 2 + k + 1]
+        coarsest[2 * k * rows : (2 * k + 1) * rows, :] = jnp.where(low[0], a, b)
+        coarsest[(2 * k + 1) * rows : (2 * k + 2) * rows, :] = jnp.where(low[0], b, a)
+
+    first = lanes((ROWS, width)) % 2 == 0
+    for i in range(rows):
+        half = coarsest[pl.ds(i, WIN // 2, stride=rows), :]
+        spread[pl.ds(0, WIN // 2, stride=2), :] = half
+        spread[pl.ds(1, WIN // 2, stride=2), :] = half
+        e1[i + 1, 2 * ROWS : 3 * ROWS, :] = cfield1[i, ROWS : 2 * ROWS, :] + spread[ROWS : 2 * ROWS, :]
+        for at, ref in ((0, before), (2 * ROWS, after)):
+            mixed = ref[i]
+            other = swap_lanes(mixed, 1)
+            e1[i + 1, ROWS + at : 2 * ROWS + at, :] = jnp.where(first, mixed, other) + spread[at : at + ROWS, :]
+            wide0[i, at : at + ROWS, :] = jnp.where(first, other, mixed)
+        wide0[i, ROWS : 2 * ROWS, :] = cscaled0[i, ROWS : 2 * ROWS, :]
+
+    for _ in range(SWEEPS):
+        coarse_pass(0, e0, e1, cshare0, wide0)
+        coarse_pass(1, e1, e0, cshare1, cscaled1)
+
+    even = coarse_low(0, width)
+
+    def correct(i, _):
+        a, b = e0[i + 1, MID, :], e1[i + 1, MID, :]
+        for half, add in ((0, jnp.where(even, a, b)), (1, jnp.where(even, b, a))):
+            for parity in (0, 1):
+                x = 4 * i + 2 * half + parity
+                v1[x + 1, MID, :] = field1[x] + add
+        return 0
+
+    lax.fori_loop(0, rows, correct, 0)
+
+    for _ in range(SWEEPS):
+        fine_pass(0, v0, v1, share0, scaled0)
+        fine_pass(1, v1, v0, share1, scaled1)
+
+    here = slice(2 * ROWS, 3 * ROWS)
+
+    def fold(i, _):
+        rest = []
+        for parity in range(4):
+            x = 4 * i + parity
+            sides = around_fine(v1, x, fine_low(parity % 2, 0, width))
+            full = diagonal0[x] * (relax(scaled0[x], share0[:, x], sides) - v0[x + 1, MID, :])
+            rest.append(full[ROWS : 2 * ROWS])
+        for a, tiles in (
+            (0, [v0[4 * i + b + 1, here, :] for b in range(4)]),
+            (1, [v1[4 * i + b + 1, here, :] for b in range(4)]),
+            (2, rest),
+        ):
+            for j, tile in enumerate(swap_blocks(tiles)):
+                out[4 * i + j, a * ROWS : (a + 1) * ROWS, :] = tile
+        return 0
+
+    lax.fori_loop(0, rows, fold, 0)
+
+
+def local_slabs(shape, right_side, phase, pressure_guess):
+    across, columns = shape
+    count = across * columns
+    bx, by, length = right_side.shape
+    planes, width = across * bx, columns * by
+    f32 = jnp.float32
+    order = place_of(across, columns)
+    path = sorted(range(count), key=lambda device: order[device])
+    up = [(path[k], path[k + 1]) for k in range(count - 1)]
+    down = [(b, a) for a, b in up]
+    axes = ("gx", "yz")
+    params = pltpu.CompilerParams(vmem_limit_bytes=56 * 1024 * 1024)
+
+    def struct(*dims):
+        return jax.ShapeDtypeStruct(dims, f32)
+
+    def vmem(*dims):
+        return pltpu.VMEM(dims, f32)
+
+    bricks = pl.pallas_call(
+        functools.partial(pack_kernel, order),
+        out_shape=struct(count, 5 * ROWS, 128),
+        scratch_shapes=[vmem(3, length, 128)],
+        compiler_params=params,
+        name="pack",
+    )(right_side, phase, pressure_guess)
+    own = lax.all_to_all(bricks, axes, 0, 0)
+    before = lax.ppermute(own, axes, up)
+    after = lax.ppermute(own, axes, down)
+
+    coarse = planes // 4
+    fine = [struct(6, planes, WIN, width)] * 2 + [struct(planes, WIN, width)] * 4
+    half = [struct(6, coarse, WIN, width)] * 2 + [struct(coarse, WIN, width)] * 3
+    padded = [vmem(planes + 2, WIN + 2 * ROWS, width)] * 2
+    cpadded = [vmem(coarse + 2, WIN + 2 * ROWS, width)] * 2
+    *state, packed, message = pl.pallas_call(
+        down_kernel,
+        out_shape=fine + half + [struct(count, 2 * coarse, width), struct(coarse, ROWS, width)],
+        scratch_shapes=padded * 2 + cpadded * 2 + [vmem(coarse, WIN, width), vmem(WIN, width)],
+        compiler_params=params,
+        name="down",
+    )(own, before, after)
+    gathered = lax.all_to_all(packed, axes, 0, 0)
+    e_before = lax.ppermute(message, axes, up)
+    e_after = lax.ppermute(message, axes, down)
+
+    cycle = pl.pallas_call(
+        functools.partial(up_kernel, columns),
+        out_shape=struct(count, 3 * ROWS, 128),
+        scratch_shapes=padded + cpadded + [
+            vmem(coarse, WIN, width),
+            vmem(2, 6, 2 * (2 * REACH + 1), coarse, width),
+            vmem(WIN // 2 * coarse, width),
+            vmem(WIN, width),
+        ],
+        compiler_params=params,
+        name="up",
+    )(gathered, e_before, e_after, *state)
+    back = lax.all_to_all(cycle, axes, 0, 0)
+    return pl.pallas_call(
+        functools.partial(unpack_kernel, order),
+        out_shape=[struct(bx, by, length)] * 2,
+        scratch_shapes=[vmem(2, length, 128)],
+        compiler_params=params,
+        name="unpack",
+    )(back)
+
+
 def solution(mesh):
-    in_specs = (P("gx", "yz", None), P("gx", "yz", None), P("gx", "yz", None))
-    out_specs = (P("gx", "yz", None), P("gx", "yz", None))
-    return jax.shard_map(local, mesh=mesh, in_specs=in_specs, out_specs=out_specs, check_vma=False)
+    spec = P("gx", "yz", None)
+    shape = (mesh.shape["gx"], mesh.shape["yz"])
+
+    def cycle(right_side, phase, pressure_guess):
+        bx, by, length = right_side.shape
+        slabs = (bx, by, shape[1]) == (4, 32, 4) and length == 2 * ROWS * shape[0] * shape[1]
+        if slabs and shape[0] == 8:
+            return local_slabs(shape, right_side, phase, pressure_guess)
+        return local(right_side, phase, pressure_guess)
+
+    return jax.shard_map(cycle, mesh=mesh, in_specs=(spec,) * 3, out_specs=(spec,) * 2, check_vma=False)

time: 693 us -> 113 us (0.16); the launches traced: 682 us -> 112 us
  starting transfers between devices: 237 us -> 20.3 us
  local copies, waits for them, and re-layouts: 163 us -> 1.59 us
  waiting for transfers between devices: 160 us -> 7.89 us
  other arithmetic: 119 us -> 0 us
  blocking collectives: 0 us -> 41.7 us
  Pallas kernels: 0 us -> 39.8 us
    ppermute x96 -> x4, starting transfers between devices: 237 us -> 8.68 us  [the longest x1 3.07 us: local_slabs(): before = lax.ppermute(own, axes, up)]
    ppermute x96 -> x4, waiting for transfers between devices: 160 us -> 2.68 us  [the longest x1 1.64 us: local_slabs(): before = lax.ppermute(own, axes, up)]
    select_n x35 -> x0, other arithmetic: 50.8 us -> none  [the longest x24 39.9 us: colour_pass(): return jnp.where(parity == colour, updated, centre)]
    all_to_all x0 -> x2, blocking collectives: none -> 41.7 us  [the longest x1 25.2 us: local_slabs(): own = lax.all_to_all(bricks, axes, 0, 0)]
    pallas_call x0 -> x4, Pallas kernels: none -> 39.8 us  [the longest x1 19.9 us: local_slabs(): pl.pallas_call(down_kernel, out_shape=fine + half + [struct(count, 2 * co...]
    slice x48 -> x0, local copies, waits for them, and re-layouts: 39.1 us -> none  [the longest x17 17.1 us: with_halo(): last = lax.slice_in_dim(x, length - width, length, axis=dim)]
    reshape x4 -> x0, local copies, waits for them, and re-layouts: 38.6 us -> none  [the longest x1 18.8 us: restrict_sum(): field.reshape(size_x // 2, 2, size_y // 2, 2, size_z // 2, 2)]
    unnamed x259 -> x12, local copies, waits for them, and re-layouts: 38.1 us -> 1.59 us
  transfers between devices with their start and end apart: 96 -> 5, of which waited for: 33 -> 3; matrix products, arithmetic and copies ran while one was open for 23% -> 0% of each run, Pallas kernels for 0% -> 0%
where the time goes in v1:
time: 113 us; the launch traced here: 112 us
  blocking collectives  41.7 us (37%)
  Pallas kernels  39.8 us (35%)
  starting transfers between devices  20.3 us (18%)
  waiting for transfers between devices  7.89 us (7%)
  local copies, waits for them, and re-layouts  1.59 us (1%)
    all_to_all x1, blocking collectives, local_slabs(): own = lax.all_to_all(bricks, axes, 0, 0)  25.2 us
    pallas_call x1, Pallas kernels, local_slabs(): pl.pallas_call(down_kernel, out_shape=fine + half + [struct(count, 2 * co...  19.9 us
    all_to_all x1, blocking collectives, local_slabs(): back = lax.all_to_all(cycle, axes, 0, 0)  16.5 us
    pallas_call x1, Pallas kernels, local_slabs(): pl.pallas_call(functools.partial(up_kernel, columns), out_shape=struct(co...  15.7 us
    all_to_all x1, starting transfers between devices, local_slabs(): gathered = lax.all_to_all(packed, axes, 0, 0)  11.6 us
    all_to_all x1, waiting for transfers between devices, local_slabs(): gathered = lax.all_to_all(packed, axes, 0, 0)  5.21 us
    ppermute x1, starting transfers between devices, local_slabs(): before = lax.ppermute(own, axes, up)  3.07 us
    ppermute x1, starting transfers between devices, local_slabs(): e_before = lax.ppermute(message, axes, up)  3.03 us
  transfers between devices with their start and end apart: 5, of which 3 were waited for; matrix products, arithmetic and copies ran while one was open for 0% of the time, Pallas kernels for 0%

profile of v1, /device:TPU:0, one launch (start us, length us, event | category | flops | bytes accessed | tf_op | source)
XLA Modules:
  0.0 112.0 jit_solution(311751005795886881)
XLA Ops:
  0.6 2.3 %pack.1 = f32[32,40,128]{2,1,0:T(8,128)} custom-call(f32[4,32,512]{2,1,0:T(8,128)} %source_ref.1, s32[4,32,512]{2,1,0:T(8,128)} %phase_ref.1, f32[4,32,512]{2,1,0:T(8,128)} %guess_ref.1), custom_call_target="tpu_custom_call" | custom-call | tf_op jit(solution)/shard_map/pack/pallas_call | solution.py:632
  2.9 25.2 %all_to_all.15.own = f32[32,40,128]{2,1,0:T(8,128)S(1)} all-to-all(f32[32,40,128]{2,1,0:T(8,128)} %pack.1), channel_id=1, replica_groups=mesh['gx'=8,'yz'=4] {'gx','yz'}, dimensions={0} | all-to-all | bytes 1310720 | tf_op jit(solution)/shard_map/all_to_all | solution.py:639
  28.2 1.3 %collective-permute-start.1 = (f32[32,40,128]{2,1,0:T(8,128)S(1)}, f32[32,40,128]{2,1,0:T(8,128)S(1)}, u32[]{:S(2)}, u32[]{:S(2)}) collective-permute-start(f32[32,40,128]{2,1,0:T(8,128)S(1)} %all_to_all.15.own), channel_id=1, source_target_pairs={{1,0},{2,1},{3,2},{7,3},{6,7},{5,6},{4,5},{12,4},{13,12},{14,13},{... | collective-permute-start | bytes 1966088 | tf_op jit(solution)/shard_map/ppermute | solution.py:641
  29.4 3.1 %collective-permute-start = (f32[32,40,128]{2,1,0:T(8,128)S(1)}, f32[32,40,128]{2,1,0:T(8,128)S(1)}, u32[]{:S(2)}, u32[]{:S(2)}) collective-permute-start(f32[32,40,128]{2,1,0:T(8,128)S(1)} %all_to_all.15.own), channel_id=1, source_target_pairs={{0,1},{1,2},{2,3},{3,7},{7,6},{6,5},{5,4},{4,12},{12,13},{13,14},{... | collective-permute-start | bytes 1966088 | tf_op jit(solution)/shard_map/ppermute | solution.py:640
  32.5 0.0 collective-permute-done.1.after
  32.5 0.0 copy-start.2
  32.5 1.6 %collective-permute-done.before = f32[32,40,128]{2,1,0:T(8,128)S(1)} collective-permute-done((f32[32,40,128]{2,1,0:T(8,128)S(1)}, f32[32,40,128]{2,1,0:T(8,128)S(1)}, u32[]{:S(2)}, u32[]{:S(2)}) %collective-permute-start) | collective-permute-done | bytes 655392 | tf_op jit(solution)/shard_map/ppermute | solution.py:640
  34.2 0.0 copy-done
  34.2 0.0 copy-done.2
  34.2 0.9 copy-done.3
  35.1 19.9 %down.1 = (f32[6,32,24,128]{3,2,1,0:T(8,128)}, f32[6,32,24,128]{3,2,1,0:T(8,128)}, f32[32,24,128]{2,1,0:T(8,128)}, f32[32,24,128]{2,1,0:T(8,128)}, f32[32,24,128...) custom-call(f32[32,40,128]{2,1,0:T(8,128)} %copy-done, ...), custom_call_target="tpu_custom_call" | custom-call | tf_op jit(solution)/shard_map/down/pallas_call | solution.py:648
  55.0 11.6 %all-to-all-start.1 = ((f32[32,16,128]{2,1,0:T(8,128)}), f32[32,16,128]{2,1,0:T(8,128)S(1)}, u32[]{:S(2)}, u32[]{:S(2)}) async-start(f32[32,16,128]{2,1,0:T(8,128)} %get-tuple-element.15), calls=%async_computation.1 | async-start | bytes 524288 | tf_op jit(solution)/shard_map/all_to_all | solution.py:655
  66.6 1.3 %collective-permute-start.3 = (f32[8,8,128]{2,1,0:T(8,128)}, f32[8,8,128]{2,1,0:T(8,128)S(1)}, u32[]{:S(2)}, u32[]{:S(2)}) collective-permute-start(f32[8,8,128]{2,1,0:T(8,128)} %get-tuple-element.16), channel_id=1, source_target_pairs={{1,0},{2,1},{3,2},{7,3},{6,7},{5,6},{4,5},{12,4},{13,12},{14,13},{... | collective-permute-start | bytes 98312 | tf_op jit(solution)/shard_map/ppermute | solution.py:657
  67.9 3.0 %collective-permute-start.2 = (f32[8,8,128]{2,1,0:T(8,128)}, f32[8,8,128]{2,1,0:T(8,128)S(1)}, u32[]{:S(2)}, u32[]{:S(2)}) collective-permute-start(f32[8,8,128]{2,1,0:T(8,128)} %get-tuple-element.16), channel_id=1, source_target_pairs={{0,1},{1,2},{2,3},{3,7},{7,6},{6,5},{5,4},{4,12},{12,13},{13,14},{... | collective-permute-start | bytes 98312 | tf_op jit(solution)/shard_map/ppermute | solution.py:656
  71.0 0.0 collective-permute-done.3.after
  71.0 0.0 copy-start.4
  71.0 1.0 collective-permute-done.2.before
  72.0 5.2 %all-to-all-done.1.gathered = f32[32,16,128]{2,1,0:T(8,128)S(1)} async-done(((f32[32,16,128]{2,1,0:T(8,128)}), f32[32,16,128]{2,1,0:T(8,128)S(1)}, u32[]{:S(2)}, u32[]{:S(2)}) %all-to-all-start.1) | async-done | bytes 262176 | tf_op jit(solution)/shard_map/all_to_all | solution.py:655
  77.2 0.0 copy-done.4
  77.2 0.0 copy-done.5
  77.2 0.7 copy-done.1
  77.9 15.7 %up.1 = f32[32,24,128]{2,1,0:T(8,128)} custom-call(f32[32,16,128]{2,1,0:T(8,128)} %copy-done.1, f32[8,8,128]{2,1,0:T(8,128)} %copy-done.5, f32[8,8,128]{2,1,0:T(8,128)} %copy-done.4, f32[6,32,24,128]{3,2,1,0:T(8,128)} %get-tuple-element.17.share0, f32[6,32,24,128]{3,2,1,0:T(8,128)} %get-tuple-element.18.share1, f32[32,24,128]{2,1,0:T(8,128)} %get-tuple-element.19.scaled0, ...), custom_call_target="tpu_custom_call" | custom-call | tf_op jit(solution)/shard_map/up/pallas_call | solution.py:659
  93.6 16.5 %all_to_all.16.in_ref = f32[32,24,128]{2,1,0:T(8,128)} all-to-all(f32[32,24,128]{2,1,0:T(8,128)} %up.1), channel_id=1, replica_groups=mesh['gx'=8,'yz'=4] {'gx','yz'}, dimensions={0} | all-to-all | bytes 786432 | tf_op jit(solution)/shard_map/all_to_all | solution.py:671
  110.1 1.9 %unpack.1 = (f32[4,32,512]{2,1,0:T(8,128)}, f32[4,32,512]{2,1,0:T(8,128)}) custom-call(f32[32,24,128]{2,1,0:T(8,128)} %all_to_all.16.in_ref), custom_call_target="tpu_custom_call" | custom-call | tf_op jit(solution)/shard_map/unpack/pallas_call | solution.py:672
  (4 shorter events, 0.0 us)
Async XLA Ops:
  28.2 6.0 %copy-start = (f32[32,40,128]{2,1,0:T(8,128)}, f32[32,40,128]{2,1,0:T(8,128)S(1)}, u32[]{:S(2)}) copy-start(f32[32,40,128]{2,1,0:T(8,128)S(1)} %all_to_all.15.own) | copy-start | bytes 1966084
  28.2 4.4 %collective-permute-start.1 = (f32[32,40,128]{2,1,0:T(8,128)S(1)}, f32[32,40,128]{2,1,0:T(8,128)S(1)}, u32[]{:S(2)}, u32[]{:S(2)}) collective-permute-start(f32[32,40,128]{2,1,0:T(8,128)S(1)} %all_to_all.15.own), channel_id=1, source_target_pairs={{1,0},{2,1},{3,2},{7,3},{6,7},{5,6},{4,5},{12,4},{13,12},{14,13},{... | collective-permute-start | bytes 1966088 | tf_op jit(solution)/shard_map/ppermute | solution.py:641
  29.4 4.7 %collective-permute-start = (f32[32,40,128]{2,1,0:T(8,128)S(1)}, f32[32,40,128]{2,1,0:T(8,128)S(1)}, u32[]{:S(2)}, u32[]{:S(2)}) collective-permute-start(f32[32,40,128]{2,1,0:T(8,128)S(1)} %all_to_all.15.own), channel_id=1, source_target_pairs={{0,1},{1,2},{2,3},{3,7},{7,6},{6,5},{5,4},{4,12},{12,13},{13,14},{... | collective-permute-start | bytes 1966088 | tf_op jit(solution)/shard_map/ppermute | solution.py:640
  32.5 1.7 %copy-start.2 = (f32[32,40,128]{2,1,0:T(8,128)}, f32[32,40,128]{2,1,0:T(8,128)S(1)}, u32[]{:S(2)}) copy-start(f32[32,40,128]{2,1,0:T(8,128)S(1)} %collective-permute-done.1.after) | copy-start | bytes 1966084
  34.2 0.9 copy-start.3
  55.0 22.2 %all-to-all-start.1 = ((f32[32,16,128]{2,1,0:T(8,128)}), f32[32,16,128]{2,1,0:T(8,128)S(1)}, u32[]{:S(2)}, u32[]{:S(2)}) async-start(f32[32,16,128]{2,1,0:T(8,128)} %get-tuple-element.15), calls=%async_computation.1 | async-start | bytes 524288 | tf_op jit(solution)/shard_map/all_to_all | solution.py:655
  66.6 4.3 %collective-permute-start.3 = (f32[8,8,128]{2,1,0:T(8,128)}, f32[8,8,128]{2,1,0:T(8,128)S(1)}, u32[]{:S(2)}, u32[]{:S(2)}) collective-permute-start(f32[8,8,128]{2,1,0:T(8,128)} %get-tuple-element.16), channel_id=1, source_target_pairs={{1,0},{2,1},{3,2},{7,3},{6,7},{5,6},{4,5},{12,4},{13,12},{14,13},{... | collective-permute-start | bytes 98312 | tf_op jit(solution)/shard_map/ppermute | solution.py:657
  67.9 4.1 %collective-permute-start.2 = (f32[8,8,128]{2,1,0:T(8,128)}, f32[8,8,128]{2,1,0:T(8,128)S(1)}, u32[]{:S(2)}, u32[]{:S(2)}) collective-permute-start(f32[8,8,128]{2,1,0:T(8,128)} %get-tuple-element.16), channel_id=1, source_target_pairs={{0,1},{1,2},{2,3},{3,7},{7,6},{6,5},{5,4},{4,12},{12,13},{13,14},{... | collective-permute-start | bytes 98312 | tf_op jit(solution)/shard_map/ppermute | solution.py:656
  71.0 6.3 %copy-start.4 = (f32[8,8,128]{2,1,0:T(8,128)}, f32[8,8,128]{2,1,0:T(8,128)S(1)}, u32[]{:S(2)}) copy-start(f32[8,8,128]{2,1,0:T(8,128)S(1)} %collective-permute-done.3.after) | copy-start | bytes 98308
  72.0 5.2 %copy-start.5 = (f32[8,8,128]{2,1,0:T(8,128)}, f32[8,8,128]{2,1,0:T(8,128)S(1)}, u32[]{:S(2)}) copy-start(f32[8,8,128]{2,1,0:T(8,128)S(1)} %collective-permute-done.2.before) | copy-start | bytes 98308
  77.2 0.7 copy-start.1

commit v2 on v1

--- a/solution.py
+++ b/solution.py
@@ -220,8 +220,15 @@
     return (lane // 32 + lane) % 2
 
 
-def pack_kernel(order, source_ref, phase_ref, guess_ref, out_ref, turned):
+def pack_kernel(order, source_hbm, phase_hbm, guess_hbm, out_ref, source_ref, phase_ref, guess_ref, turned, arrived):
+    copies = [
+        pltpu.make_async_copy(hbm, ref, arrived.at[a])
+        for a, (hbm, ref) in enumerate(((source_hbm, source_ref), (phase_hbm, phase_ref), (guess_hbm, guess_ref)))
+    ]
+    for copy in copies:
+        copy.start()
     for a, ref in enumerate((source_ref, phase_ref, guess_ref)):
+        copies[a].wait()
         brick = ref[...].reshape(128, ref.shape[2])
         if a == 1:
             brick = 1.0 + 999.0 * brick.astype(jnp.float32)
@@ -251,6 +258,7 @@
         ref[...] = turned[a].T.reshape(ref.shape)
 
 
+KEPT = 11
 MID = slice(ROWS, ROWS + WIN)
 BELOW = slice(ROWS - 1, ROWS + WIN - 1)
 ABOVE = slice(ROWS + 1, ROWS + WIN + 1)
@@ -355,7 +363,7 @@
             target[x + 1, MID, :] = relax(scaled[x], share[:, x], sides)
         return 0
 
-    lax.fori_loop(0, planes // 2, two, 0)
+    lax.fori_loop(0, planes // 2, two, 0, unroll=4)
 
 
 def coarse_pass(colour, target, other, share, scaled):
@@ -366,16 +374,21 @@
         target[i + 1, MID, :] = relax(scaled[i], share[:, i], sides)
         return 0
 
-    lax.fori_loop(0, planes, one, 0)
+    lax.fori_loop(0, planes, one, 0, unroll=4)
 
 
 def down_kernel(
     own, before, after,
-    share0, share1, scaled0, scaled1, diagonal0, field1,
-    cshare0, cshare1, cscaled0, cscaled1, cfield1, packed, message,
-    m0, m1, v0, v1, cm0, cm1, e0, e1, cdiagonal0, rest,
+    *refs,
 ):
+    kept, packed = refs[: KEPT + 1], refs[KEPT + 1]
+    state, work = refs[KEPT + 2 : 2 * KEPT], refs[2 * KEPT :]
+    share0, share1, scaled0, scaled1, diagonal0, cshare0, cshare1, cscaled0, cscaled1 = state
+    m0, m1, v0, v1, cm0, cm1, e0, e1, cdiagonal0, rest, message, done = work
     planes, width = share0.shape[1], share0.shape[3]
+    coarse = planes // 4
+    held = list(state) + [v1.at[1 : planes + 1, MID, :], e1.at[1 : coarse + 1, MID, :], message]
+    copies = [pltpu.make_async_copy(ref, hbm, done.at[k]) for k, (ref, hbm) in enumerate(zip(held, kept))]
     for ref in (m0, m1, v0, v1, cm0, cm1, e0, e1):
         clear_edges(ref)
 
@@ -411,10 +424,13 @@
         return 0
 
     lax.fori_loop(0, planes // 2, fine_weights, 0)
+    for copy in copies[:5]:
+        copy.start()
 
     for _ in range(SWEEPS):
         fine_pass(0, v0, v1, share0, scaled0)
         fine_pass(1, v1, v0, share1, scaled1)
+    copies[KEPT - 2].start()
 
     even = coarse_low(0, width)
 
@@ -437,12 +453,6 @@
 
     lax.fori_loop(0, planes // 4, restrict, 0)
 
-    def copy_field(x, _):
-        field1[x] = v1[x + 1, MID, :]
-        return 0
-
-    lax.fori_loop(0, planes, copy_field, 0)
-
     def coarse_weights(i, _):
         for colour, mine, other, share, scaled in ((0, cm0, cm1, cshare0, cscaled0), (1, cm1, cm0, cshare1, cscaled1)):
             u = mine[i + 1, MID, :]
@@ -457,19 +467,25 @@
         return 0
 
     lax.fori_loop(0, planes // 4, coarse_weights, 0)
+    for copy in copies[5 : KEPT - 2]:
+        copy.start()
 
     for sweep in range(SWEEPS):
         if sweep:
             coarse_pass(0, e0, e1, cshare0, cscaled0)
         coarse_pass(1, e1, e0, cshare1, cscaled1)
+    copies[KEPT - 1].start()
 
     here = slice(ROWS, 2 * ROWS)
     part = lanes((ROWS, width)) % 4
     row = lax.broadcasted_iota(jnp.int32, (ROWS, width), 0)
     pick = jnp.logical_and(row % 2 == 0, part == row // 2)
     first = lanes((ROWS, width)) % 2 == 0
+    for i in range(coarse):
+        message[i] = jnp.where(first, e1[i + 1, 2 * ROWS : 3 * ROWS, :], cscaled0[i, here, :])
+    copies[KEPT].start()
     low = coarse_low(0, width)
-    for i in range(planes // 4):
+    for i in range(coarse):
         sides = around_coarse(e1, i, low)
         rest[...] = cdiagonal0[i] * (relax(cscaled0[i], cshare0[:, i], sides) - e0[i + 1, MID, :])
         pair = rest[ROWS : 2 * ROWS, :] + rest[ROWS + 1 : 2 * ROWS + 1, :]
@@ -480,22 +496,27 @@
         pair = 0.125 * (pair + swap_lanes(pair, 2))
         at = planes // 4 + i
         packed[0, at : at + 1, :] = jnp.sum(jnp.where(pick, pair, 0.0), axis=0, keepdims=True)
-        cfield1[i] = e1[i + 1, MID, :]
-        message[i] = jnp.where(first, cfield1[i, here, :], cscaled0[i, here, :])
     tile = packed[0]
     for device in range(1, packed.shape[0]):
         packed[device] = tile
+    for copy in copies:
+        copy.wait()
 
 
 def up_kernel(
     columns,
-    gathered, before, after,
-    share0, share1, scaled0, scaled1, diagonal0, field1,
-    cshare0, cshare1, cscaled0, cscaled1, cfield1,
-    out,
-    v0, v1, e0, e1, wide0, bshare, coarsest, spread,
+    gathered,
+    *refs,
 ):
+    kept, out = refs[: KEPT + 2], refs[KEPT + 2]
+    state, work = refs[KEPT + 3 : 2 * KEPT + 1], refs[2 * KEPT + 1 :]
+    share0, share1, scaled0, scaled1, diagonal0, cshare0, cshare1, cscaled0, cscaled1 = state
+    v0, v1, e0, e1, before, after, bshare, coarsest, spread, done = work
     planes, width = share0.shape[1], share0.shape[3]
+    held = list(state) + [v1.at[1 : planes + 1, MID, :], e1.at[1 : planes // 4 + 1, MID, :], before, after]
+    copies = [pltpu.make_async_copy(hbm, ref, done.at[k]) for k, (ref, hbm) in enumerate(zip(held, kept))]
+    for copy in copies[5 : KEPT - 2] + copies[KEPT - 1 :] + copies[:5] + copies[KEPT - 2 : KEPT - 1]:
+        copy.start()
     count = gathered.shape[0]
     rows = planes // 4
     for ref in (v0, v1, e0, e1):
@@ -556,31 +577,35 @@
         coarsest[2 * k * rows : (2 * k + 1) * rows, :] = jnp.where(low[0], a, b)
         coarsest[(2 * k + 1) * rows : (2 * k + 2) * rows, :] = jnp.where(low[0], b, a)
 
+    for copy in copies[5 : KEPT - 2] + copies[KEPT - 1 :]:
+        copy.wait()
     first = lanes((ROWS, width)) % 2 == 0
     for i in range(rows):
         half = coarsest[pl.ds(i, WIN // 2, stride=rows), :]
         spread[pl.ds(0, WIN // 2, stride=2), :] = half
         spread[pl.ds(1, WIN // 2, stride=2), :] = half
-        e1[i + 1, 2 * ROWS : 3 * ROWS, :] = cfield1[i, ROWS : 2 * ROWS, :] + spread[ROWS : 2 * ROWS, :]
+        e1[i + 1, 2 * ROWS : 3 * ROWS, :] = e1[i + 1, 2 * ROWS : 3 * ROWS, :] + spread[ROWS : 2 * ROWS, :]
         for at, ref in ((0, before), (2 * ROWS, after)):
             mixed = ref[i]
             other = swap_lanes(mixed, 1)
             e1[i + 1, ROWS + at : 2 * ROWS + at, :] = jnp.where(first, mixed, other) + spread[at : at + ROWS, :]
-            wide0[i, at : at + ROWS, :] = jnp.where(first, other, mixed)
-        wide0[i, ROWS : 2 * ROWS, :] = cscaled0[i, ROWS : 2 * ROWS, :]
+            cscaled0[i, at : at + ROWS, :] = jnp.where(first, other, mixed)
 
     for _ in range(SWEEPS):
-        coarse_pass(0, e0, e1, cshare0, wide0)
+        coarse_pass(0, e0, e1, cshare0, cscaled0)
         coarse_pass(1, e1, e0, cshare1, cscaled1)
 
     even = coarse_low(0, width)
+
+    for copy in copies[:5] + copies[KEPT - 2 : KEPT - 1]:
+        copy.wait()
 
     def correct(i, _):
         a, b = e0[i + 1, MID, :], e1[i + 1, MID, :]
         for half, add in ((0, jnp.where(even, a, b)), (1, jnp.where(even, b, a))):
             for parity in (0, 1):
                 x = 4 * i + 2 * half + parity
-                v1[x + 1, MID, :] = field1[x] + add
+                v1[x + 1, MID, :] = v1[x + 1, MID, :] + add
         return 0
 
     lax.fori_loop(0, rows, correct, 0)
@@ -621,7 +646,7 @@
     up = [(path[k], path[k + 1]) for k in range(count - 1)]
     down = [(b, a) for a, b in up]
     axes = ("gx", "yz")
-    params = pltpu.CompilerParams(vmem_limit_bytes=56 * 1024 * 1024)
+    params = pltpu.CompilerParams(vmem_limit_bytes=20 * 1024 * 1024)
 
     def struct(*dims):
         return jax.ShapeDtypeStruct(dims, f32)
@@ -631,24 +656,38 @@
 
     bricks = pl.pallas_call(
         functools.partial(pack_kernel, order),
+        in_specs=[pl.BlockSpec(memory_space=pltpu.HBM)] * 3,
         out_shape=struct(count, 5 * ROWS, 128),
-        scratch_shapes=[vmem(3, length, 128)],
+        scratch_shapes=[
+            vmem(bx, by, length),
+            pltpu.VMEM((bx, by, length), phase.dtype),
+            vmem(bx, by, length),
+            vmem(3, length, 128),
+            pltpu.SemaphoreType.DMA((3,)),
+        ],
         compiler_params=params,
         name="pack",
-    )(right_side, phase, pressure_guess)
+    )(*(pltpu.with_memory_space_constraint(x, pltpu.HBM) for x in (right_side, phase, pressure_guess)))
     own = lax.all_to_all(bricks, axes, 0, 0)
     before = lax.ppermute(own, axes, up)
     after = lax.ppermute(own, axes, down)
 
     coarse = planes // 4
-    fine = [struct(6, planes, WIN, width)] * 2 + [struct(planes, WIN, width)] * 4
-    half = [struct(6, coarse, WIN, width)] * 2 + [struct(coarse, WIN, width)] * 3
+    fine = [vmem(6, planes, WIN, width)] * 2 + [vmem(planes, WIN, width)] * 3
+    half = [vmem(6, coarse, WIN, width)] * 2 + [vmem(coarse, WIN, width)] * 2
+    kept = fine + half + [struct(planes, WIN, width), struct(coarse, WIN, width)]
     padded = [vmem(planes + 2, WIN + 2 * ROWS, width)] * 2
     cpadded = [vmem(coarse + 2, WIN + 2 * ROWS, width)] * 2
-    *state, packed, message = pl.pallas_call(
+    *state, message, packed = pl.pallas_call(
         down_kernel,
-        out_shape=fine + half + [struct(count, 2 * coarse, width), struct(coarse, ROWS, width)],
-        scratch_shapes=padded * 2 + cpadded * 2 + [vmem(coarse, WIN, width), vmem(WIN, width)],
+        out_shape=[pltpu.HBM(x.shape, x.dtype) for x in kept + [struct(coarse, ROWS, width)]] + [struct(count, 2 * coarse, width)],
+        out_specs=[pl.BlockSpec(memory_space=pltpu.HBM)] * (len(kept) + 1) + [pl.BlockSpec(memory_space=pltpu.VMEM)],
+        scratch_shapes=fine + half + padded * 2 + cpadded * 2 + [
+            vmem(coarse, WIN, width),
+            vmem(WIN, width),
+            vmem(coarse, ROWS, width),
+            pltpu.SemaphoreType.DMA((len(kept) + 1,)),
+        ],
         compiler_params=params,
         name="down",
     )(own, before, after)
@@ -659,15 +698,16 @@
     cycle = pl.pallas_call(
         functools.partial(up_kernel, columns),
         out_shape=struct(count, 3 * ROWS, 128),
-        scratch_shapes=padded + cpadded + [
-            vmem(coarse, WIN, width),
+        in_specs=[pl.BlockSpec(memory_space=pltpu.VMEM)] + [pl.BlockSpec(memory_space=pltpu.HBM)] * (len(kept) + 2),
+        scratch_shapes=fine + half + padded + cpadded + [vmem(coarse, ROWS, width)] * 2 + [
             vmem(2, 6, 2 * (2 * REACH + 1), coarse, width),
             vmem(WIN // 2 * coarse, width),
             vmem(WIN, width),
+            pltpu.SemaphoreType.DMA((len(kept) + 2,)),
         ],
         compiler_params=params,
         name="up",
-    )(gathered, e_before, e_after, *state)
+    )(gathered, *(pltpu.with_memory_space_constraint(x, pltpu.HBM) for x in (*state, e_before, e_after)))
     back = lax.all_to_all(cycle, axes, 0, 0)
     return pl.pallas_call(
         functools.partial(unpack_kernel, order),

time: 113 us -> 91.9 us (0.81)
  Pallas kernels: 39.8 us -> 21.2 us
  local copies, waits for them, and re-layouts: 1.59 us -> 0.01 us
    pallas_call x2, Pallas kernels: 22.2 us -> 13 us  [the longest x1 11.6 us: local_slabs(): pl.pallas_call(down_kernel, out_shape=[pltpu.HBM(x.shape, x.dtype) for x...]
    pallas_call x1, Pallas kernels: 15.7 us -> 7.23 us  [local_slabs(): pl.pallas_call(functools.partial(up_kernel, columns), out_shape=struct(co...]
    unnamed x12 -> x4, local copies, waits for them, and re-layouts: 1.59 us -> 0.01 us
where the time goes in v2:
time: 91.9 us; the launch traced here: 91.6 us
  blocking collectives  41.5 us (45%)
  Pallas kernels  21.2 us (23%)
  starting transfers between devices  20.3 us (22%)
  waiting for transfers between devices  7.9 us (9%)
    all_to_all x1, blocking collectives, local_slabs(): own = lax.all_to_all(bricks, axes, 0, 0)  25 us
    all_to_all x1, blocking collectives, local_slabs(): back = lax.all_to_all(cycle, axes, 0, 0)  16.5 us
    all_to_all x1, starting transfers between devices, local_slabs(): gathered = lax.all_to_all(packed, axes, 0, 0)  11.6 us
    pallas_call x1, Pallas kernels, local_slabs(): pl.pallas_call(down_kernel, out_shape=[pltpu.HBM(x.shape, x.dtype) for x...  11.6 us
    pallas_call x1, Pallas kernels, local_slabs(): pl.pallas_call(functools.partial(up_kernel, columns), out_shape=struct(co...  7.23 us
    all_to_all x1, waiting for transfers between devices, local_slabs(): gathered = lax.all_to_all(packed, axes, 0, 0)  5.21 us
    ppermute x1, starting transfers between devices, local_slabs(): before = lax.ppermute(own, axes, up)  3.07 us
    ppermute x1, starting transfers between devices, local_slabs(): e_before = lax.ppermute(message, axes, up)  3.03 us
  transfers between devices with their start and end apart: 5, of which 3 were waited for; matrix products, arithmetic and copies ran while one was open for 0% of the time, Pallas kernels for 0%

profile of v2, /device:TPU:0, one launch (start us, length us, event | category | flops | bytes accessed | tf_op | source)
XLA Modules:
  0.0 91.6 jit_solution(7355674079857702610)
XLA Ops:
  0.6 1.4 %pack.1 = f32[32,40,128]{2,1,0:T(8,128)S(1)} custom-call(f32[4,32,512]{2,1,0:T(8,128)} %source_hbm.1, s32[4,32,512]{2,1,0:T(8,128)} %phase_hbm.1, f32[4,32,512]{2,1,0:T(8,128)} %guess_hbm.1), custom_call_target="tpu_custom_call" | custom-call | tf_op jit(solution)/shard_map/pack/pallas_call | solution.py:657
  2.1 25.0 %all_to_all.15.own = f32[32,40,128]{2,1,0:T(8,128)S(1)} all-to-all(f32[32,40,128]{2,1,0:T(8,128)S(1)} %pack.1), channel_id=1, replica_groups=mesh['gx'=8,'yz'=4] {'gx','yz'}, dimensions={0} | all-to-all | bytes 1310720 | tf_op jit(solution)/shard_map/all_to_all | solution.py:671
  27.1 1.3 %collective-permute-start.1 = (f32[32,40,128]{2,1,0:T(8,128)S(1)}, f32[32,40,128]{2,1,0:T(8,128)S(1)}, u32[]{:S(2)}, u32[]{:S(2)}) collective-permute-start(f32[32,40,128]{2,1,0:T(8,128)S(1)} %all_to_all.15.own), channel_id=1, source_target_pairs={{1,0},{2,1},{3,2},{7,3},{6,7},{5,6},{4,5},{12,4},{13,12},{14,13},{... | collective-permute-start | bytes 1966088 | tf_op jit(solution)/shard_map/ppermute | solution.py:673
  28.4 3.1 %collective-permute-start = (f32[32,40,128]{2,1,0:T(8,128)S(1)}, f32[32,40,128]{2,1,0:T(8,128)S(1)}, u32[]{:S(2)}, u32[]{:S(2)}) collective-permute-start(f32[32,40,128]{2,1,0:T(8,128)S(1)} %all_to_all.15.own), channel_id=1, source_target_pairs={{0,1},{1,2},{2,3},{3,7},{7,6},{6,5},{5,4},{4,12},{12,13},{13,14},{... | collective-permute-start | bytes 1966088 | tf_op jit(solution)/shard_map/ppermute | solution.py:672
  31.5 0.0 collective-permute-done.1.after
  31.5 1.7 %collective-permute-done.before = f32[32,40,128]{2,1,0:T(8,128)S(1)} collective-permute-done((f32[32,40,128]{2,1,0:T(8,128)S(1)}, f32[32,40,128]{2,1,0:T(8,128)S(1)}, u32[]{:S(2)}, u32[]{:S(2)}) %collective-permute-start) | collective-permute-done | bytes 655392 | tf_op jit(solution)/shard_map/ppermute | solution.py:672
  33.1 11.6 %down.1 = (f32[6,32,24,128]{3,2,1,0:T(8,128)}, f32[6,32,24,128]{3,2,1,0:T(8,128)}, f32[32,24,128]{2,1,0:T(8,128)}, f32[32,24,128]{2,1,0:T(8,128)}, f32[32,24,128...) custom-call(f32[32,40,128]{2,1,0:T(8,128)S(1)} %all_to_all.15.own, ...), custom_call_target="tpu_custom_call" | custom-call | tf_op jit(solution)/shard_map/down/pallas_call | solution.py:681
  44.7 11.6 %all-to-all-start.1 = ((f32[32,16,128]{2,1,0:T(8,128)}), f32[32,16,128]{2,1,0:T(8,128)S(1)}, u32[]{:S(2)}, u32[]{:S(2)}) async-start(f32[32,16,128]{2,1,0:T(8,128)} %get-tuple-element.15), calls=%async_computation.1 | async-start | bytes 524288 | tf_op jit(solution)/shard_map/all_to_all | solution.py:694
  56.4 1.3 %collective-permute-start.3 = (f32[8,8,128]{2,1,0:T(8,128)}, f32[8,8,128]{2,1,0:T(8,128)S(1)}, u32[]{:S(2)}, u32[]{:S(2)}) collective-permute-start(f32[8,8,128]{2,1,0:T(8,128)} %get-tuple-element.27), channel_id=1, source_target_pairs={{1,0},{2,1},{3,2},{7,3},{6,7},{5,6},{4,5},{12,4},{13,12},{14,13},{... | collective-permute-start | bytes 98312 | tf_op jit(solution)/shard_map/ppermute | solution.py:696
  57.7 3.0 %collective-permute-start.2 = (f32[8,8,128]{2,1,0:T(8,128)}, f32[8,8,128]{2,1,0:T(8,128)S(1)}, u32[]{:S(2)}, u32[]{:S(2)}) collective-permute-start(f32[8,8,128]{2,1,0:T(8,128)} %get-tuple-element.27), channel_id=1, source_target_pairs={{0,1},{1,2},{2,3},{3,7},{7,6},{6,5},{5,4},{4,12},{12,13},{13,14},{... | collective-permute-start | bytes 98312 | tf_op jit(solution)/shard_map/ppermute | solution.py:695
  60.7 0.0 collective-permute-done.3.refs_12_
  60.7 0.0 copy-start
  60.7 1.0 %collective-permute-done.2.refs_11_ = f32[8,8,128]{2,1,0:T(8,128)S(1)} collective-permute-done((f32[8,8,128]{2,1,0:T(8,128)}, f32[8,8,128]{2,1,0:T(8,128)S(1)}, u32[]{:S(2)}, u32[]{:S(2)}) %collective-permute-start.2) | collective-permute-done | bytes 32800 | tf_op jit(solution)/shard_map/ppermute | solution.py:695
  61.8 0.0 copy-start.1
  61.8 5.2 %all-to-all-done.1.gathered = f32[32,16,128]{2,1,0:T(8,128)S(1)} async-done(((f32[32,16,128]{2,1,0:T(8,128)}), f32[32,16,128]{2,1,0:T(8,128)S(1)}, u32[]{:S(2)}, u32[]{:S(2)}) %all-to-all-start.1) | async-done | bytes 262176 | tf_op jit(solution)/shard_map/all_to_all | solution.py:694
  67.0 0.0 copy-done
  67.0 0.0 copy-done.1
  67.0 7.2 %up.1 = f32[32,24,128]{2,1,0:T(8,128)S(1)} custom-call(f32[32,16,128]{2,1,0:T(8,128)S(1)} %all-to-all-done.1.gathered, f32[6,32,24,128]{3,2,1,0:T(8,128)} %get-tuple-element.16.refs_0_, f32[6,32,24,128]{3,2,1,0:T(8,128)} %get-tuple-element.17.refs_1_, f32[32,24,128]{2,1,0:T(8,128)} %get-tuple-element.18.refs_2_, f32[32,24,128]{2,1,0:T(8,128)} %get-tuple-element.19.refs_3_, ...), custom_call_target="tpu_custom_call" | custom-call | tf_op jit(solution)/shard_map/up/pallas_call | solution.py:698
  74.2 16.5 %all_to_all.16.in_ref = f32[32,24,128]{2,1,0:T(8,128)S(1)} all-to-all(f32[32,24,128]{2,1,0:T(8,128)S(1)} %up.1), channel_id=1, replica_groups=mesh['gx'=8,'yz'=4] {'gx','yz'}, dimensions={0} | all-to-all | bytes 786432 | tf_op jit(solution)/shard_map/all_to_all | solution.py:711
  90.7 0.9 %unpack.1 = (f32[4,32,512]{2,1,0:T(8,128)}, f32[4,32,512]{2,1,0:T(8,128)}) custom-call(f32[32,24,128]{2,1,0:T(8,128)S(1)} %all_to_all.16.in_ref), custom_call_target="tpu_custom_call" | custom-call | tf_op jit(solution)/shard_map/unpack/pallas_call | solution.py:712
Async XLA Ops:
  27.1 4.4 %collective-permute-start.1 = (f32[32,40,128]{2,1,0:T(8,128)S(1)}, f32[32,40,128]{2,1,0:T(8,128)S(1)}, u32[]{:S(2)}, u32[]{:S(2)}) collective-permute-start(f32[32,40,128]{2,1,0:T(8,128)S(1)} %all_to_all.15.own), channel_id=1, source_target_pairs={{1,0},{2,1},{3,2},{7,3},{6,7},{5,6},{4,5},{12,4},{13,12},{14,13},{... | collective-permute-start | bytes 1966088 | tf_op jit(solution)/shard_map/ppermute | solution.py:673
  28.4 4.7 %collective-permute-start = (f32[32,40,128]{2,1,0:T(8,128)S(1)}, f32[32,40,128]{2,1,0:T(8,128)S(1)}, u32[]{:S(2)}, u32[]{:S(2)}) collective-permute-start(f32[32,40,128]{2,1,0:T(8,128)S(1)} %all_to_all.15.own), channel_id=1, source_target_pairs={{0,1},{1,2},{2,3},{3,7},{7,6},{6,5},{5,4},{4,12},{12,13},{13,14},{... | collective-permute-start | bytes 1966088 | tf_op jit(solution)/shard_map/ppermute | solution.py:672
  44.7 22.2 %all-to-all-start.1 = ((f32[32,16,128]{2,1,0:T(8,128)}), f32[32,16,128]{2,1,0:T(8,128)S(1)}, u32[]{:S(2)}, u32[]{:S(2)}) async-start(f32[32,16,128]{2,1,0:T(8,128)} %get-tuple-element.15), calls=%async_computation.1 | async-start | bytes 524288 | tf_op jit(solution)/shard_map/all_to_all | solution.py:694
  56.4 4.3 %collective-permute-start.3 = (f32[8,8,128]{2,1,0:T(8,128)}, f32[8,8,128]{2,1,0:T(8,128)S(1)}, u32[]{:S(2)}, u32[]{:S(2)}) collective-permute-start(f32[8,8,128]{2,1,0:T(8,128)} %get-tuple-element.27), channel_id=1, source_target_pairs={{1,0},{2,1},{3,2},{7,3},{6,7},{5,6},{4,5},{12,4},{13,12},{14,13},{... | collective-permute-start | bytes 98312 | tf_op jit(solution)/shard_map/ppermute | solution.py:696
  57.7 4.1 %collective-permute-start.2 = (f32[8,8,128]{2,1,0:T(8,128)}, f32[8,8,128]{2,1,0:T(8,128)S(1)}, u32[]{:S(2)}, u32[]{:S(2)}) collective-permute-start(f32[8,8,128]{2,1,0:T(8,128)} %get-tuple-element.27), channel_id=1, source_target_pairs={{0,1},{1,2},{2,3},{3,7},{7,6},{6,5},{5,4},{4,12},{12,13},{13,14},{... | collective-permute-start | bytes 98312 | tf_op jit(solution)/shard_map/ppermute | solution.py:695
  60.7 6.3 %copy-start = (f32[8,8,128]{2,1,0:T(8,128)}, f32[8,8,128]{2,1,0:T(8,128)S(1)}, u32[]{:S(2)}) copy-start(f32[8,8,128]{2,1,0:T(8,128)S(1)} %collective-permute-done.3.refs_12_) | copy-start | bytes 98308
  61.8 5.2 %copy-start.1 = (f32[8,8,128]{2,1,0:T(8,128)}, f32[8,8,128]{2,1,0:T(8,128)S(1)}, u32[]{:S(2)}) copy-start(f32[8,8,128]{2,1,0:T(8,128)S(1)} %collective-permute-done.2.refs_11_) | copy-start | bytes 98308

commit v3 on v2

--- a/solution.py
+++ b/solution.py
@@ -203,16 +203,14 @@
 
 def swap_blocks(tiles):
     block = lanes(tiles[0].shape) // 32
-    low, even = block < 2, block % 2 == 0
-    t = [None] * 4
-    for a in (0, 1):
-        t[a] = jnp.where(low, tiles[a], pltpu.roll(tiles[a + 2], 64, 1))
-        t[a + 2] = jnp.where(low, pltpu.roll(tiles[a], 64, 1), tiles[a + 2])
-    out = [None] * 4
-    for a in (0, 2):
-        out[a] = jnp.where(even, t[a], pltpu.roll(t[a + 1], 32, 1))
-        out[a + 1] = jnp.where(even, pltpu.roll(t[a], 96, 1), t[a + 1])
-    return out
+    at = [block == b for b in range(3)]
+
+    def choose(four):
+        return jnp.where(at[0], four[0], jnp.where(at[1], four[1], jnp.where(at[2], four[2], four[3])))
+
+    turned = [choose([tiles[(b + d) % 4] for b in range(4)]) for d in range(4)]
+    turned = [turned[0]] + [pltpu.roll(turned[d], 32 * d, 1) for d in (1, 2, 3)]
+    return [choose([turned[(b - a) % 4] for b in range(4)]) for a in range(4)]
 
 
 def brick_parity(shape):
@@ -322,7 +320,7 @@
 
 
 def mean_fine(u, w):
-    return jnp.where(u == w, u, u * w * MIX)
+    return jnp.where(u == w, u, (u * MIX) * w)
 
 
 def mean_any(u, w):
@@ -363,7 +361,7 @@
             target[x + 1, MID, :] = relax(scaled[x], share[:, x], sides)
         return 0
 
-    lax.fori_loop(0, planes // 2, two, 0, unroll=4)
+    lax.fori_loop(0, planes // 2, two, 0, unroll=True)
 
 
 def coarse_pass(colour, target, other, share, scaled):
@@ -374,7 +372,7 @@
         target[i + 1, MID, :] = relax(scaled[i], share[:, i], sides)
         return 0
 
-    lax.fori_loop(0, planes, one, 0, unroll=4)
+    lax.fori_loop(0, planes, one, 0, unroll=True)
 
 
 def down_kernel(
@@ -403,7 +401,7 @@
                     to[4 * i + j + shift, row : row + ROWS, :] = tile
         return 0
 
-    lax.fori_loop(0, planes // 4, unfold, 0)
+    lax.fori_loop(0, planes // 4, unfold, 0, unroll=True)
 
     lane = lanes((WIN, width))
 
@@ -423,7 +421,7 @@
                     diagonal0[x] = diagonal
         return 0
 
-    lax.fori_loop(0, planes // 2, fine_weights, 0)
+    lax.fori_loop(0, planes // 2, fine_weights, 0, unroll=2)
     for copy in copies[:5]:
         copy.start()
 
@@ -451,7 +449,7 @@
         cm1[i + 1, MID, :] = jnp.where(even, mobilities[1], mobilities[0])
         return 0
 
-    lax.fori_loop(0, planes // 4, restrict, 0)
+    lax.fori_loop(0, planes // 4, restrict, 0, unroll=2)
 
     def coarse_weights(i, _):
         for colour, mine, other, share, scaled in ((0, cm0, cm1, cshare0, cscaled0), (1, cm1, cm0, cshare1, cscaled1)):
@@ -466,7 +464,7 @@
         e0[i + 1, MID, :] = cscaled0[i]
         return 0
 
-    lax.fori_loop(0, planes // 4, coarse_weights, 0)
+    lax.fori_loop(0, planes // 4, coarse_weights, 0, unroll=True)
     for copy in copies[5 : KEPT - 2]:
         copy.start()
 
@@ -632,7 +630,7 @@
                 out[4 * i + j, a * ROWS : (a + 1) * ROWS, :] = tile
         return 0
 
-    lax.fori_loop(0, rows, fold, 0)
+    lax.fori_loop(0, rows, fold, 0, unroll=True)
 
 
 def local_slabs(shape, right_side, phase, pressure_guess):

time: 91.9 us -> 84.7 us (0.922)
  Pallas kernels: 21.2 us -> 13.9 us
    pallas_call x1, Pallas kernels: 11.6 us -> 6.9 us  [local_slabs(): pl.pallas_call(down_kernel, out_shape=[pltpu.HBM(x.shape, x.dtype) for x...]
    pallas_call x1, Pallas kernels: 7.23 us -> 4.64 us  [local_slabs(): pl.pallas_call(functools.partial(up_kernel, columns), out_shape=struct(co...]
where the time goes in v3:
time: 84.7 us; the launch traced here: 84.4 us
  blocking collectives  41.5 us (49%)
  starting transfers between devices  20.3 us (24%)
  Pallas kernels  13.9 us (16%)
  waiting for transfers between devices  7.9 us (9%)
    all_to_all x1, blocking collectives, local_slabs(): own = lax.all_to_all(bricks, axes, 0, 0)  25 us
    all_to_all x1, blocking collectives, local_slabs(): back = lax.all_to_all(cycle, axes, 0, 0)  16.5 us
    all_to_all x1, starting transfers between devices, local_slabs(): gathered = lax.all_to_all(packed, axes, 0, 0)  11.6 us
    pallas_call x1, Pallas kernels, local_slabs(): pl.pallas_call(down_kernel, out_shape=[pltpu.HBM(x.shape, x.dtype) for x...  6.9 us
    all_to_all x1, waiting for transfers between devices, local_slabs(): gathered = lax.all_to_all(packed, axes, 0, 0)  5.21 us
    pallas_call x1, Pallas kernels, local_slabs(): pl.pallas_call(functools.partial(up_kernel, columns), out_shape=struct(co...  4.64 us
    ppermute x1, starting transfers between devices, local_slabs(): before = lax.ppermute(own, axes, up)  3.07 us
    ppermute x1, starting transfers between devices, local_slabs(): e_before = lax.ppermute(message, axes, up)  3.03 us
  transfers between devices with their start and end apart: 5, of which 3 were waited for; matrix products, arithmetic and copies ran while one was open for 0% of the time, Pallas kernels for 0%

profile of v3, /device:TPU:0, one launch (start us, length us, event | category | flops | bytes accessed | tf_op | source)
XLA Modules:
  0.0 84.4 jit_solution(5720031760105617127)
XLA Ops:
  0.6 1.4 %pack.1 = f32[32,40,128]{2,1,0:T(8,128)S(1)} custom-call(f32[4,32,512]{2,1,0:T(8,128)} %source_hbm.1, s32[4,32,512]{2,1,0:T(8,128)} %phase_hbm.1, f32[4,32,512]{2,1,0:T(8,128)} %guess_hbm.1), custom_call_target="tpu_custom_call" | custom-call | tf_op jit(solution)/shard_map/pack/pallas_call | solution.py:655
  2.1 25.0 %all_to_all.15.own = f32[32,40,128]{2,1,0:T(8,128)S(1)} all-to-all(f32[32,40,128]{2,1,0:T(8,128)S(1)} %pack.1), channel_id=1, replica_groups=mesh['gx'=8,'yz'=4] {'gx','yz'}, dimensions={0} | all-to-all | bytes 1310720 | tf_op jit(solution)/shard_map/all_to_all | solution.py:669
  27.1 1.3 %collective-permute-start.1 = (f32[32,40,128]{2,1,0:T(8,128)S(1)}, f32[32,40,128]{2,1,0:T(8,128)S(1)}, u32[]{:S(2)}, u32[]{:S(2)}) collective-permute-start(f32[32,40,128]{2,1,0:T(8,128)S(1)} %all_to_all.15.own), channel_id=1, source_target_pairs={{1,0},{2,1},{3,2},{7,3},{6,7},{5,6},{4,5},{12,4},{13,12},{14,13},{... | collective-permute-start | bytes 1966088 | tf_op jit(solution)/shard_map/ppermute | solution.py:671
  28.4 3.1 %collective-permute-start = (f32[32,40,128]{2,1,0:T(8,128)S(1)}, f32[32,40,128]{2,1,0:T(8,128)S(1)}, u32[]{:S(2)}, u32[]{:S(2)}) collective-permute-start(f32[32,40,128]{2,1,0:T(8,128)S(1)} %all_to_all.15.own), channel_id=1, source_target_pairs={{0,1},{1,2},{2,3},{3,7},{7,6},{6,5},{5,4},{4,12},{12,13},{13,14},{... | collective-permute-start | bytes 1966088 | tf_op jit(solution)/shard_map/ppermute | solution.py:670
  31.5 0.0 collective-permute-done.1.after
  31.5 1.7 %collective-permute-done.before = f32[32,40,128]{2,1,0:T(8,128)S(1)} collective-permute-done((f32[32,40,128]{2,1,0:T(8,128)S(1)}, f32[32,40,128]{2,1,0:T(8,128)S(1)}, u32[]{:S(2)}, u32[]{:S(2)}) %collective-permute-start) | collective-permute-done | bytes 655392 | tf_op jit(solution)/shard_map/ppermute | solution.py:670
  33.1 6.9 %down.1 = (f32[6,32,24,128]{3,2,1,0:T(8,128)}, f32[6,32,24,128]{3,2,1,0:T(8,128)}, f32[32,24,128]{2,1,0:T(8,128)}, f32[32,24,128]{2,1,0:T(8,128)}, f32[32,24,128...) custom-call(f32[32,40,128]{2,1,0:T(8,128)S(1)} %all_to_all.15.own, ...), custom_call_target="tpu_custom_call" | custom-call | tf_op jit(solution)/shard_map/down/pallas_call | solution.py:679
  40.0 11.6 %all-to-all-start.1 = ((f32[32,16,128]{2,1,0:T(8,128)}), f32[32,16,128]{2,1,0:T(8,128)S(1)}, u32[]{:S(2)}, u32[]{:S(2)}) async-start(f32[32,16,128]{2,1,0:T(8,128)} %get-tuple-element.15), calls=%async_computation.1 | async-start | bytes 524288 | tf_op jit(solution)/shard_map/all_to_all | solution.py:692
  51.7 1.3 %collective-permute-start.3 = (f32[8,8,128]{2,1,0:T(8,128)}, f32[8,8,128]{2,1,0:T(8,128)S(1)}, u32[]{:S(2)}, u32[]{:S(2)}) collective-permute-start(f32[8,8,128]{2,1,0:T(8,128)} %get-tuple-element.27), channel_id=1, source_target_pairs={{1,0},{2,1},{3,2},{7,3},{6,7},{5,6},{4,5},{12,4},{13,12},{14,13},{... | collective-permute-start | bytes 98312 | tf_op jit(solution)/shard_map/ppermute | solution.py:694
  53.0 3.0 %collective-permute-start.2 = (f32[8,8,128]{2,1,0:T(8,128)}, f32[8,8,128]{2,1,0:T(8,128)S(1)}, u32[]{:S(2)}, u32[]{:S(2)}) collective-permute-start(f32[8,8,128]{2,1,0:T(8,128)} %get-tuple-element.27), channel_id=1, source_target_pairs={{0,1},{1,2},{2,3},{3,7},{7,6},{6,5},{5,4},{4,12},{12,13},{13,14},{... | collective-permute-start | bytes 98312 | tf_op jit(solution)/shard_map/ppermute | solution.py:693
  56.0 0.0 collective-permute-done.3.refs_12_
  56.0 0.0 copy-start
  56.0 1.0 %collective-permute-done.2.refs_11_ = f32[8,8,128]{2,1,0:T(8,128)S(1)} collective-permute-done((f32[8,8,128]{2,1,0:T(8,128)}, f32[8,8,128]{2,1,0:T(8,128)S(1)}, u32[]{:S(2)}, u32[]{:S(2)}) %collective-permute-start.2) | collective-permute-done | bytes 32800 | tf_op jit(solution)/shard_map/ppermute | solution.py:693
  57.1 0.0 copy-start.1
  57.1 5.2 %all-to-all-done.1.gathered = f32[32,16,128]{2,1,0:T(8,128)S(1)} async-done(((f32[32,16,128]{2,1,0:T(8,128)}), f32[32,16,128]{2,1,0:T(8,128)S(1)}, u32[]{:S(2)}, u32[]{:S(2)}) %all-to-all-start.1) | async-done | bytes 262176 | tf_op jit(solution)/shard_map/all_to_all | solution.py:692
  62.3 0.0 copy-done
  62.3 0.0 copy-done.1
  62.3 4.6 %up.1 = f32[32,24,128]{2,1,0:T(8,128)S(1)} custom-call(f32[32,16,128]{2,1,0:T(8,128)S(1)} %all-to-all-done.1.gathered, f32[6,32,24,128]{3,2,1,0:T(8,128)} %get-tuple-element.16.refs_0_, f32[6,32,24,128]{3,2,1,0:T(8,128)} %get-tuple-element.17.refs_1_, f32[32,24,128]{2,1,0:T(8,128)} %get-tuple-element.18.refs_2_, f32[32,24,128]{2,1,0:T(8,128)} %get-tuple-element.19.refs_3_, ...), custom_call_target="tpu_custom_call" | custom-call | tf_op jit(solution)/shard_map/up/pallas_call | solution.py:696
  66.9 16.5 %all_to_all.16.in_ref = f32[32,24,128]{2,1,0:T(8,128)S(1)} all-to-all(f32[32,24,128]{2,1,0:T(8,128)S(1)} %up.1), channel_id=1, replica_groups=mesh['gx'=8,'yz'=4] {'gx','yz'}, dimensions={0} | all-to-all | bytes 786432 | tf_op jit(solution)/shard_map/all_to_all | solution.py:709
  83.4 0.9 %unpack.1 = (f32[4,32,512]{2,1,0:T(8,128)}, f32[4,32,512]{2,1,0:T(8,128)}) custom-call(f32[32,24,128]{2,1,0:T(8,128)S(1)} %all_to_all.16.in_ref), custom_call_target="tpu_custom_call" | custom-call | tf_op jit(solution)/shard_map/unpack/pallas_call | solution.py:710
Async XLA Ops:
  27.1 4.4 %collective-permute-start.1 = (f32[32,40,128]{2,1,0:T(8,128)S(1)}, f32[32,40,128]{2,1,0:T(8,128)S(1)}, u32[]{:S(2)}, u32[]{:S(2)}) collective-permute-start(f32[32,40,128]{2,1,0:T(8,128)S(1)} %all_to_all.15.own), channel_id=1, source_target_pairs={{1,0},{2,1},{3,2},{7,3},{6,7},{5,6},{4,5},{12,4},{13,12},{14,13},{... | collective-permute-start | bytes 1966088 | tf_op jit(solution)/shard_map/ppermute | solution.py:671
  28.4 4.7 %collective-permute-start = (f32[32,40,128]{2,1,0:T(8,128)S(1)}, f32[32,40,128]{2,1,0:T(8,128)S(1)}, u32[]{:S(2)}, u32[]{:S(2)}) collective-permute-start(f32[32,40,128]{2,1,0:T(8,128)S(1)} %all_to_all.15.own), channel_id=1, source_target_pairs={{0,1},{1,2},{2,3},{3,7},{7,6},{6,5},{5,4},{4,12},{12,13},{13,14},{... | collective-permute-start | bytes 1966088 | tf_op jit(solution)/shard_map/ppermute | solution.py:670
  40.0 22.2 %all-to-all-start.1 = ((f32[32,16,128]{2,1,0:T(8,128)}), f32[32,16,128]{2,1,0:T(8,128)S(1)}, u32[]{:S(2)}, u32[]{:S(2)}) async-start(f32[32,16,128]{2,1,0:T(8,128)} %get-tuple-element.15), calls=%async_computation.1 | async-start | bytes 524288 | tf_op jit(solution)/shard_map/all_to_all | solution.py:692
  51.7 4.3 %collective-permute-start.3 = (f32[8,8,128]{2,1,0:T(8,128)}, f32[8,8,128]{2,1,0:T(8,128)S(1)}, u32[]{:S(2)}, u32[]{:S(2)}) collective-permute-start(f32[8,8,128]{2,1,0:T(8,128)} %get-tuple-element.27), channel_id=1, source_target_pairs={{1,0},{2,1},{3,2},{7,3},{6,7},{5,6},{4,5},{12,4},{13,12},{14,13},{... | collective-permute-start | bytes 98312 | tf_op jit(solution)/shard_map/ppermute | solution.py:694
  53.0 4.1 %collective-permute-start.2 = (f32[8,8,128]{2,1,0:T(8,128)}, f32[8,8,128]{2,1,0:T(8,128)S(1)}, u32[]{:S(2)}, u32[]{:S(2)}) collective-permute-start(f32[8,8,128]{2,1,0:T(8,128)} %get-tuple-element.27), channel_id=1, source_target_pairs={{0,1},{1,2},{2,3},{3,7},{7,6},{6,5},{5,4},{4,12},{12,13},{13,14},{... | collective-permute-start | bytes 98312 | tf_op jit(solution)/shard_map/ppermute | solution.py:693
  56.0 6.3 %copy-start = (f32[8,8,128]{2,1,0:T(8,128)}, f32[8,8,128]{2,1,0:T(8,128)S(1)}, u32[]{:S(2)}) copy-start(f32[8,8,128]{2,1,0:T(8,128)S(1)} %collective-permute-done.3.refs_12_) | copy-start | bytes 98308
  57.1 5.2 %copy-start.1 = (f32[8,8,128]{2,1,0:T(8,128)}, f32[8,8,128]{2,1,0:T(8,128)S(1)}, u32[]{:S(2)}) copy-start(f32[8,8,128]{2,1,0:T(8,128)S(1)} %collective-permute-done.2.refs_11_) | copy-start | bytes 98308

commit v4 on v3

--- a/solution.py
+++ b/solution.py
@@ -257,9 +257,14 @@
 
 
 KEPT = 11
+ALL = (0, WIN)
+INNER = (ROWS // 2, WIN - ROWS // 2)
+OWN = (ROWS, 2 * ROWS)
 MID = slice(ROWS, ROWS + WIN)
-BELOW = slice(ROWS - 1, ROWS + WIN - 1)
-ABOVE = slice(ROWS + 1, ROWS + WIN + 1)
+
+
+def shifted(rows, by):
+    return slice(ROWS + rows[0] + by, ROWS + rows[1] + by)
 
 
 def clear_edges(ref):
@@ -276,29 +281,31 @@
     lax.fori_loop(1, planes - 1, one, 0)
 
 
-def around_fine(ref, x, low):
-    centre = ref[x + 1, MID, :]
+def around_fine(ref, x, low, rows=ALL):
+    here = shifted(rows, 0)
+    centre = ref[x + 1, here, :]
     width = centre.shape[1]
     return (
-        ref[x, MID, :],
-        ref[x + 2, MID, :],
+        ref[x, here, :],
+        ref[x + 2, here, :],
         pltpu.roll(centre, 1, 1),
         pltpu.roll(centre, width - 1, 1),
         centre,
-        jnp.where(low, ref[x + 1, BELOW, :], ref[x + 1, ABOVE, :]),
+        jnp.where(low, ref[x + 1, shifted(rows, -1), :], ref[x + 1, shifted(rows, 1), :]),
     )
 
 
-def around_coarse(ref, i, low):
-    centre = ref[i + 1, MID, :]
+def around_coarse(ref, i, low, rows=ALL):
+    here = shifted(rows, 0)
+    centre = ref[i + 1, here, :]
     width = centre.shape[1]
     return (
-        ref[i + 1, BELOW, :],
-        ref[i + 1, ABOVE, :],
+        ref[i + 1, shifted(rows, -1), :],
+        ref[i + 1, shifted(rows, 1), :],
         pltpu.roll(centre, 2, 1),
         pltpu.roll(centre, width - 2, 1),
         centre,
-        jnp.where(low, ref[i, MID, :], ref[i + 2, MID, :]),
+        jnp.where(low, ref[i, here, :], ref[i + 2, here, :]),
     )
 
 
@@ -342,73 +349,101 @@
     return scaled + ((parts[0] + parts[1]) + (parts[2] + parts[3]) + (parts[4] + parts[5]))
 
 
-def fine_low(x_parity, colour, width):
-    return (lanes((WIN, width)) + (x_parity + colour)) % 2 == 0
-
-
-def coarse_low(colour, width):
-    row = lax.broadcasted_iota(jnp.int32, (WIN, width), 0)
-    return (row + lanes((WIN, width)) // 2 + colour) % 2 == 0
-
-
-def fine_pass(colour, target, other, share, scaled):
+def fine_low(x_parity, colour, width, rows=ALL):
+    return (lanes((rows[1] - rows[0], width)) + (x_parity + colour)) % 2 == 0
+
+
+def coarse_low(colour, width, rows=ALL):
+    shape = (rows[1] - rows[0], width)
+    row = lax.broadcasted_iota(jnp.int32, shape, 0) + rows[0]
+    return (row + lanes(shape) // 2 + colour) % 2 == 0
+
+
+def fine_pass(colour, target, other, share, scaled, rows=ALL):
     planes, width = share.shape[1], share.shape[3]
+    part = slice(*rows)
 
     def two(i, _):
         for parity in (0, 1):
             x = 2 * i + parity
-            sides = around_fine(other, x, fine_low(parity, colour, width))
-            target[x + 1, MID, :] = relax(scaled[x], share[:, x], sides)
+            sides = around_fine(other, x, fine_low(parity, colour, width, rows), rows)
+            target[x + 1, shifted(rows, 0), :] = relax(scaled[x, part, :], share[:, x, part, :], sides)
         return 0
 
     lax.fori_loop(0, planes // 2, two, 0, unroll=True)
 
 
-def coarse_pass(colour, target, other, share, scaled):
+def coarse_pass(colour, target, other, share, scaled, rows=ALL):
     planes, width = share.shape[1], share.shape[3]
+    part = slice(*rows)
 
     def one(i, _):
-        sides = around_coarse(other, i, coarse_low(colour, width))
-        target[i + 1, MID, :] = relax(scaled[i], share[:, i], sides)
+        sides = around_coarse(other, i, coarse_low(colour, width, rows), rows)
+        target[i + 1, shifted(rows, 0), :] = relax(scaled[i, part, :], share[:, i, part, :], sides)
         return 0
 
     lax.fori_loop(0, planes, one, 0, unroll=True)
 
 
-def down_kernel(
-    own, before, after,
-    *refs,
-):
-    kept, packed = refs[: KEPT + 1], refs[KEPT + 1]
-    state, work = refs[KEPT + 2 : 2 * KEPT], refs[2 * KEPT :]
-    share0, share1, scaled0, scaled1, diagonal0, cshare0, cshare1, cscaled0, cscaled1 = state
-    m0, m1, v0, v1, cm0, cm1, e0, e1, cdiagonal0, rest, message, done = work
+def neighbour_rows(columns):
+    near = jnp.where(slab_index(columns) % 2 == 0, 2 * ROWS, 0)
+    return pl.multiple_of(near, ROWS), pl.multiple_of(2 * ROWS - near, ROWS)
+
+
+def unfold_slabs(places, arrays, planes):
+    def unfold(i, _):
+        for ref, start, at in places:
+            for first, store in arrays:
+                tiles = [ref[4 * i + j, start + first : start + first + ROWS, :] for j in range(4)]
+                for j, tile in enumerate(swap_blocks(tiles)):
+                    store(4 * i + j, at, tile)
+        return 0
+
+    lax.fori_loop(0, planes // 4, unfold, 0, unroll=True)
+
+
+def padded_store(ref):
+    def store(x, at, tile):
+        ref[x + 1, pl.ds(at + ROWS, ROWS), :] = tile
+
+    return store
+
+
+def scaled_store(ref, factor):
+    def store(x, at, tile):
+        rows = pl.ds(at, ROWS)
+        ref[x, rows, :] = tile * factor[x, rows, :]
+
+    return store
+
+
+def pair_sum(ref):
+    return ref[ROWS : 2 * ROWS, :] + ref[ROWS + 1 : 2 * ROWS + 1, :]
+
+
+def picked(width):
+    row = lax.broadcasted_iota(jnp.int32, (ROWS, width), 0)
+    return jnp.logical_and(row % 2 == 0, lanes((ROWS, width)) % 4 == row // 2)
+
+
+def weights_kernel(columns, own, near, far, *refs):
+    share0, share1, inverse0, inverse1, diagonal0, cshare0, cshare1, cinverse0, cinverse1, cdiagonal0, packed = refs[:11]
+    kept, (m0, m1, cm0, cm1, rest, done) = refs[11:16], refs[16:]
+    held = (share0, share1, diagonal0, cshare0, cshare1)
+    copies = [pltpu.make_async_copy(ref, hbm, done.at[k]) for k, (ref, hbm) in enumerate(zip(held, kept))]
     planes, width = share0.shape[1], share0.shape[3]
-    coarse = planes // 4
-    held = list(state) + [v1.at[1 : planes + 1, MID, :], e1.at[1 : coarse + 1, MID, :], message]
-    copies = [pltpu.make_async_copy(ref, hbm, done.at[k]) for k, (ref, hbm) in enumerate(zip(held, kept))]
-    for ref in (m0, m1, v0, v1, cm0, cm1, e0, e1):
+    for ref in (m0, m1, cm0, cm1):
         clear_edges(ref)
-
-    def unfold(i, _):
-        for slab, ref in enumerate((before, own, after)):
-            at = slab * ROWS
-            for a, to in enumerate((m0, m1, scaled0, scaled1, v1)):
-                tiles = [ref[4 * i + j, a * ROWS : (a + 1) * ROWS, :] for j in range(4)]
-                shift = 1 if a in (0, 1, 4) else 0
-                for j, tile in enumerate(swap_blocks(tiles)):
-                    row = at + ROWS * shift
-                    to[4 * i + j + shift, row : row + ROWS, :] = tile
-        return 0
-
-    lax.fori_loop(0, planes // 4, unfold, 0, unroll=True)
+    near_at, far_at = neighbour_rows(columns)
+    places = ((own, 0, ROWS), (near, 0, near_at), (far, 0, far_at))
+    unfold_slabs(places, ((0, padded_store(m0)), (ROWS, padded_store(m1))), planes)
 
     lane = lanes((WIN, width))
 
     def fine_weights(i, _):
         for parity in (0, 1):
             x = 2 * i + parity
-            for colour, mine, other, share, scaled in ((0, m0, m1, share0, scaled0), (1, m1, m0, share1, scaled1)):
+            for colour, mine, other, share, factor in ((0, m0, m1, share0, inverse0), (1, m1, m0, share1, inverse1)):
                 low = fine_low(parity, colour, width)
                 u = mine[x + 1, MID, :]
                 sides = walls(around_fine(other, x, low), lane == 0, lane == width - 1)
@@ -416,35 +451,23 @@
                 shares, inverse, diagonal = weights(mean_fine, u, sides, top)
                 for a in range(6):
                     share[a, x] = shares[a]
-                scaled[x] = scaled[x] * inverse
+                factor[x] = inverse
                 if colour == 0:
                     diagonal0[x] = diagonal
         return 0
 
     lax.fori_loop(0, planes // 2, fine_weights, 0, unroll=2)
-    for copy in copies[:5]:
+    for copy in copies[:3]:
         copy.start()
 
-    for _ in range(SWEEPS):
-        fine_pass(0, v0, v1, share0, scaled0)
-        fine_pass(1, v1, v0, share1, scaled1)
-    copies[KEPT - 2].start()
-
     even = coarse_low(0, width)
 
     def restrict(i, _):
-        fields, mobilities = [], []
+        mobilities = []
         for half in (0, 1):
-            total, mass = 0.0, 0.0
-            for parity in (0, 1):
-                x = 4 * i + 2 * half + parity
-                sides = around_fine(v1, x, fine_low(parity, 0, width))
-                total = total + diagonal0[x] * (relax(scaled0[x], share0[:, x], sides) - v0[x + 1, MID, :])
-                mass = mass + (m0[x + 1, MID, :] + m1[x + 1, MID, :])
-            fields.append(0.5 * (total + swap_lanes(total, 1)))
+            x = 4 * i + 2 * half
+            mass = (m0[x + 1, MID, :] + m1[x + 1, MID, :]) + (m0[x + 2, MID, :] + m1[x + 2, MID, :])
             mobilities.append(0.125 * (mass + swap_lanes(mass, 1)))
-        cscaled0[i] = jnp.where(even, fields[0], fields[1])
-        cscaled1[i] = jnp.where(even, fields[1], fields[0])
         cm0[i + 1, MID, :] = jnp.where(even, mobilities[0], mobilities[1])
         cm1[i + 1, MID, :] = jnp.where(even, mobilities[1], mobilities[0])
         return 0
@@ -452,48 +475,108 @@
     lax.fori_loop(0, planes // 4, restrict, 0, unroll=2)
 
     def coarse_weights(i, _):
-        for colour, mine, other, share, scaled in ((0, cm0, cm1, cshare0, cscaled0), (1, cm1, cm0, cshare1, cscaled1)):
+        for colour, mine, other, share, factor in ((0, cm0, cm1, cshare0, cinverse0), (1, cm1, cm0, cshare1, cinverse1)):
             u = mine[i + 1, MID, :]
             sides = walls(around_coarse(other, i, coarse_low(colour, width)), lane < 2, lane >= width - 2)
             shares, inverse, diagonal = weights(mean_any, u, sides, sides[1] == 0)
             for a in range(6):
                 share[a, i] = shares[a]
-            scaled[i] = scaled[i] * inverse
+            factor[i] = inverse
             if colour == 0:
                 cdiagonal0[i] = diagonal
-        e0[i + 1, MID, :] = cscaled0[i]
         return 0
 
     lax.fori_loop(0, planes // 4, coarse_weights, 0, unroll=True)
-    for copy in copies[5 : KEPT - 2]:
+    for copy in copies[3:]:
+        copy.start()
+
+    pick = picked(width)
+    for i in range(planes // 4):
+        rest[...] = cm0[i + 1, MID, :] + cm1[i + 1, MID, :]
+        pair = pair_sum(rest)
+        pair = 0.125 * (pair + swap_lanes(pair, 2))
+        packed[i : i + 1, :] = jnp.sum(jnp.where(pick, pair, 0.0), axis=0, keepdims=True)
+    for copy in copies:
+        copy.wait()
+
+
+def down_kernel(
+    columns,
+    share0, share1, inverse0, inverse1, diagonal0,
+    cshare0, cshare1, cinverse0, cinverse1, cdiagonal0, coarsest,
+    own, near, far,
+    *refs,
+):
+    kept, packed = refs[:7], refs[7]
+    scaled0, scaled1, cscaled0, cscaled1, v0, v1, e0, e1, rest, message, done = refs[8:]
+    planes, width = share0.shape[1], share0.shape[3]
+    coarse = planes // 4
+    held = (scaled0, scaled1, cscaled0, cscaled1, v1.at[1 : planes + 1, MID, :], e1.at[1 : coarse + 1, MID, :], message)
+    copies = [pltpu.make_async_copy(ref, hbm, done.at[k]) for k, (ref, hbm) in enumerate(zip(held, kept))]
+    for ref in (v0, v1, e0, e1):
+        clear_edges(ref)
+    near_at, far_at = neighbour_rows(columns)
+    places = ((own, 2 * ROWS, ROWS), (near, 2 * ROWS, near_at), (far, 0, far_at))
+    arrays = (
+        (0, scaled_store(scaled0, inverse0)),
+        (ROWS, scaled_store(scaled1, inverse1)),
+        (2 * ROWS, padded_store(v1)),
+    )
+    unfold_slabs(places, arrays, planes)
+    for copy in copies[:2]:
+        copy.start()
+
+    for _ in range(SWEEPS):
+        fine_pass(0, v0, v1, share0, scaled0)
+        fine_pass(1, v1, v0, share1, scaled1)
+    copies[4].start()
+
+    part = slice(*INNER)
+    even = coarse_low(0, width, INNER)
+
+    def restrict(i, _):
+        fields = []
+        for half in (0, 1):
+            total = 0.0
+            for parity in (0, 1):
+                x = 4 * i + 2 * half + parity
+                sides = around_fine(v1, x, fine_low(parity, 0, width, INNER), INNER)
+                updated = relax(scaled0[x, part, :], share0[:, x, part, :], sides)
+                total = total + diagonal0[x, part, :] * (updated - v0[x + 1, shifted(INNER, 0), :])
+            fields.append(0.5 * (total + swap_lanes(total, 1)))
+        first = jnp.where(even, fields[0], fields[1]) * cinverse0[i, part, :]
+        cscaled0[i, part, :] = first
+        e0[i + 1, shifted(INNER, 0), :] = first
+        cscaled1[i, part, :] = jnp.where(even, fields[1], fields[0]) * cinverse1[i, part, :]
+        return 0
+
+    lax.fori_loop(0, coarse, restrict, 0, unroll=2)
+    for copy in copies[2:4]:
         copy.start()
 
     for sweep in range(SWEEPS):
         if sweep:
-            coarse_pass(0, e0, e1, cshare0, cscaled0)
-        coarse_pass(1, e1, e0, cshare1, cscaled1)
-    copies[KEPT - 1].start()
-
-    here = slice(ROWS, 2 * ROWS)
-    part = lanes((ROWS, width)) % 4
-    row = lax.broadcasted_iota(jnp.int32, (ROWS, width), 0)
-    pick = jnp.logical_and(row % 2 == 0, part == row // 2)
+            coarse_pass(0, e0, e1, cshare0, cscaled0, INNER)
+        coarse_pass(1, e1, e0, cshare1, cscaled1, INNER)
+    copies[5].start()
+
     first = lanes((ROWS, width)) % 2 == 0
     for i in range(coarse):
-        message[i] = jnp.where(first, e1[i + 1, 2 * ROWS : 3 * ROWS, :], cscaled0[i, here, :])
-    copies[KEPT].start()
-    low = coarse_low(0, width)
+        message[i, 0:ROWS, :] = jnp.where(first, e1[i + 1, 2 * ROWS : 3 * ROWS, :], cscaled0[i, ROWS : 2 * ROWS, :])
+        message[i, ROWS : 2 * ROWS, :] = cscaled1[i, ROWS : 2 * ROWS, :]
+    copies[6].start()
+
+    pick = picked(width)
+    low = coarse_low(0, width, OWN)
+    part = slice(*OWN)
     for i in range(coarse):
-        sides = around_coarse(e1, i, low)
-        rest[...] = cdiagonal0[i] * (relax(cscaled0[i], cshare0[:, i], sides) - e0[i + 1, MID, :])
-        pair = rest[ROWS : 2 * ROWS, :] + rest[ROWS + 1 : 2 * ROWS + 1, :]
+        sides = around_coarse(e1, i, low, OWN)
+        updated = relax(cscaled0[i, part, :], cshare0[:, i, part, :], sides)
+        rest[part, :] = cdiagonal0[i, part, :] * (updated - e0[i + 1, shifted(OWN, 0), :])
+        pair = pair_sum(rest)
         pair = 0.5 * (pair + swap_lanes(pair, 2))
         packed[0, i : i + 1, :] = jnp.sum(jnp.where(pick, pair, 0.0), axis=0, keepdims=True)
-        rest[...] = cm0[i + 1, MID, :] + cm1[i + 1, MID, :]
-        pair = rest[ROWS : 2 * ROWS, :] + rest[ROWS + 1 : 2 * ROWS + 1, :]
-        pair = 0.125 * (pair + swap_lanes(pair, 2))
-        at = planes // 4 + i
-        packed[0, at : at + 1, :] = jnp.sum(jnp.where(pick, pair, 0.0), axis=0, keepdims=True)
+    packed[0, coarse : 2 * coarse, :] = coarsest[...]
     tile = packed[0]
     for device in range(1, packed.shape[0]):
         packed[device] = tile
@@ -509,9 +592,9 @@
     kept, out = refs[: KEPT + 2], refs[KEPT + 2]
     state, work = refs[KEPT + 3 : 2 * KEPT + 1], refs[2 * KEPT + 1 :]
     share0, share1, scaled0, scaled1, diagonal0, cshare0, cshare1, cscaled0, cscaled1 = state
-    v0, v1, e0, e1, before, after, bshare, coarsest, spread, done = work
+    v0, v1, e0, e1, near, far, bshare, coarsest, spread, done = work
     planes, width = share0.shape[1], share0.shape[3]
-    held = list(state) + [v1.at[1 : planes + 1, MID, :], e1.at[1 : planes // 4 + 1, MID, :], before, after]
+    held = list(state) + [v1.at[1 : planes + 1, MID, :], e1.at[1 : planes // 4 + 1, MID, :], near, far]
     copies = [pltpu.make_async_copy(hbm, ref, done.at[k]) for k, (ref, hbm) in enumerate(zip(held, kept))]
     for copy in copies[5 : KEPT - 2] + copies[KEPT - 1 :] + copies[:5] + copies[KEPT - 2 : KEPT - 1]:
         copy.start()
@@ -525,9 +608,9 @@
     part = lane % 4
     sources, mobilities = [], []
     for w in range(-REACH, REACH + 1):
-        near = slab + w
-        inside = jnp.logical_and(near >= 0, near < count)
-        device = device_of(jnp.clip(near, 0, count - 1), columns)
+        other = slab + w
+        inside = jnp.logical_and(other >= 0, other < count)
+        device = device_of(jnp.clip(other, 0, count - 1), columns)
         keep = jnp.where(inside, 1.0, 0.0)
         for at, into in ((0, sources), (rows, mobilities)):
             tile = gathered[device, at : at + rows, :] * keep
@@ -577,50 +660,54 @@
 
     for copy in copies[5 : KEPT - 2] + copies[KEPT - 1 :]:
         copy.wait()
+    near_at, far_at = neighbour_rows(columns)
     first = lanes((ROWS, width)) % 2 == 0
     for i in range(rows):
         half = coarsest[pl.ds(i, WIN // 2, stride=rows), :]
         spread[pl.ds(0, WIN // 2, stride=2), :] = half
         spread[pl.ds(1, WIN // 2, stride=2), :] = half
         e1[i + 1, 2 * ROWS : 3 * ROWS, :] = e1[i + 1, 2 * ROWS : 3 * ROWS, :] + spread[ROWS : 2 * ROWS, :]
-        for at, ref in ((0, before), (2 * ROWS, after)):
-            mixed = ref[i]
+        for at, ref in ((near_at, near), (far_at, far)):
+            mixed = ref[i, 0:ROWS, :]
             other = swap_lanes(mixed, 1)
-            e1[i + 1, ROWS + at : 2 * ROWS + at, :] = jnp.where(first, mixed, other) + spread[at : at + ROWS, :]
-            cscaled0[i, at : at + ROWS, :] = jnp.where(first, other, mixed)
+            e1[i + 1, pl.ds(at + ROWS, ROWS), :] = jnp.where(first, mixed, other) + spread[pl.ds(at, ROWS), :]
+            cscaled0[i, pl.ds(at, ROWS), :] = jnp.where(first, other, mixed)
+            cscaled1[i, pl.ds(at, ROWS), :] = ref[i, ROWS : 2 * ROWS, :]
 
     for _ in range(SWEEPS):
         coarse_pass(0, e0, e1, cshare0, cscaled0)
         coarse_pass(1, e1, e0, cshare1, cscaled1)
 
-    even = coarse_low(0, width)
+    even = coarse_low(0, width, INNER)
 
     for copy in copies[:5] + copies[KEPT - 2 : KEPT - 1]:
         copy.wait()
 
+    here = shifted(INNER, 0)
+
     def correct(i, _):
-        a, b = e0[i + 1, MID, :], e1[i + 1, MID, :]
+        a, b = e0[i + 1, here, :], e1[i + 1, here, :]
         for half, add in ((0, jnp.where(even, a, b)), (1, jnp.where(even, b, a))):
             for parity in (0, 1):
                 x = 4 * i + 2 * half + parity
-                v1[x + 1, MID, :] = v1[x + 1, MID, :] + add
+                v1[x + 1, here, :] = v1[x + 1, here, :] + add
         return 0
 
     lax.fori_loop(0, rows, correct, 0)
 
     for _ in range(SWEEPS):
-        fine_pass(0, v0, v1, share0, scaled0)
-        fine_pass(1, v1, v0, share1, scaled1)
-
-    here = slice(2 * ROWS, 3 * ROWS)
+        fine_pass(0, v0, v1, share0, scaled0, INNER)
+        fine_pass(1, v1, v0, share1, scaled1, INNER)
+
+    here, part = shifted(OWN, 0), slice(*OWN)
 
     def fold(i, _):
         rest = []
         for parity in range(4):
             x = 4 * i + parity
-            sides = around_fine(v1, x, fine_low(parity % 2, 0, width))
-            full = diagonal0[x] * (relax(scaled0[x], share0[:, x], sides) - v0[x + 1, MID, :])
-            rest.append(full[ROWS : 2 * ROWS])
+            sides = around_fine(v1, x, fine_low(parity % 2, 0, width, OWN), OWN)
+            updated = relax(scaled0[x, part, :], share0[:, x, part, :], sides)
+            rest.append(diagonal0[x, part, :] * (updated - v0[x + 1, here, :]))
         for a, tiles in (
             (0, [v0[4 * i + b + 1, here, :] for b in range(4)]),
             (1, [v1[4 * i + b + 1, here, :] for b in range(4)]),
@@ -641,8 +728,8 @@
     f32 = jnp.float32
     order = place_of(across, columns)
     path = sorted(range(count), key=lambda device: order[device])
-    up = [(path[k], path[k + 1]) for k in range(count - 1)]
-    down = [(b, a) for a, b in up]
+    near = [pair for k in range(0, count, 2) for pair in ((path[k], path[k + 1]), (path[k + 1], path[k]))]
+    far = [pair for k in range(1, count - 1, 2) for pair in ((path[k], path[k + 1]), (path[k + 1], path[k]))]
     axes = ("gx", "yz")
     params = pltpu.CompilerParams(vmem_limit_bytes=20 * 1024 * 1024)
 
@@ -667,45 +754,69 @@
         name="pack",
     )(*(pltpu.with_memory_space_constraint(x, pltpu.HBM) for x in (right_side, phase, pressure_guess)))
     own = lax.all_to_all(bricks, axes, 0, 0)
-    before = lax.ppermute(own, axes, up)
-    after = lax.ppermute(own, axes, down)
+    mobility, fields = own[:, : 2 * ROWS], own[:, 2 * ROWS :]
+    mobility_far = lax.ppermute(mobility, axes, far)
+    own_near = lax.ppermute(own, axes, near)
+    fields_far = lax.ppermute(fields, axes, far)
 
     coarse = planes // 4
-    fine = [vmem(6, planes, WIN, width)] * 2 + [vmem(planes, WIN, width)] * 3
-    half = [vmem(6, coarse, WIN, width)] * 2 + [vmem(coarse, WIN, width)] * 2
-    kept = fine + half + [struct(planes, WIN, width), struct(coarse, WIN, width)]
+    share, cshare = (6, planes, WIN, width), (6, coarse, WIN, width)
+    plane, cplane = (planes, WIN, width), (coarse, WIN, width)
     padded = [vmem(planes + 2, WIN + 2 * ROWS, width)] * 2
     cpadded = [vmem(coarse + 2, WIN + 2 * ROWS, width)] * 2
-    *state, message, packed = pl.pallas_call(
-        down_kernel,
-        out_shape=[pltpu.HBM(x.shape, x.dtype) for x in kept + [struct(coarse, ROWS, width)]] + [struct(count, 2 * coarse, width)],
-        out_specs=[pl.BlockSpec(memory_space=pltpu.HBM)] * (len(kept) + 1) + [pl.BlockSpec(memory_space=pltpu.VMEM)],
-        scratch_shapes=fine + half + padded * 2 + cpadded * 2 + [
-            vmem(coarse, WIN, width),
+
+    def hbm(*shapes):
+        return [pltpu.HBM(dims, f32) for dims in shapes], [pl.BlockSpec(memory_space=pltpu.HBM)] * len(shapes)
+
+    def near_core(*shapes):
+        return [struct(*dims) for dims in shapes], [pl.BlockSpec(memory_space=pltpu.VMEM)] * len(shapes)
+
+    first = near_core(share, share, plane, plane, plane, cshare, cshare, cplane, cplane, cplane, (coarse, width))
+    second = hbm(share, share, plane, cshare, cshare)
+    *made, share0, share1, diagonal0, cshare0, cshare1 = pl.pallas_call(
+        functools.partial(weights_kernel, columns),
+        out_shape=first[0] + second[0],
+        out_specs=first[1] + second[1],
+        scratch_shapes=padded + cpadded + [vmem(WIN, width), pltpu.SemaphoreType.DMA((5,))],
+        compiler_params=params,
+        cost_estimate=pl.CostEstimate(flops=20_000_000_000, bytes_accessed=100_000_000, transcendentals=0),
+        name="weights",
+    )(own, own_near, mobility_far)
+
+    first = hbm(plane, plane, cplane, cplane, plane, cplane, (coarse, 2 * ROWS, width))
+    second = near_core((count, 2 * coarse, width))
+    scaled0, scaled1, cscaled0, cscaled1, field1, cfield1, message, packed = pl.pallas_call(
+        functools.partial(down_kernel, columns),
+        out_shape=first[0] + second[0],
+        out_specs=first[1] + second[1],
+        scratch_shapes=[vmem(*plane)] * 2 + [vmem(*cplane)] * 2 + padded + cpadded + [
             vmem(WIN, width),
-            vmem(coarse, ROWS, width),
-            pltpu.SemaphoreType.DMA((len(kept) + 1,)),
+            vmem(coarse, 2 * ROWS, width),
+            pltpu.SemaphoreType.DMA((7,)),
         ],
         compiler_params=params,
         name="down",
-    )(own, before, after)
+    )(*made, own, own_near, fields_far)
+    state = (share0, share1, scaled0, scaled1, diagonal0, cshare0, cshare1, cscaled0, cscaled1, field1, cfield1)
+    fine = [vmem(*share)] * 2 + [vmem(*plane)] * 3
+    half = [vmem(*cshare)] * 2 + [vmem(*cplane)] * 2
     gathered = lax.all_to_all(packed, axes, 0, 0)
-    e_before = lax.ppermute(message, axes, up)
-    e_after = lax.ppermute(message, axes, down)
+    message_far = lax.ppermute(message, axes, far)
+    message_near = lax.ppermute(message, axes, near)
 
     cycle = pl.pallas_call(
         functools.partial(up_kernel, columns),
         out_shape=struct(count, 3 * ROWS, 128),
-        in_specs=[pl.BlockSpec(memory_space=pltpu.VMEM)] + [pl.BlockSpec(memory_space=pltpu.HBM)] * (len(kept) + 2),
-        scratch_shapes=fine + half + padded + cpadded + [vmem(coarse, ROWS, width)] * 2 + [
+        in_specs=[pl.BlockSpec(memory_space=pltpu.VMEM)] + [pl.BlockSpec(memory_space=pltpu.HBM)] * (KEPT + 2),
+        scratch_shapes=fine + half + padded + cpadded + [vmem(coarse, 2 * ROWS, width)] * 2 + [
             vmem(2, 6, 2 * (2 * REACH + 1), coarse, width),
             vmem(WIN // 2 * coarse, width),
             vmem(WIN, width),
-            pltpu.SemaphoreType.DMA((len(kept) + 2,)),
+            pltpu.SemaphoreType.DMA((KEPT + 2,)),
         ],
         compiler_params=params,
         name="up",
-    )(gathered, *(pltpu.with_memory_space_constraint(x, pltpu.HBM) for x in (*state, e_before, e_after)))
+    )(gathered, *(pltpu.with_memory_space_constraint(x, pltpu.HBM) for x in (*state, message_near, message_far)))
     back = lax.all_to_all(cycle, axes, 0, 0)
     return pl.pallas_call(
         functools.partial(unpack_kernel, order),

time: 84.7 us -> 79.2 us (0.935)
  starting transfers between devices: 20.3 us -> 14.5 us
  Pallas kernels: 13.9 us -> 15.9 us
  blocking collectives: 41.5 us -> 40.4 us
    ppermute x4 -> x5, starting transfers between devices: 8.68 us -> 5.3 us  [the longest x1 3.19 us: local_slabs(): message_near = lax.ppermute(message, axes, near)]
    all_to_all x1, starting transfers between devices: 11.6 us -> 9.16 us  [local_slabs(): gathered = lax.all_to_all(packed, axes, 0, 0)]
    pallas_call x1 -> x2, Pallas kernels: 6.9 us -> 9.17 us  [the longest x1 4.72 us: local_slabs(): pl.pallas_call(functools.partial(weights_kernel, columns), out_shape=firs...]
    all_to_all x1, blocking collectives: 16.5 us -> 15.4 us  [local_slabs(): back = lax.all_to_all(cycle, axes, 0, 0)]
    ppermute x4 -> x5, waiting for transfers between devices: 2.69 us -> 1.69 us  [the longest x1 1.11 us: local_slabs(): message_near = lax.ppermute(message, axes, near)]
  transfers between devices with their start and end apart: 5 -> 6, of which waited for: 3 -> 3; matrix products, arithmetic and copies ran while one was open for 0% -> 0% of each run, Pallas kernels for 0% -> 6%
where the time goes in v4:
time: 79.2 us; the launch traced here: 78.9 us
  blocking collectives  40.4 us (51%)
  Pallas kernels  15.9 us (20%)
  starting transfers between devices  14.5 us (18%)
  waiting for transfers between devices  7.31 us (9%)
    all_to_all x1, blocking collectives, local_slabs(): own = lax.all_to_all(bricks, axes, 0, 0)  25 us
    all_to_all x1, blocking collectives, local_slabs(): back = lax.all_to_all(cycle, axes, 0, 0)  15.4 us
    all_to_all x1, starting transfers between devices, local_slabs(): gathered = lax.all_to_all(packed, axes, 0, 0)  9.16 us
    all_to_all x1, waiting for transfers between devices, local_slabs(): gathered = lax.all_to_all(packed, axes, 0, 0)  5.62 us
    pallas_call x1, Pallas kernels, local_slabs(): pl.pallas_call(functools.partial(weights_kernel, columns), out_shape=firs...  4.72 us
    pallas_call x1, Pallas kernels, local_slabs(): pl.pallas_call(functools.partial(down_kernel, columns), out_shape=first[0...  4.45 us
    pallas_call x1, Pallas kernels, local_slabs(): pl.pallas_call(functools.partial(up_kernel, columns), out_shape=struct(co...  4.38 us
    ppermute x1, starting transfers between devices, local_slabs(): message_near = lax.ppermute(message, axes, near)  3.19 us
  transfers between devices with their start and end apart: 6, of which 3 were waited for; matrix products, arithmetic and copies ran while one was open for 0% of the time, Pallas kernels for 6%

profile of v4, /device:TPU:0, one launch (start us, length us, event | category | flops | bytes accessed | tf_op | source)
XLA Modules:
  0.0 78.9 jit_solution(13761867632193715582)
XLA Ops:
  0.6 1.4 %pack.1 = f32[32,40,128]{2,1,0:T(8,128)S(1)} custom-call(f32[4,32,512]{2,1,0:T(8,128)} %source_hbm.1, s32[4,32,512]{2,1,0:T(8,128)} %phase_hbm.1, f32[4,32,512]{2,1,0:T(8,128)} %guess_hbm.1), custom_call_target="tpu_custom_call" | custom-call | tf_op jit(solution)/shard_map/pack/pallas_call | solution.py:742
  2.1 25.0 %all_to_all.15.own = f32[32,40,128]{2,1,0:T(8,128)S(1)} all-to-all(f32[32,40,128]{2,1,0:T(8,128)S(1)} %pack.1), channel_id=1, replica_groups=mesh['gx'=8,'yz'=4] {'gx','yz'}, dimensions={0} | all-to-all | bytes 1310720 | tf_op jit(solution)/shard_map/all_to_all | solution.py:756
  27.1 0.1 collective-permute-start
  27.2 0.7 collective-permute-start.1
  27.9 0.7 collective-permute-start.2
  28.6 0.0 collective-permute-done.1.far
  28.6 0.6 collective-permute-done.near
  29.2 4.7 %weights.1 = (f32[6,32,24,128]{3,2,1,0:T(8,128)S(1)}, f32[6,32,24,128]{3,2,1,0:T(8,128)S(1)}, f32[32,24,128]{2,1,0:T(8,128)S(1)}, f32[32,24,128]{2,1,0:T(8,128)S...) custom-call(f32[32,40,128]{2,1,0:T(8,128)S(1)} %all_to_all.15.own, ...), custom_call_target="tpu_custom_call" | custom-call | flops 20000000000 | bytes 100000000 | tf_op jit(solution)/shard_map/weights/pallas_call | solution.py:776
  33.9 0.0 collective-permute-done.2.far
  33.9 4.4 %down.1 = (f32[32,24,128]{2,1,0:T(8,128)}, f32[32,24,128]{2,1,0:T(8,128)}, f32[8,24,128]{2,1,0:T(8,128)}, f32[8,24,128]{2,1,0:T(8,128)}, f32[32,24,128]{2,1,0:T(...) custom-call(f32[6,32,24,128]{3,2,1,0:T(8,128)S(1)} %get-tuple-element.26.share0, ...), custom_call_target="tpu_custom_call" | custom-call | tf_op jit(solution)/shard_map/down/pallas_call | solution.py:788
  38.4 9.2 %all-to-all-start.1 = ((f32[32,16,128]{2,1,0:T(8,128)}), f32[32,16,128]{2,1,0:T(8,128)S(1)}, u32[]{:S(2)}, u32[]{:S(2)}) async-start(f32[32,16,128]{2,1,0:T(8,128)} %get-tuple-element.37), calls=%async_computation.1 | async-start | bytes 524288 | tf_op jit(solution)/shard_map/all_to_all | solution.py:803
  47.6 0.7 collective-permute-start.4
  48.2 3.2 %collective-permute-start.3 = (f32[8,16,128]{2,1,0:T(8,128)}, f32[8,16,128]{2,1,0:T(8,128)S(1)}, u32[]{:S(2)}, u32[]{:S(2)}) collective-permute-start(f32[8,16,128]{2,1,0:T(8,128)} %get-tuple-element.49), channel_id=1, source_target_pairs={{0,1},{1,0},{2,3},{3,2},{7,6},{6,7},{5,4},{4,5},{12,13},{13,12},{1... | collective-permute-start | bytes 196616 | tf_op jit(solution)/shard_map/ppermute | solution.py:805
  51.4 0.0 collective-permute-done.4.refs_12_
  51.4 0.0 copy-start
  51.4 1.1 %collective-permute-done.3.refs_11_ = f32[8,16,128]{2,1,0:T(8,128)S(1)} collective-permute-done((f32[8,16,128]{2,1,0:T(8,128)}, f32[8,16,128]{2,1,0:T(8,128)S(1)}, u32[]{:S(2)}, u32[]{:S(2)}) %collective-permute-start.3) | collective-permute-done | bytes 65568 | tf_op jit(solution)/shard_map/ppermute | solution.py:805
  52.5 0.0 copy-start.1
  52.5 5.6 %all-to-all-done.1.gathered = f32[32,16,128]{2,1,0:T(8,128)S(1)} async-done(((f32[32,16,128]{2,1,0:T(8,128)}), f32[32,16,128]{2,1,0:T(8,128)S(1)}, u32[]{:S(2)}, u32[]{:S(2)}) %all-to-all-start.1) | async-done | bytes 262176 | tf_op jit(solution)/shard_map/all_to_all | solution.py:803
  58.2 0.0 copy-done
  58.2 0.0 copy-done.1
  58.2 4.4 %up.1 = f32[32,24,128]{2,1,0:T(8,128)S(1)} custom-call(f32[32,16,128]{2,1,0:T(8,128)S(1)} %all-to-all-done.1.gathered, f32[6,32,24,128]{3,2,1,0:T(8,128)} %get-tuple-element.38.refs_0_, f32[6,32,24,128]{3,2,1,0:T(8,128)} %get-tuple-element.39.refs_1_, f32[32,24,128]{2,1,0:T(8,128)} %get-tuple-element.40.refs_2_, f32[32,24,128]{2,1,0:T(8,128)} %get-tuple-element.41.refs_3_, ...), custom_call_target="tpu_custom_call" | custom-call | tf_op jit(solution)/shard_map/up/pallas_call | solution.py:807
  62.6 15.4 %all_to_all.16.in_ref = f32[32,24,128]{2,1,0:T(8,128)S(1)} all-to-all(f32[32,24,128]{2,1,0:T(8,128)S(1)} %up.1), channel_id=1, replica_groups=mesh['gx'=8,'yz'=4] {'gx','yz'}, dimensions={0} | all-to-all | bytes 786432 | tf_op jit(solution)/shard_map/all_to_all | solution.py:820
  77.9 0.9 %unpack.1 = (f32[4,32,512]{2,1,0:T(8,128)}, f32[4,32,512]{2,1,0:T(8,128)}) custom-call(f32[32,24,128]{2,1,0:T(8,128)S(1)} %all_to_all.16.in_ref), custom_call_target="tpu_custom_call" | custom-call | tf_op jit(solution)/shard_map/unpack/pallas_call | solution.py:821
  (2 shorter events, 0.0 us)
Async XLA Ops:
  27.1 2.1 %collective-permute-start = (f32[32,40,128]{2,1,0:T(8,128)S(1)}, f32[32,40,128]{2,1,0:T(8,128)S(1)}, u32[]{:S(2)}, u32[]{:S(2)}) collective-permute-start(f32[32,40,128]{2,1,0:T(8,128)S(1)} %all_to_all.15.own), channel_id=1, source_target_pairs={{0,1},{1,0},{2,3},{3,2},{7,6},{6,7},{5,4},{4,5},{12,13},{13,12},{1... | collective-permute-start | bytes 1966088 | tf_op jit(solution)/shard_map/ppermute | solution.py:759
  27.2 1.4 %collective-permute-start.1 = (f32[32,16,128]{2,1,0:T(8,128)S(1)}, f32[32,16,128]{2,1,0:T(8,128)S(1)}, u32[]{:S(2)}, u32[]{:S(2)}) collective-permute-start(f32[32,16,128]{2,1,0:T(8,128)S(1)} %slice.8), channel_id=1, source_target_pairs={{1,2},{2,1},{3,7},{7,3},{6,5},{5,6},{4,12},{12,4},{13,14},{14,13},... | collective-permute-start | bytes 786440 | tf_op jit(solution)/shard_map/ppermute | solution.py:758
  27.9 6.0 %collective-permute-start.2 = (f32[32,24,128]{2,1,0:T(8,128)S(1)}, f32[32,24,128]{2,1,0:T(8,128)S(1)}, u32[]{:S(2)}, u32[]{:S(2)}) collective-permute-start(f32[32,24,128]{2,1,0:T(8,128)S(1)} %slice.9), channel_id=1, source_target_pairs={{1,2},{2,1},{3,7},{7,3},{6,5},{5,6},{4,12},{12,4},{13,14},{14,13},... | collective-permute-start | bytes 1179656 | tf_op jit(solution)/shard_map/ppermute | solution.py:760
  38.4 19.8 %all-to-all-start.1 = ((f32[32,16,128]{2,1,0:T(8,128)}), f32[32,16,128]{2,1,0:T(8,128)S(1)}, u32[]{:S(2)}, u32[]{:S(2)}) async-start(f32[32,16,128]{2,1,0:T(8,128)} %get-tuple-element.37), calls=%async_computation.1 | async-start | bytes 524288 | tf_op jit(solution)/shard_map/all_to_all | solution.py:803
  47.6 3.9 %collective-permute-start.4 = (f32[8,16,128]{2,1,0:T(8,128)}, f32[8,16,128]{2,1,0:T(8,128)S(1)}, u32[]{:S(2)}, u32[]{:S(2)}) collective-permute-start(f32[8,16,128]{2,1,0:T(8,128)} %get-tuple-element.49), channel_id=1, source_target_pairs={{1,2},{2,1},{3,7},{7,3},{6,5},{5,6},{4,12},{12,4},{13,14},{14,13},... | collective-permute-start | bytes 196616 | tf_op jit(solution)/shard_map/ppermute | solution.py:804
  48.2 4.3 %collective-permute-start.3 = (f32[8,16,128]{2,1,0:T(8,128)}, f32[8,16,128]{2,1,0:T(8,128)S(1)}, u32[]{:S(2)}, u32[]{:S(2)}) collective-permute-start(f32[8,16,128]{2,1,0:T(8,128)} %get-tuple-element.49), channel_id=1, source_target_pairs={{0,1},{1,0},{2,3},{3,2},{7,6},{6,7},{5,4},{4,5},{12,13},{13,12},{1... | collective-permute-start | bytes 196616 | tf_op jit(solution)/shard_map/ppermute | solution.py:805
  51.4 6.7 %copy-start = (f32[8,16,128]{2,1,0:T(8,128)}, f32[8,16,128]{2,1,0:T(8,128)S(1)}, u32[]{:S(2)}) copy-start(f32[8,16,128]{2,1,0:T(8,128)S(1)} %collective-permute-done.4.refs_12_) | copy-start | bytes 196612
  52.5 5.6 %copy-start.1 = (f32[8,16,128]{2,1,0:T(8,128)}, f32[8,16,128]{2,1,0:T(8,128)S(1)}, u32[]{:S(2)}) copy-start(f32[8,16,128]{2,1,0:T(8,128)S(1)} %collective-permute-done.3.refs_11_) | copy-start | bytes 196612

commit v5 on v4

--- a/solution.py
+++ b/solution.py
@@ -256,7 +256,6 @@
         ref[...] = turned[a].T.reshape(ref.shape)
 
 
-KEPT = 11
 ALL = (0, WIN)
 INNER = (ROWS // 2, WIN - ROWS // 2)
 OWN = (ROWS, 2 * ROWS)
@@ -267,18 +266,15 @@
     return slice(ROWS + rows[0] + by, ROWS + rows[1] + by)
 
 
-def clear_edges(ref):
-    planes, _, width = ref.shape
-    zero = jnp.zeros((ref.shape[1], width), jnp.float32)
-    ref[0] = zero
-    ref[planes - 1] = zero
-
-    def one(x, _):
-        ref[x, 0:ROWS, :] = zero[:ROWS]
-        ref[x, ROWS + WIN :, :] = zero[:ROWS]
-        return 0
-
-    lax.fori_loop(1, planes - 1, one, 0)
+def within(ref, rows):
+    start = (WIN - ref.shape[-2]) // 2
+    return slice(rows[0] - start, rows[1] - start)
+
+
+def clear_outside(ref):
+    planes, rows, width = ref.shape
+    for plane in (0, planes - 1):
+        ref[plane] = jnp.zeros((rows, width), jnp.float32)
 
 
 def around_fine(ref, x, low, rows=ALL):
@@ -361,13 +357,13 @@
 
 def fine_pass(colour, target, other, share, scaled, rows=ALL):
     planes, width = share.shape[1], share.shape[3]
-    part = slice(*rows)
+    part, held = slice(*rows), within(share, rows)
 
     def two(i, _):
         for parity in (0, 1):
             x = 2 * i + parity
             sides = around_fine(other, x, fine_low(parity, colour, width, rows), rows)
-            target[x + 1, shifted(rows, 0), :] = relax(scaled[x, part, :], share[:, x, part, :], sides)
+            target[x + 1, shifted(rows, 0), :] = relax(scaled[x, part, :], share[:, x, held, :], sides)
         return 0
 
     lax.fori_loop(0, planes // 2, two, 0, unroll=True)
@@ -426,38 +422,63 @@
     return jnp.logical_and(row % 2 == 0, lanes((ROWS, width)) % 4 == row // 2)
 
 
+def fine_weights(m0, m1, outputs, diagonal0, rows):
+    planes, width = m0.shape[0] - 2, m0.shape[2]
+    lane = lanes((rows[1] - rows[0], width))
+
+    def fine(i, _):
+        for parity in (0, 1):
+            x = 2 * i + parity
+            for colour, mine, other in ((0, m0, m1), (1, m1, m0)):
+                low = fine_low(parity, colour, width, rows)
+                u = mine[x + 1, shifted(rows, 0), :]
+                sides = walls(around_fine(other, x, low, rows), lane == 0, lane == width - 1)
+                top = jnp.logical_and(jnp.logical_not(low), sides[5] == 0)
+                shares, inverse, diagonal = weights(mean_fine, u, sides, top)
+                share, factor = outputs[colour]
+                for a in range(6):
+                    share[a, x] = shares[a]
+                if factor is not None:
+                    factor[x] = inverse
+                if colour == 0:
+                    diagonal0[x] = diagonal
+        return 0
+
+    lax.fori_loop(0, planes // 2, fine, 0, unroll=2)
+
+
+def coarse_weights(cm0, cm1, outputs, diagonal0):
+    planes, width = cm0.shape[0] - 2, cm0.shape[2]
+    lane = lanes((WIN, width))
+
+    def coarse(i, _):
+        for colour, mine, other in ((0, cm0, cm1), (1, cm1, cm0)):
+            u = mine[i + 1, MID, :]
+            sides = walls(around_coarse(other, i, coarse_low(colour, width)), lane < 2, lane >= width - 2)
+            shares, inverse, diagonal = weights(mean_any, u, sides, sides[1] == 0)
+            share, factor = outputs[colour]
+            for a in range(6):
+                share[a, i] = shares[a]
+            if factor is not None:
+                factor[i] = inverse
+            if colour == 0 and diagonal0 is not None:
+                diagonal0[i] = diagonal
+        return 0
+
+    lax.fori_loop(0, planes, coarse, 0, unroll=True)
+
+
 def weights_kernel(columns, own, near, far, *refs):
     share0, share1, inverse0, inverse1, diagonal0, cshare0, cshare1, cinverse0, cinverse1, cdiagonal0, packed = refs[:11]
-    kept, (m0, m1, cm0, cm1, rest, done) = refs[11:16], refs[16:]
-    held = (share0, share1, diagonal0, cshare0, cshare1)
-    copies = [pltpu.make_async_copy(ref, hbm, done.at[k]) for k, (ref, hbm) in enumerate(zip(held, kept))]
+    kept, (m0, m1, cm0, cm1, rest, done) = refs[11:15], refs[15:]
+    copies = [pltpu.make_async_copy(ref, hbm, done.at[k]) for k, (ref, hbm) in enumerate(zip((m0, m1, cm0, cm1), kept))]
     planes, width = share0.shape[1], share0.shape[3]
     for ref in (m0, m1, cm0, cm1):
-        clear_edges(ref)
+        clear_outside(ref)
     near_at, far_at = neighbour_rows(columns)
     places = ((own, 0, ROWS), (near, 0, near_at), (far, 0, far_at))
     unfold_slabs(places, ((0, padded_store(m0)), (ROWS, padded_store(m1))), planes)
-
-    lane = lanes((WIN, width))
-
-    def fine_weights(i, _):
-        for parity in (0, 1):
-            x = 2 * i + parity
-            for colour, mine, other, share, factor in ((0, m0, m1, share0, inverse0), (1, m1, m0, share1, inverse1)):
-                low = fine_low(parity, colour, width)
-                u = mine[x + 1, MID, :]
-                sides = walls(around_fine(other, x, low), lane == 0, lane == width - 1)
-                top = jnp.logical_and(jnp.logical_not(low), sides[5] == 0)
-                shares, inverse, diagonal = weights(mean_fine, u, sides, top)
-                for a in range(6):
-                    share[a, x] = shares[a]
-                factor[x] = inverse
-                if colour == 0:
-                    diagonal0[x] = diagonal
-        return 0
-
-    lax.fori_loop(0, planes // 2, fine_weights, 0, unroll=2)
-    for copy in copies[:3]:
+    for copy in copies[:2]:
         copy.start()
 
     even = coarse_low(0, width)
@@ -473,22 +494,10 @@
         return 0
 
     lax.fori_loop(0, planes // 4, restrict, 0, unroll=2)
-
-    def coarse_weights(i, _):
-        for colour, mine, other, share, factor in ((0, cm0, cm1, cshare0, cinverse0), (1, cm1, cm0, cshare1, cinverse1)):
-            u = mine[i + 1, MID, :]
-            sides = walls(around_coarse(other, i, coarse_low(colour, width)), lane < 2, lane >= width - 2)
-            shares, inverse, diagonal = weights(mean_any, u, sides, sides[1] == 0)
-            for a in range(6):
-                share[a, i] = shares[a]
-            factor[i] = inverse
-            if colour == 0:
-                cdiagonal0[i] = diagonal
-        return 0
-
-    lax.fori_loop(0, planes // 4, coarse_weights, 0, unroll=True)
-    for copy in copies[3:]:
+    for copy in copies[2:]:
         copy.start()
+    fine_weights(m0, m1, ((share0, inverse0), (share1, inverse1)), diagonal0, ALL)
+    coarse_weights(cm0, cm1, ((cshare0, cinverse0), (cshare1, cinverse1)), cdiagonal0)
 
     pick = picked(width)
     for i in range(planes // 4):
@@ -497,6 +506,26 @@
         pair = 0.125 * (pair + swap_lanes(pair, 2))
         packed[i : i + 1, :] = jnp.sum(jnp.where(pick, pair, 0.0), axis=0, keepdims=True)
     for copy in copies:
+        copy.wait()
+
+
+def again_kernel(*refs):
+    kept, made = refs[:4], refs[5:10]
+    share0, share1 = made[:2]
+    diagonal0, cshare0, cshare1, m0, m1, cm0, cm1, done = refs[10:]
+    copies = [pltpu.make_async_copy(hbm, ref, done.at[k]) for k, (ref, hbm) in enumerate(zip((m0, m1, cm0, cm1), kept))]
+    held = (diagonal0, cshare0, cshare1)
+    copies += [pltpu.make_async_copy(ref, hbm, done.at[4 + k]) for k, (ref, hbm) in enumerate(zip(held, made[2:]))]
+    for copy in copies[:4]:
+        copy.start()
+    for copy in copies[:4]:
+        copy.wait()
+    coarse_weights(cm0, cm1, ((cshare0, None), (cshare1, None)), None)
+    for copy in copies[5:]:
+        copy.start()
+    fine_weights(m0, m1, ((share0, None), (share1, None)), diagonal0, INNER)
+    copies[4].start()
+    for copy in copies[4:]:
         copy.wait()
 
 
@@ -514,7 +543,7 @@
     held = (scaled0, scaled1, cscaled0, cscaled1, v1.at[1 : planes + 1, MID, :], e1.at[1 : coarse + 1, MID, :], message)
     copies = [pltpu.make_async_copy(ref, hbm, done.at[k]) for k, (ref, hbm) in enumerate(zip(held, kept))]
     for ref in (v0, v1, e0, e1):
-        clear_edges(ref)
+        clear_outside(ref)
     near_at, far_at = neighbour_rows(columns)
     places = ((own, 2 * ROWS, ROWS), (near, 2 * ROWS, near_at), (far, 0, far_at))
     arrays = (
@@ -586,22 +615,22 @@
 
 def up_kernel(
     columns,
-    gathered,
+    gathered, share0, share1,
     *refs,
 ):
-    kept, out = refs[: KEPT + 2], refs[KEPT + 2]
-    state, work = refs[KEPT + 3 : 2 * KEPT + 1], refs[2 * KEPT + 1 :]
-    share0, share1, scaled0, scaled1, diagonal0, cshare0, cshare1, cscaled0, cscaled1 = state
+    kept, out, held, work = refs[:11], refs[11], refs[12:19], refs[19:]
+    cscaled0, cscaled1, cshare0, cshare1, scaled0, scaled1, diagonal0 = held
     v0, v1, e0, e1, near, far, bshare, coarsest, spread, done = work
     planes, width = share0.shape[1], share0.shape[3]
-    held = list(state) + [v1.at[1 : planes + 1, MID, :], e1.at[1 : planes // 4 + 1, MID, :], near, far]
-    copies = [pltpu.make_async_copy(hbm, ref, done.at[k]) for k, (ref, hbm) in enumerate(zip(held, kept))]
-    for copy in copies[5 : KEPT - 2] + copies[KEPT - 1 :] + copies[:5] + copies[KEPT - 2 : KEPT - 1]:
-        copy.start()
     count = gathered.shape[0]
     rows = planes // 4
+    held = (near, far, e1.at[1 : rows + 1, MID, :]) + held[:4] + (v1.at[1 : planes + 1, MID, :],) + held[4:]
+    copies = [pltpu.make_async_copy(hbm, ref, done.at[k]) for k, (ref, hbm) in enumerate(zip(held, kept))]
+    early, late = copies[:7], copies[7:]
+    for copy in early + late:
+        copy.start()
     for ref in (v0, v1, e0, e1):
-        clear_edges(ref)
+        clear_outside(ref)
 
     slab = slab_index(columns)
     lane = lanes((rows, width))
@@ -658,7 +687,7 @@
         coarsest[2 * k * rows : (2 * k + 1) * rows, :] = jnp.where(low[0], a, b)
         coarsest[(2 * k + 1) * rows : (2 * k + 2) * rows, :] = jnp.where(low[0], b, a)
 
-    for copy in copies[5 : KEPT - 2] + copies[KEPT - 1 :]:
+    for copy in early:
         copy.wait()
     near_at, far_at = neighbour_rows(columns)
     first = lanes((ROWS, width)) % 2 == 0
@@ -680,7 +709,7 @@
 
     even = coarse_low(0, width, INNER)
 
-    for copy in copies[:5] + copies[KEPT - 2 : KEPT - 1]:
+    for copy in late:
         copy.wait()
 
     here = shifted(INNER, 0)
@@ -699,15 +728,15 @@
         fine_pass(0, v0, v1, share0, scaled0, INNER)
         fine_pass(1, v1, v0, share1, scaled1, INNER)
 
-    here, part = shifted(OWN, 0), slice(*OWN)
+    here, part, own = shifted(OWN, 0), slice(*OWN), within(share0, OWN)
 
     def fold(i, _):
         rest = []
         for parity in range(4):
             x = 4 * i + parity
             sides = around_fine(v1, x, fine_low(parity % 2, 0, width, OWN), OWN)
-            updated = relax(scaled0[x, part, :], share0[:, x, part, :], sides)
-            rest.append(diagonal0[x, part, :] * (updated - v0[x + 1, here, :]))
+            updated = relax(scaled0[x, part, :], share0[:, x, own, :], sides)
+            rest.append(diagonal0[x, own, :] * (updated - v0[x + 1, here, :]))
         for a, tiles in (
             (0, [v0[4 * i + b + 1, here, :] for b in range(4)]),
             (1, [v1[4 * i + b + 1, here, :] for b in range(4)]),
@@ -731,6 +760,7 @@
     near = [pair for k in range(0, count, 2) for pair in ((path[k], path[k + 1]), (path[k + 1], path[k]))]
     far = [pair for k in range(1, count - 1, 2) for pair in ((path[k], path[k + 1]), (path[k + 1], path[k]))]
     axes = ("gx", "yz")
+    cost = pl.CostEstimate(flops=20_000_000_000, bytes_accessed=100_000_000, transcendentals=0)
     params = pltpu.CompilerParams(vmem_limit_bytes=20 * 1024 * 1024)
 
     def struct(*dims):
@@ -772,14 +802,14 @@
         return [struct(*dims) for dims in shapes], [pl.BlockSpec(memory_space=pltpu.VMEM)] * len(shapes)
 
     first = near_core(share, share, plane, plane, plane, cshare, cshare, cplane, cplane, cplane, (coarse, width))
-    second = hbm(share, share, plane, cshare, cshare)
-    *made, share0, share1, diagonal0, cshare0, cshare1 = pl.pallas_call(
+    second = hbm((planes + 2, WIN + 2 * ROWS, width), (planes + 2, WIN + 2 * ROWS, width), (coarse + 2, WIN + 2 * ROWS, width), (coarse + 2, WIN + 2 * ROWS, width))
+    *made, m0, m1, cm0, cm1 = pl.pallas_call(
         functools.partial(weights_kernel, columns),
         out_shape=first[0] + second[0],
         out_specs=first[1] + second[1],
-        scratch_shapes=padded + cpadded + [vmem(WIN, width), pltpu.SemaphoreType.DMA((5,))],
+        scratch_shapes=padded + cpadded + [vmem(WIN, width), pltpu.SemaphoreType.DMA((4,))],
         compiler_params=params,
-        cost_estimate=pl.CostEstimate(flops=20_000_000_000, bytes_accessed=100_000_000, transcendentals=0),
+        cost_estimate=cost,
         name="weights",
     )(own, own_near, mobility_far)
 
@@ -797,26 +827,42 @@
         compiler_params=params,
         name="down",
     )(*made, own, own_near, fields_far)
-    state = (share0, share1, scaled0, scaled1, diagonal0, cshare0, cshare1, cscaled0, cscaled1, field1, cfield1)
-    fine = [vmem(*share)] * 2 + [vmem(*plane)] * 3
-    half = [vmem(*cshare)] * 2 + [vmem(*cplane)] * 2
     gathered = lax.all_to_all(packed, axes, 0, 0)
     message_far = lax.ppermute(message, axes, far)
     message_near = lax.ppermute(message, axes, near)
 
+    def in_hbm(*arrays):
+        return [pltpu.with_memory_space_constraint(x, pltpu.HBM) for x in arrays]
+
+    middle = (planes, INNER[1] - INNER[0], width)
+    made = [(6,) + middle, (6,) + middle, middle, cshare, cshare]
+    first, second = near_core(*made[:2]), hbm(*made[2:])
+    share0, share1, diagonal0, cshare0, cshare1 = pl.pallas_call(
+        again_kernel,
+        out_shape=first[0] + second[0],
+        in_specs=[pl.BlockSpec(memory_space=pltpu.HBM)] * 5,
+        out_specs=first[1] + second[1],
+        scratch_shapes=[vmem(*dims) for dims in made[2:]] + padded + cpadded + [pltpu.SemaphoreType.DMA((7,))],
+        compiler_params=params,
+        cost_estimate=pl.CostEstimate(flops=1_000_000_000, bytes_accessed=1_000_000, transcendentals=0),
+        name="again",
+    )(*in_hbm(m0, m1, cm0, cm1, message))
+
+    kept = (message_near, message_far, cfield1, cscaled0, cscaled1, cshare0, cshare1, field1)
+    kept += (scaled0, scaled1, diagonal0)
     cycle = pl.pallas_call(
         functools.partial(up_kernel, columns),
         out_shape=struct(count, 3 * ROWS, 128),
-        in_specs=[pl.BlockSpec(memory_space=pltpu.VMEM)] + [pl.BlockSpec(memory_space=pltpu.HBM)] * (KEPT + 2),
-        scratch_shapes=fine + half + padded + cpadded + [vmem(coarse, 2 * ROWS, width)] * 2 + [
+        in_specs=[pl.BlockSpec(memory_space=pltpu.VMEM)] * 3 + [pl.BlockSpec(memory_space=pltpu.HBM)] * len(kept),
+        scratch_shapes=[vmem(*dims) for dims in (cplane, cplane, cshare, cshare, plane, plane, middle)] + padded + cpadded + [vmem(coarse, 2 * ROWS, width)] * 2 + [
             vmem(2, 6, 2 * (2 * REACH + 1), coarse, width),
             vmem(WIN // 2 * coarse, width),
             vmem(WIN, width),
-            pltpu.SemaphoreType.DMA((KEPT + 2,)),
+            pltpu.SemaphoreType.DMA((len(kept),)),
         ],
         compiler_params=params,
         name="up",
-    )(gathered, *(pltpu.with_memory_space_constraint(x, pltpu.HBM) for x in (*state, message_near, message_far)))
+    )(gathered, share0, share1, *in_hbm(*kept))
     back = lax.all_to_all(cycle, axes, 0, 0)
     return pl.pallas_call(
         functools.partial(unpack_kernel, order),

time: 79.2 us -> 77.8 us (0.982)
  waiting for transfers between devices: 7.31 us -> 3.63 us
  starting transfers between devices: 14.5 us -> 16.2 us
    pallas_call x0 -> x1, Pallas kernels: none -> 3.64 us  [local_slabs(): pl.pallas_call(again_kernel, out_shape=first[0] + second[0], in_specs=[pl...]
    all_to_all x1, waiting for transfers between devices: 5.62 us -> 3.05 us  [local_slabs(): gathered = lax.all_to_all(packed, axes, 0, 0)]
    pallas_call x1, Pallas kernels: 4.72 us -> 2.38 us  [local_slabs(): pl.pallas_call(functools.partial(weights_kernel, columns), out_shape=firs...]
    all_to_all x1, starting transfers between devices: 9.16 us -> 10.9 us  [local_slabs(): gathered = lax.all_to_all(packed, axes, 0, 0)]
    ppermute x1, waiting for transfers between devices: 1.11 us -> 0.01 us  [local_slabs(): message_near = lax.ppermute(message, axes, near)]
  transfers between devices with their start and end apart: 6 -> 6, of which waited for: 3 -> 2; matrix products, arithmetic and copies ran while one was open for 0% -> 0% of each run, Pallas kernels for 6% -> 8%
where the time goes in v5:
time: 77.8 us; the launch traced here: 77.4 us
  blocking collectives  40.4 us (52%)
  Pallas kernels  16.3 us (21%)
  starting transfers between devices  16.2 us (21%)
  waiting for transfers between devices  3.63 us (5%)
    all_to_all x1, blocking collectives, local_slabs(): own = lax.all_to_all(bricks, axes, 0, 0)  25 us
    all_to_all x1, blocking collectives, local_slabs(): back = lax.all_to_all(cycle, axes, 0, 0)  15.4 us
    all_to_all x1, starting transfers between devices, local_slabs(): gathered = lax.all_to_all(packed, axes, 0, 0)  10.9 us
    pallas_call x1, Pallas kernels, local_slabs(): pl.pallas_call(functools.partial(down_kernel, columns), out_shape=first[0...  4 us
    pallas_call x1, Pallas kernels, local_slabs(): pl.pallas_call(functools.partial(up_kernel, columns), out_shape=struct(co...  3.88 us
    pallas_call x1, Pallas kernels, local_slabs(): pl.pallas_call(again_kernel, out_shape=first[0] + second[0], in_specs=[pl...  3.64 us
    ppermute x1, starting transfers between devices, local_slabs(): message_near = lax.ppermute(message, axes, near)  3.19 us
    all_to_all x1, waiting for transfers between devices, local_slabs(): gathered = lax.all_to_all(packed, axes, 0, 0)  3.05 us
  transfers between devices with their start and end apart: 6, of which 2 were waited for; matrix products, arithmetic and copies ran while one was open for 0% of the time, Pallas kernels for 8%

profile of v5, /device:TPU:0, one launch (start us, length us, event | category | flops | bytes accessed | tf_op | source)
XLA Modules:
  0.0 77.4 jit_solution(15407591101190027809)
XLA Ops:
  0.6 1.4 %pack.1 = f32[32,40,128]{2,1,0:T(8,128)S(1)} custom-call(f32[4,32,512]{2,1,0:T(8,128)} %source_hbm.1, s32[4,32,512]{2,1,0:T(8,128)} %phase_hbm.1, f32[4,32,512]{2,1,0:T(8,128)} %guess_hbm.1), custom_call_target="tpu_custom_call" | custom-call | tf_op jit(solution)/shard_map/pack/pallas_call | solution.py:772
  2.1 25.0 %all_to_all.15.own = f32[32,40,128]{2,1,0:T(8,128)S(1)} all-to-all(f32[32,40,128]{2,1,0:T(8,128)S(1)} %pack.1), channel_id=1, replica_groups=mesh['gx'=8,'yz'=4] {'gx','yz'}, dimensions={0} | all-to-all | bytes 1310720 | tf_op jit(solution)/shard_map/all_to_all | solution.py:786
  27.1 0.1 collective-permute-start
  27.2 0.7 collective-permute-start.1
  27.9 0.7 collective-permute-start.2
  28.6 0.0 collective-permute-done.1.far
  28.6 0.6 collective-permute-done.near
  29.2 2.4 %weights.1 = (f32[6,32,24,128]{3,2,1,0:T(8,128)S(1)}, f32[6,32,24,128]{3,2,1,0:T(8,128)S(1)}, f32[32,24,128]{2,1,0:T(8,128)S(1)}, f32[32,24,128]{2,1,0:T(8,128)S...) custom-call(f32[32,40,128]{2,1,0:T(8,128)S(1)} %all_to_all.15.own, ...), custom_call_target="tpu_custom_call" | custom-call | flops 20000000000 | bytes 100000000 | tf_op jit(solution)/shard_map/weights/pallas_call | solution.py:806
  31.6 0.0 collective-permute-done.2.far
  31.6 4.0 %down.1 = (f32[32,24,128]{2,1,0:T(8,128)}, f32[32,24,128]{2,1,0:T(8,128)}, f32[8,24,128]{2,1,0:T(8,128)}, f32[8,24,128]{2,1,0:T(8,128)}, f32[32,24,128]{2,1,0:T(...) custom-call(f32[6,32,24,128]{3,2,1,0:T(8,128)S(1)} %get-tuple-element.30.share0, ...), custom_call_target="tpu_custom_call" | custom-call | tf_op jit(solution)/shard_map/down/pallas_call | solution.py:818
  35.6 10.9 %all-to-all-start.1 = ((f32[32,16,128]{2,1,0:T(8,128)}), f32[32,16,128]{2,1,0:T(8,128)S(1)}, u32[]{:S(2)}, u32[]{:S(2)}) async-start(f32[32,16,128]{2,1,0:T(8,128)} %get-tuple-element.41), calls=%async_computation.1 | async-start | bytes 524288 | tf_op jit(solution)/shard_map/all_to_all | solution.py:830
  46.6 0.7 collective-permute-start.4
  47.2 3.2 %collective-permute-start.3 = (f32[8,16,128]{2,1,0:T(8,128)}, f32[8,16,128]{2,1,0:T(8,128)S(1)}, u32[]{:S(2)}, u32[]{:S(2)}) collective-permute-start(f32[8,16,128]{2,1,0:T(8,128)} %get-tuple-element.46.refs_4_), channel_id=1, source_target_pairs={{0,1},{1,0},{2,3},{3,2},{7,6},{6,7},{5,4},{4,5},{12,13},{13,12},{1... | collective-permute-start | bytes 196616 | tf_op jit(solution)/shard_map/ppermute | solution.py:832
  50.4 3.6 %again.1 = (f32[6,32,16,128]{3,2,1,0:T(8,128)S(1)}, f32[6,32,16,128]{3,2,1,0:T(8,128)S(1)}, f32[32,16,128]{2,1,0:T(8,128)}, f32[6,8,24,128]{3,2,1,0:T(8,128)}, f32[6,8,24,128]{3,2,1,0:T(8,128)}) custom-call(f32[34,40,128]{2,1,0:T(8,128)} %get-tuple-element.42.refs_0_, f32[34,40,128]{2,1,0:T(8,128)} %get-tuple-element.43.refs_1_, ...), custom_call_target="tpu_custom_call" | custom-call | flops 1000000000 | bytes 1000000 | tf_op jit(solution)/shard_map/again/pallas_call | solution.py:840
  54.1 0.0 collective-permute-done.4.refs_1_
  54.1 0.0 copy-start
  54.1 0.0 collective-permute-done.3.refs_0_
  54.1 0.0 copy-start.1
  54.1 3.0 %all-to-all-done.1.gathered = f32[32,16,128]{2,1,0:T(8,128)S(1)} async-done(((f32[32,16,128]{2,1,0:T(8,128)}), f32[32,16,128]{2,1,0:T(8,128)S(1)}, u32[]{:S(2)}, u32[]{:S(2)}) %all-to-all-start.1) | async-done | bytes 262176 | tf_op jit(solution)/shard_map/all_to_all | solution.py:830
  57.2 0.0 copy-done
  57.2 0.0 copy-done.1
  57.2 3.9 %up.1 = f32[32,24,128]{2,1,0:T(8,128)S(1)} custom-call(f32[32,16,128]{2,1,0:T(8,128)S(1)} %all-to-all-done.1.gathered, f32[6,32,16,128]{3,2,1,0:T(8,128)S(1)} %get-tuple-element.47.share0, f32[6,32,16,128]{3,2,1,0:T(8,128)S(1)} %get-tuple-element.48.share1, f32[8,16,128]{2,1,0:T(8,128)} %copy-done.1, f32[8,16,128]{2,1,0:T(8,128)} %copy-done, ...), custom_call_target="tpu_custom_call" | custom-call | tf_op jit(solution)/shard_map/up/pallas_call | solution.py:853
  61.1 15.4 %all_to_all.16.in_ref = f32[32,24,128]{2,1,0:T(8,128)S(1)} all-to-all(f32[32,24,128]{2,1,0:T(8,128)S(1)} %up.1), channel_id=1, replica_groups=mesh['gx'=8,'yz'=4] {'gx','yz'}, dimensions={0} | all-to-all | bytes 786432 | tf_op jit(solution)/shard_map/all_to_all | solution.py:866
  76.4 0.9 %unpack.1 = (f32[4,32,512]{2,1,0:T(8,128)}, f32[4,32,512]{2,1,0:T(8,128)}) custom-call(f32[32,24,128]{2,1,0:T(8,128)S(1)} %all_to_all.16.in_ref), custom_call_target="tpu_custom_call" | custom-call | tf_op jit(solution)/shard_map/unpack/pallas_call | solution.py:867
  (2 shorter events, 0.0 us)
Async XLA Ops:
  27.1 2.1 %collective-permute-start = (f32[32,40,128]{2,1,0:T(8,128)S(1)}, f32[32,40,128]{2,1,0:T(8,128)S(1)}, u32[]{:S(2)}, u32[]{:S(2)}) collective-permute-start(f32[32,40,128]{2,1,0:T(8,128)S(1)} %all_to_all.15.own), channel_id=1, source_target_pairs={{0,1},{1,0},{2,3},{3,2},{7,6},{6,7},{5,4},{4,5},{12,13},{13,12},{1... | collective-permute-start | bytes 1966088 | tf_op jit(solution)/shard_map/ppermute | solution.py:789
  27.2 1.4 %collective-permute-start.1 = (f32[32,16,128]{2,1,0:T(8,128)S(1)}, f32[32,16,128]{2,1,0:T(8,128)S(1)}, u32[]{:S(2)}, u32[]{:S(2)}) collective-permute-start(f32[32,16,128]{2,1,0:T(8,128)S(1)} %slice.8), channel_id=1, source_target_pairs={{1,2},{2,1},{3,7},{7,3},{6,5},{5,6},{4,12},{12,4},{13,14},{14,13},... | collective-permute-start | bytes 786440 | tf_op jit(solution)/shard_map/ppermute | solution.py:788
  27.9 3.7 %collective-permute-start.2 = (f32[32,24,128]{2,1,0:T(8,128)S(1)}, f32[32,24,128]{2,1,0:T(8,128)S(1)}, u32[]{:S(2)}, u32[]{:S(2)}) collective-permute-start(f32[32,24,128]{2,1,0:T(8,128)S(1)} %slice.9), channel_id=1, source_target_pairs={{1,2},{2,1},{3,7},{7,3},{6,5},{5,6},{4,12},{12,4},{13,14},{14,13},... | collective-permute-start | bytes 1179656 | tf_op jit(solution)/shard_map/ppermute | solution.py:790
  35.6 21.6 %all-to-all-start.1 = ((f32[32,16,128]{2,1,0:T(8,128)}), f32[32,16,128]{2,1,0:T(8,128)S(1)}, u32[]{:S(2)}, u32[]{:S(2)}) async-start(f32[32,16,128]{2,1,0:T(8,128)} %get-tuple-element.41), calls=%async_computation.1 | async-start | bytes 524288 | tf_op jit(solution)/shard_map/all_to_all | solution.py:830
  46.6 7.5 %collective-permute-start.4 = (f32[8,16,128]{2,1,0:T(8,128)}, f32[8,16,128]{2,1,0:T(8,128)S(1)}, u32[]{:S(2)}, u32[]{:S(2)}) collective-permute-start(f32[8,16,128]{2,1,0:T(8,128)} %get-tuple-element.46.refs_4_), channel_id=1, source_target_pairs={{1,2},{2,1},{3,7},{7,3},{6,5},{5,6},{4,12},{12,4},{13,14},{14,13},... | collective-permute-start | bytes 196616 | tf_op jit(solution)/shard_map/ppermute | solution.py:831
  47.2 6.9 %collective-permute-start.3 = (f32[8,16,128]{2,1,0:T(8,128)}, f32[8,16,128]{2,1,0:T(8,128)S(1)}, u32[]{:S(2)}, u32[]{:S(2)}) collective-permute-start(f32[8,16,128]{2,1,0:T(8,128)} %get-tuple-element.46.refs_4_), channel_id=1, source_target_pairs={{0,1},{1,0},{2,3},{3,2},{7,6},{6,7},{5,4},{4,5},{12,13},{13,12},{1... | collective-permute-start | bytes 196616 | tf_op jit(solution)/shard_map/ppermute | solution.py:832
  54.1 3.1 %copy-start = (f32[8,16,128]{2,1,0:T(8,128)}, f32[8,16,128]{2,1,0:T(8,128)S(1)}, u32[]{:S(2)}) copy-start(f32[8,16,128]{2,1,0:T(8,128)S(1)} %collective-permute-done.4.refs_1_) | copy-start | bytes 196612
  54.1 3.1 %copy-start.1 = (f32[8,16,128]{2,1,0:T(8,128)}, f32[8,16,128]{2,1,0:T(8,128)S(1)}, u32[]{:S(2)}) copy-start(f32[8,16,128]{2,1,0:T(8,128)S(1)} %collective-permute-done.3.refs_0_) | copy-start | bytes 196612

commit v6 on v4

--- a/solution.py
+++ b/solution.py
@@ -256,57 +256,28 @@
         ref[...] = turned[a].T.reshape(ref.shape)
 
 
-KEPT = 11
-ALL = (0, WIN)
+FACE_ROWS = (1, WIN - 1)
 INNER = (ROWS // 2, WIN - ROWS // 2)
 OWN = (ROWS, 2 * ROWS)
-MID = slice(ROWS, ROWS + WIN)
-
-
-def shifted(rows, by):
-    return slice(ROWS + rows[0] + by, ROWS + rows[1] + by)
-
-
-def clear_edges(ref):
-    planes, _, width = ref.shape
-    zero = jnp.zeros((ref.shape[1], width), jnp.float32)
-    ref[0] = zero
-    ref[planes - 1] = zero
-
-    def one(x, _):
-        ref[x, 0:ROWS, :] = zero[:ROWS]
-        ref[x, ROWS + WIN :, :] = zero[:ROWS]
-        return 0
-
-    lax.fori_loop(1, planes - 1, one, 0)
-
-
-def around_fine(ref, x, low, rows=ALL):
-    here = shifted(rows, 0)
-    centre = ref[x + 1, here, :]
-    width = centre.shape[1]
-    return (
-        ref[x, here, :],
-        ref[x + 2, here, :],
-        pltpu.roll(centre, 1, 1),
-        pltpu.roll(centre, width - 1, 1),
-        centre,
-        jnp.where(low, ref[x + 1, shifted(rows, -1), :], ref[x + 1, shifted(rows, 1), :]),
-    )
-
-
-def around_coarse(ref, i, low, rows=ALL):
-    here = shifted(rows, 0)
-    centre = ref[i + 1, here, :]
-    width = centre.shape[1]
-    return (
-        ref[i + 1, shifted(rows, -1), :],
-        ref[i + 1, shifted(rows, 1), :],
-        pltpu.roll(centre, 2, 1),
-        pltpu.roll(centre, width - 2, 1),
-        centre,
-        jnp.where(low, ref[i, here, :], ref[i + 2, here, :]),
-    )
+
+
+def wider(rows, by):
+    return (rows[0] - by, rows[1] + by)
+
+
+def at(ref, rows, by=0):
+    start = (WIN - ref.shape[-2]) // 2
+    return slice(rows[0] - start + by, rows[1] - start + by)
+
+
+def beyond(ref, i, low, rows, *lead):
+    return jnp.where(low, ref[(*lead, i, at(ref, rows, -1))], ref[(*lead, i, at(ref, rows, 1))])
+
+
+def add_up(terms):
+    while len(terms) > 1:
+        terms = [sum(terms[k : k + 2]) for k in range(0, len(terms), 2)]
+    return terms[0]
 
 
 def around_coarsest(planes, k, low):
@@ -349,40 +320,156 @@
     return scaled + ((parts[0] + parts[1]) + (parts[2] + parts[3]) + (parts[4] + parts[5]))
 
 
-def fine_low(x_parity, colour, width, rows=ALL):
-    return (lanes((rows[1] - rows[0], width)) + (x_parity + colour)) % 2 == 0
-
-
-def coarse_low(colour, width, rows=ALL):
+def fine_low(x, colour, width, rows):
+    return (lanes((rows[1] - rows[0], width)) + (x + colour) % 2) % 2 == 0
+
+
+def coarse_low(colour, width, rows):
     shape = (rows[1] - rows[0], width)
     row = lax.broadcasted_iota(jnp.int32, shape, 0) + rows[0]
     return (row + lanes(shape) // 2 + colour) % 2 == 0
 
 
-def fine_pass(colour, target, other, share, scaled, rows=ALL):
-    planes, width = share.shape[1], share.shape[3]
-    part = slice(*rows)
-
-    def two(i, _):
-        for parity in (0, 1):
-            x = 2 * i + parity
-            sides = around_fine(other, x, fine_low(parity, colour, width, rows), rows)
-            target[x + 1, shifted(rows, 0), :] = relax(scaled[x, part, :], share[:, x, part, :], sides)
-        return 0
-
-    lax.fori_loop(0, planes // 2, two, 0, unroll=True)
-
-
-def coarse_pass(colour, target, other, share, scaled, rows=ALL):
-    planes, width = share.shape[1], share.shape[3]
-    part = slice(*rows)
-
-    def one(i, _):
-        sides = around_coarse(other, i, coarse_low(colour, width, rows), rows)
-        target[i + 1, shifted(rows, 0), :] = relax(scaled[i, part, :], share[:, i, part, :], sides)
-        return 0
-
-    lax.fori_loop(0, planes, one, 0, unroll=True)
+def fine_sides(v, x, low, rows):
+    here = at(v, rows)
+    centre = v[x, here, :]
+    width = centre.shape[1]
+    return (
+        v[x - 1, here, :] if x > 0 else None,
+        v[x + 1, here, :] if x + 1 < v.shape[0] else None,
+        pltpu.roll(centre, 1, 1),
+        pltpu.roll(centre, width - 1, 1),
+        centre,
+        beyond(v, x, low, rows),
+    )
+
+
+def fine_flow(colour, face, v, x, rows):
+    planes, width = face.shape[1], face.shape[3]
+    part = at(face, rows)
+    low = fine_low(x, colour, width, rows)
+    if colour == 0:
+        sides = fine_sides(v, x, low, rows)
+        return add_up([face[a, x, part, :] * side for a, side in enumerate(sides) if side is not None])
+
+    def carried(a, plane):
+        values = face[a, plane, part, :]
+        return values if v is None else values * v[plane, at(v, rows), :]
+
+    away = beyond(face, x, low, rows, 5)
+    terms = [
+        pltpu.roll(carried(3, x), 1, 1),
+        pltpu.roll(carried(2, x), width - 1, 1),
+        carried(4, x),
+        away if v is None else away * beyond(v, x, low, rows),
+    ]
+    if x > 0:
+        terms.append(carried(1, x - 1))
+    if x + 1 < planes:
+        terms.append(carried(0, x + 1))
+    return add_up(terms)
+
+
+def coarse_sides(v, i, low, rows):
+    here = at(v, rows)
+    centre = v[i, here, :]
+    width = centre.shape[1]
+    below = v[i - 1, here, :] if i > 0 else jnp.zeros_like(centre)
+    above = v[i + 1, here, :] if i + 1 < v.shape[0] else jnp.zeros_like(centre)
+    return (
+        v[i, at(v, rows, -1), :],
+        v[i, at(v, rows, 1), :],
+        pltpu.roll(centre, 2, 1),
+        pltpu.roll(centre, width - 2, 1),
+        centre,
+        jnp.where(low, below, above),
+    )
+
+
+def coarse_flow(colour, face, v, i, rows):
+    planes, width = face.shape[1], face.shape[3]
+    low = coarse_low(colour, width, rows)
+    if colour == 0:
+        sides = coarse_sides(v, i, low, rows)
+        return add_up([face[a, i, at(face, rows), :] * side for a, side in enumerate(sides)])
+
+    def carried(a, plane, by=0):
+        values = face[a, plane, at(face, rows, by), :]
+        return values if v is None else values * v[plane, at(v, rows, by), :]
+
+    centre = carried(4, i)
+    below = carried(5, i - 1) if i > 0 else jnp.zeros_like(centre)
+    above = carried(5, i + 1) if i + 1 < planes else jnp.zeros_like(centre)
+    return add_up(
+        [
+            carried(1, i, -1),
+            carried(0, i, 1),
+            pltpu.roll(carried(3, i), 2, 1),
+            pltpu.roll(carried(2, i), width - 2, 1),
+            centre,
+            jnp.where(low, below, above),
+        ]
+    )
+
+
+def renew(flow, colour, target, other, face, inverse, scaled, rows):
+    for x in range(face.shape[1]):
+        moved = inverse[x, at(inverse, rows), :] * flow(colour, face, other, x, rows)
+        target[x, at(target, rows), :] = scaled[x, at(scaled, rows), :] + moved
+
+
+def rest_of(flow, v0, v1, face, inverse0, scaled0, x, rows):
+    factor = inverse0[x, at(inverse0, rows), :]
+    updated = scaled0[x, at(scaled0, rows), :] + factor * flow(0, face, v1, x, rows)
+    return (updated - v0[x, at(v0, rows), :]) / factor
+
+
+def one_over(diagonal):
+    return 1.0 / jnp.where(diagonal > 0, diagonal, 1.0)
+
+
+def fine_faces(m0, m1, face, inverse0, inverse1):
+    planes, width = face.shape[1], face.shape[3]
+    rows = FACE_ROWS
+    here = at(face, rows)
+    lane = lanes((rows[1] - rows[0], width))
+    for x in range(planes):
+        low = fine_low(x, 0, width, rows)
+        u = m0[x, here, :]
+        sides = walls(fine_sides(m1, x, low, rows), lane == 0, lane == width - 1)
+        terms = []
+        for a, side in enumerate(sides):
+            value = jnp.zeros_like(u) if side is None else mean_fine(u, side)
+            face[a, x, here, :] = value
+            terms.append(value)
+        top = jnp.logical_and(jnp.logical_not(low), sides[5] == 0)
+        inverse0[x, here, :] = one_over(add_up(terms) + jnp.where(top, 2.0 * u, 0.0))
+    rows = wider(rows, -1)
+    for x in range(planes):
+        low = fine_low(x, 1, width, rows)
+        top = jnp.logical_and(jnp.logical_not(low), m0[x, at(m0, rows, 1), :] == 0)
+        total = fine_flow(1, face, None, x, rows) + jnp.where(top, 2.0 * m1[x, at(m1, rows), :], 0.0)
+        inverse1[x, at(inverse1, rows), :] = one_over(total)
+
+
+def coarse_faces(m0, m1, face, inverse0, inverse1):
+    planes, width = face.shape[1], face.shape[3]
+    rows = FACE_ROWS
+    here = at(face, rows)
+    lane = lanes((rows[1] - rows[0], width))
+    for i in range(planes):
+        u = m0[i, here, :]
+        sides = walls(coarse_sides(m1, i, coarse_low(0, width, rows), rows), lane < 2, lane >= width - 2)
+        terms = []
+        for a, side in enumerate(sides):
+            value = mean_any(u, side)
+            face[a, i, here, :] = value
+            terms.append(value)
+        inverse0[i, here, :] = one_over(add_up(terms) + jnp.where(sides[1] == 0, 2.0 * u, 0.0))
+    rows = wider(rows, -1)
+    for i in range(planes):
+        top = jnp.where(m0[i, at(m0, rows, 1), :] == 0, 2.0 * m1[i, at(m1, rows), :], 0.0)
+        inverse1[i, at(inverse1, rows), :] = one_over(coarse_flow(1, face, None, i, rows) + top)
 
 
 def neighbour_rows(columns):
@@ -402,17 +489,17 @@
     lax.fori_loop(0, planes // 4, unfold, 0, unroll=True)
 
 
-def padded_store(ref):
-    def store(x, at, tile):
-        ref[x + 1, pl.ds(at + ROWS, ROWS), :] = tile
+def plain_store(ref):
+    def store(x, row, tile):
+        ref[x, pl.ds(row, ROWS), :] = tile
 
     return store
 
 
 def scaled_store(ref, factor):
-    def store(x, at, tile):
-        rows = pl.ds(at, ROWS)
-        ref[x, rows, :] = tile * factor[x, rows, :]
+    def store(x, row, tile):
+        part = pl.ds(row, ROWS)
+        ref[x, part, :] = tile * factor[x, part, :]
 
     return store
 
@@ -426,153 +513,92 @@
     return jnp.logical_and(row % 2 == 0, lanes((ROWS, width)) % 4 == row // 2)
 
 
-def weights_kernel(columns, own, near, far, *refs):
-    share0, share1, inverse0, inverse1, diagonal0, cshare0, cshare1, cinverse0, cinverse1, cdiagonal0, packed = refs[:11]
-    kept, (m0, m1, cm0, cm1, rest, done) = refs[11:16], refs[16:]
-    held = (share0, share1, diagonal0, cshare0, cshare1)
-    copies = [pltpu.make_async_copy(ref, hbm, done.at[k]) for k, (ref, hbm) in enumerate(zip(held, kept))]
-    planes, width = share0.shape[1], share0.shape[3]
-    for ref in (m0, m1, cm0, cm1):
-        clear_edges(ref)
+def weights_kernel(
+    columns,
+    own, near, far,
+    face, inverse0, inverse1, cface, cinverse0, cinverse1, coarsest,
+    m0, m1, cm0, cm1, rest,
+):
+    planes, width = face.shape[1], face.shape[3]
     near_at, far_at = neighbour_rows(columns)
     places = ((own, 0, ROWS), (near, 0, near_at), (far, 0, far_at))
-    unfold_slabs(places, ((0, padded_store(m0)), (ROWS, padded_store(m1))), planes)
-
-    lane = lanes((WIN, width))
-
-    def fine_weights(i, _):
-        for parity in (0, 1):
-            x = 2 * i + parity
-            for colour, mine, other, share, factor in ((0, m0, m1, share0, inverse0), (1, m1, m0, share1, inverse1)):
-                low = fine_low(parity, colour, width)
-                u = mine[x + 1, MID, :]
-                sides = walls(around_fine(other, x, low), lane == 0, lane == width - 1)
-                top = jnp.logical_and(jnp.logical_not(low), sides[5] == 0)
-                shares, inverse, diagonal = weights(mean_fine, u, sides, top)
-                for a in range(6):
-                    share[a, x] = shares[a]
-                factor[x] = inverse
-                if colour == 0:
-                    diagonal0[x] = diagonal
-        return 0
-
-    lax.fori_loop(0, planes // 2, fine_weights, 0, unroll=2)
-    for copy in copies[:3]:
-        copy.start()
-
-    even = coarse_low(0, width)
-
-    def restrict(i, _):
+    unfold_slabs(places, ((0, plain_store(m0)), (ROWS, plain_store(m1))), planes)
+    fine_faces(m0, m1, face, inverse0, inverse1)
+    even = coarse_low(0, width, (0, WIN))
+    for i in range(planes // 4):
         mobilities = []
-        for half in (0, 1):
-            x = 4 * i + 2 * half
-            mass = (m0[x + 1, MID, :] + m1[x + 1, MID, :]) + (m0[x + 2, MID, :] + m1[x + 2, MID, :])
+        for x in (4 * i, 4 * i + 2):
+            mass = (m0[x] + m1[x]) + (m0[x + 1] + m1[x + 1])
             mobilities.append(0.125 * (mass + swap_lanes(mass, 1)))
-        cm0[i + 1, MID, :] = jnp.where(even, mobilities[0], mobilities[1])
-        cm1[i + 1, MID, :] = jnp.where(even, mobilities[1], mobilities[0])
-        return 0
-
-    lax.fori_loop(0, planes // 4, restrict, 0, unroll=2)
-
-    def coarse_weights(i, _):
-        for colour, mine, other, share, factor in ((0, cm0, cm1, cshare0, cinverse0), (1, cm1, cm0, cshare1, cinverse1)):
-            u = mine[i + 1, MID, :]
-            sides = walls(around_coarse(other, i, coarse_low(colour, width)), lane < 2, lane >= width - 2)
-            shares, inverse, diagonal = weights(mean_any, u, sides, sides[1] == 0)
-            for a in range(6):
-                share[a, i] = shares[a]
-            factor[i] = inverse
-            if colour == 0:
-                cdiagonal0[i] = diagonal
-        return 0
-
-    lax.fori_loop(0, planes // 4, coarse_weights, 0, unroll=True)
-    for copy in copies[3:]:
-        copy.start()
-
+        cm0[i] = jnp.where(even, mobilities[0], mobilities[1])
+        cm1[i] = jnp.where(even, mobilities[1], mobilities[0])
+    coarse_faces(cm0, cm1, cface, cinverse0, cinverse1)
     pick = picked(width)
     for i in range(planes // 4):
-        rest[...] = cm0[i + 1, MID, :] + cm1[i + 1, MID, :]
+        rest[...] = cm0[i] + cm1[i]
         pair = pair_sum(rest)
         pair = 0.125 * (pair + swap_lanes(pair, 2))
-        packed[i : i + 1, :] = jnp.sum(jnp.where(pick, pair, 0.0), axis=0, keepdims=True)
-    for copy in copies:
-        copy.wait()
+        coarsest[i : i + 1, :] = jnp.sum(jnp.where(pick, pair, 0.0), axis=0, keepdims=True)
 
 
 def down_kernel(
     columns,
-    share0, share1, inverse0, inverse1, diagonal0,
-    cshare0, cshare1, cinverse0, cinverse1, cdiagonal0, coarsest,
+    face, inverse0, inverse1, cface, cinverse0, cinverse1, coarsest,
     own, near, far,
     *refs,
 ):
-    kept, packed = refs[:7], refs[7]
-    scaled0, scaled1, cscaled0, cscaled1, v0, v1, e0, e1, rest, message, done = refs[8:]
-    planes, width = share0.shape[1], share0.shape[3]
+    state, cstate, message_hbm, packed_hbm = refs[:4]
+    scaled0, scaled1, cscaled0, cscaled1, v0, v1, e0, e1, rest, message, packed, done = refs[4:]
+    planes, width = face.shape[1], face.shape[3]
     coarse = planes // 4
-    held = (scaled0, scaled1, cscaled0, cscaled1, v1.at[1 : planes + 1, MID, :], e1.at[1 : coarse + 1, MID, :], message)
-    copies = [pltpu.make_async_copy(ref, hbm, done.at[k]) for k, (ref, hbm) in enumerate(zip(held, kept))]
-    for ref in (v0, v1, e0, e1):
-        clear_edges(ref)
+    middle = slice(*INNER)
+    held = [(face.at[:, :, middle, :], state.at[0:6])]
+    held += [(ref.at[:, middle, :], state.at[6 + k]) for k, ref in enumerate((inverse0, inverse1, scaled0, scaled1, v1))]
+    held += [(cface, cstate.at[0:6])]
+    held += [(ref, cstate.at[6 + k]) for k, ref in enumerate((cinverse0, cinverse1, cscaled0, cscaled1, e1))]
+    held += [(message, message_hbm)]
+    copies = [pltpu.make_async_copy(ref, out, done.at[k]) for k, (ref, out) in enumerate(held)]
+    for copy in copies[:3] + copies[6:9]:
+        copy.start()
     near_at, far_at = neighbour_rows(columns)
     places = ((own, 2 * ROWS, ROWS), (near, 2 * ROWS, near_at), (far, 0, far_at))
     arrays = (
         (0, scaled_store(scaled0, inverse0)),
         (ROWS, scaled_store(scaled1, inverse1)),
-        (2 * ROWS, padded_store(v1)),
+        (2 * ROWS, plain_store(v1)),
     )
     unfold_slabs(places, arrays, planes)
-    for copy in copies[:2]:
+    for copy in copies[3:5]:
         copy.start()
 
-    for _ in range(SWEEPS):
-        fine_pass(0, v0, v1, share0, scaled0)
-        fine_pass(1, v1, v0, share1, scaled1)
-    copies[4].start()
-
-    part = slice(*INNER)
+    renew(fine_flow, 0, v0, v1, face, inverse0, scaled0, (1, WIN - 1))
+    renew(fine_flow, 1, v1, v0, face, inverse1, scaled1, (2, WIN - 2))
+    renew(fine_flow, 0, v0, v1, face, inverse0, scaled0, (3, WIN - 3))
+    renew(fine_flow, 1, v1, v0, face, inverse1, scaled1, (3, WIN - 3))
+    copies[5].start()
+
     even = coarse_low(0, width, INNER)
-
-    def restrict(i, _):
+    for i in range(coarse):
         fields = []
-        for half in (0, 1):
-            total = 0.0
-            for parity in (0, 1):
-                x = 4 * i + 2 * half + parity
-                sides = around_fine(v1, x, fine_low(parity, 0, width, INNER), INNER)
-                updated = relax(scaled0[x, part, :], share0[:, x, part, :], sides)
-                total = total + diagonal0[x, part, :] * (updated - v0[x + 1, shifted(INNER, 0), :])
+        for x in (4 * i, 4 * i + 2):
+            total = rest_of(fine_flow, v0, v1, face, inverse0, scaled0, x, INNER)
+            total = total + rest_of(fine_flow, v0, v1, face, inverse0, scaled0, x + 1, INNER)
             fields.append(0.5 * (total + swap_lanes(total, 1)))
-        first = jnp.where(even, fields[0], fields[1]) * cinverse0[i, part, :]
-        cscaled0[i, part, :] = first
-        e0[i + 1, shifted(INNER, 0), :] = first
-        cscaled1[i, part, :] = jnp.where(even, fields[1], fields[0]) * cinverse1[i, part, :]
-        return 0
-
-    lax.fori_loop(0, coarse, restrict, 0, unroll=2)
-    for copy in copies[2:4]:
+        first = jnp.where(even, fields[0], fields[1]) * cinverse0[i, middle, :]
+        cscaled0[i, middle, :] = first
+        e0[i, middle, :] = first
+        cscaled1[i, middle, :] = jnp.where(even, fields[1], fields[0]) * cinverse1[i, middle, :]
+    for copy in copies[9:11]:
         copy.start()
 
-    for sweep in range(SWEEPS):
-        if sweep:
-            coarse_pass(0, e0, e1, cshare0, cscaled0, INNER)
-        coarse_pass(1, e1, e0, cshare1, cscaled1, INNER)
-    copies[5].start()
-
-    first = lanes((ROWS, width)) % 2 == 0
+    renew(coarse_flow, 1, e1, e0, cface, cinverse1, cscaled1, wider(INNER, -1))
+    renew(coarse_flow, 0, e0, e1, cface, cinverse0, cscaled0, wider(INNER, -2))
+    renew(coarse_flow, 1, e1, e0, cface, cinverse1, cscaled1, wider(OWN, 1))
+    copies[11].start()
+
+    pick = picked(width)
     for i in range(coarse):
-        message[i, 0:ROWS, :] = jnp.where(first, e1[i + 1, 2 * ROWS : 3 * ROWS, :], cscaled0[i, ROWS : 2 * ROWS, :])
-        message[i, ROWS : 2 * ROWS, :] = cscaled1[i, ROWS : 2 * ROWS, :]
-    copies[6].start()
-
-    pick = picked(width)
-    low = coarse_low(0, width, OWN)
-    part = slice(*OWN)
-    for i in range(coarse):
-        sides = around_coarse(e1, i, low, OWN)
-        updated = relax(cscaled0[i, part, :], cshare0[:, i, part, :], sides)
-        rest[part, :] = cdiagonal0[i, part, :] * (updated - e0[i + 1, shifted(OWN, 0), :])
+        rest[slice(*OWN), :] = rest_of(coarse_flow, e0, e1, cface, cinverse0, cscaled0, i, OWN)
         pair = pair_sum(rest)
         pair = 0.5 * (pair + swap_lanes(pair, 2))
         packed[0, i : i + 1, :] = jnp.sum(jnp.where(pick, pair, 0.0), axis=0, keepdims=True)
@@ -580,28 +606,35 @@
     tile = packed[0]
     for device in range(1, packed.shape[0]):
         packed[device] = tile
+    sent = pltpu.make_async_copy(packed, packed_hbm, done.at[13])
+    sent.start()
+
+    first = lanes((ROWS, width)) % 2 == 0
+    here = slice(*OWN)
+    for i in range(coarse):
+        message[i, 0:ROWS, :] = jnp.where(first, e1[i, here, :], cscaled0[i, here, :])
+        message[i, ROWS : 2 * ROWS, :] = cscaled1[i, here, :]
+    copies[12].start()
     for copy in copies:
         copy.wait()
+    sent.wait()
 
 
 def up_kernel(
     columns,
-    gathered,
-    *refs,
+    gathered, state, cstate_hbm, near_hbm, far_hbm,
+    out,
+    cstate, v0, v1, e0, near, far, bshare, coarsest, spread, done,
 ):
-    kept, out = refs[: KEPT + 2], refs[KEPT + 2]
-    state, work = refs[KEPT + 3 : 2 * KEPT + 1], refs[2 * KEPT + 1 :]
-    share0, share1, scaled0, scaled1, diagonal0, cshare0, cshare1, cscaled0, cscaled1 = state
-    v0, v1, e0, e1, near, far, bshare, coarsest, spread, done = work
-    planes, width = share0.shape[1], share0.shape[3]
-    held = list(state) + [v1.at[1 : planes + 1, MID, :], e1.at[1 : planes // 4 + 1, MID, :], near, far]
-    copies = [pltpu.make_async_copy(hbm, ref, done.at[k]) for k, (ref, hbm) in enumerate(zip(held, kept))]
-    for copy in copies[5 : KEPT - 2] + copies[KEPT - 1 :] + copies[:5] + copies[KEPT - 2 : KEPT - 1]:
-        copy.start()
+    planes, width = state.shape[1], state.shape[3]
     count = gathered.shape[0]
     rows = planes // 4
-    for ref in (v0, v1, e0, e1):
-        clear_edges(ref)
+    face, (inverse0, inverse1, scaled0, scaled1, field1) = state, [state.at[k] for k in range(6, 11)]
+    cface, (cinverse0, cinverse1, cscaled0, cscaled1, e1) = cstate, [cstate.at[k] for k in range(6, 11)]
+    held = ((cstate_hbm, cstate), (near_hbm, near), (far_hbm, far))
+    copies = [pltpu.make_async_copy(hbm, ref, done.at[k]) for k, (hbm, ref) in enumerate(held)]
+    for copy in copies:
+        copy.start()
 
     slab = slab_index(columns)
     lane = lanes((rows, width))
@@ -612,8 +645,8 @@
         inside = jnp.logical_and(other >= 0, other < count)
         device = device_of(jnp.clip(other, 0, count - 1), columns)
         keep = jnp.where(inside, 1.0, 0.0)
-        for at, into in ((0, sources), (rows, mobilities)):
-            tile = gathered[device, at : at + rows, :] * keep
+        for part_of, into in ((slice(0, rows), sources), (slice(rows, 2 * rows), mobilities)):
+            tile = gathered[device, part_of, :] * keep
             for z in range(4):
                 v = jnp.where(part == z, tile, 0.0)
                 v = v + swap_lanes(v, 1)
@@ -658,66 +691,51 @@
         coarsest[2 * k * rows : (2 * k + 1) * rows, :] = jnp.where(low[0], a, b)
         coarsest[(2 * k + 1) * rows : (2 * k + 2) * rows, :] = jnp.where(low[0], b, a)
 
-    for copy in copies[5 : KEPT - 2] + copies[KEPT - 1 :]:
+    for copy in copies:
         copy.wait()
     near_at, far_at = neighbour_rows(columns)
+    here = slice(*OWN)
     first = lanes((ROWS, width)) % 2 == 0
     for i in range(rows):
         half = coarsest[pl.ds(i, WIN // 2, stride=rows), :]
         spread[pl.ds(0, WIN // 2, stride=2), :] = half
         spread[pl.ds(1, WIN // 2, stride=2), :] = half
-        e1[i + 1, 2 * ROWS : 3 * ROWS, :] = e1[i + 1, 2 * ROWS : 3 * ROWS, :] + spread[ROWS : 2 * ROWS, :]
-        for at, ref in ((near_at, near), (far_at, far)):
+        e1[i, here, :] = e1[i, here, :] + spread[here, :]
+        for row, ref in ((near_at, near), (far_at, far)):
             mixed = ref[i, 0:ROWS, :]
             other = swap_lanes(mixed, 1)
-            e1[i + 1, pl.ds(at + ROWS, ROWS), :] = jnp.where(first, mixed, other) + spread[pl.ds(at, ROWS), :]
-            cscaled0[i, pl.ds(at, ROWS), :] = jnp.where(first, other, mixed)
-            cscaled1[i, pl.ds(at, ROWS), :] = ref[i, ROWS : 2 * ROWS, :]
-
-    for _ in range(SWEEPS):
-        coarse_pass(0, e0, e1, cshare0, cscaled0)
-        coarse_pass(1, e1, e0, cshare1, cscaled1)
+            part = pl.ds(row, ROWS)
+            e1[i, part, :] = jnp.where(first, mixed, other) + spread[part, :]
+            cscaled0[i, part, :] = jnp.where(first, other, mixed)
+            cscaled1[i, part, :] = ref[i, ROWS : 2 * ROWS, :]
+
+    renew(coarse_flow, 0, e0, e1, cface, cinverse0, cscaled0, (1, WIN - 1))
+    renew(coarse_flow, 1, e1, e0, cface, cinverse1, cscaled1, (2, WIN - 2))
+    renew(coarse_flow, 0, e0, e1, cface, cinverse0, cscaled0, (3, WIN - 3))
+    renew(coarse_flow, 1, e1, e0, cface, cinverse1, cscaled1, INNER)
 
     even = coarse_low(0, width, INNER)
-
-    for copy in copies[:5] + copies[KEPT - 2 : KEPT - 1]:
-        copy.wait()
-
-    here = shifted(INNER, 0)
-
-    def correct(i, _):
-        a, b = e0[i + 1, here, :], e1[i + 1, here, :]
+    for i in range(rows):
+        a, b = e0[i, at(e0, INNER), :], e1[i, at(e1, INNER), :]
         for half, add in ((0, jnp.where(even, a, b)), (1, jnp.where(even, b, a))):
-            for parity in (0, 1):
-                x = 4 * i + 2 * half + parity
-                v1[x + 1, here, :] = v1[x + 1, here, :] + add
-        return 0
-
-    lax.fori_loop(0, rows, correct, 0)
-
-    for _ in range(SWEEPS):
-        fine_pass(0, v0, v1, share0, scaled0, INNER)
-        fine_pass(1, v1, v0, share1, scaled1, INNER)
-
-    here, part = shifted(OWN, 0), slice(*OWN)
-
-    def fold(i, _):
-        rest = []
-        for parity in range(4):
-            x = 4 * i + parity
-            sides = around_fine(v1, x, fine_low(parity % 2, 0, width, OWN), OWN)
-            updated = relax(scaled0[x, part, :], share0[:, x, part, :], sides)
-            rest.append(diagonal0[x, part, :] * (updated - v0[x + 1, here, :]))
+            for x in (4 * i + 2 * half, 4 * i + 2 * half + 1):
+                v1[x] = field1[x] + add
+
+    renew(fine_flow, 0, v0, v1, face, inverse0, scaled0, wider(INNER, -1))
+    renew(fine_flow, 1, v1, v0, face, inverse1, scaled1, wider(INNER, -2))
+    renew(fine_flow, 0, v0, v1, face, inverse0, scaled0, wider(OWN, 1))
+    renew(fine_flow, 1, v1, v0, face, inverse1, scaled1, wider(OWN, 1))
+
+    for i in range(rows):
+        planes_of = range(4 * i, 4 * i + 4)
+        rest = [rest_of(fine_flow, v0, v1, face, inverse0, scaled0, x, OWN) for x in planes_of]
         for a, tiles in (
-            (0, [v0[4 * i + b + 1, here, :] for b in range(4)]),
-            (1, [v1[4 * i + b + 1, here, :] for b in range(4)]),
+            (0, [v0[x, at(v0, OWN), :] for x in planes_of]),
+            (1, [v1[x, at(v1, OWN), :] for x in planes_of]),
             (2, rest),
         ):
             for j, tile in enumerate(swap_blocks(tiles)):
                 out[4 * i + j, a * ROWS : (a + 1) * ROWS, :] = tile
-        return 0
-
-    lax.fori_loop(0, rows, fold, 0, unroll=True)
 
 
 def local_slabs(shape, right_side, phase, pressure_guess):
@@ -731,6 +749,7 @@
     near = [pair for k in range(0, count, 2) for pair in ((path[k], path[k + 1]), (path[k + 1], path[k]))]
     far = [pair for k in range(1, count - 1, 2) for pair in ((path[k], path[k + 1]), (path[k + 1], path[k]))]
     axes = ("gx", "yz")
+    cost = pl.CostEstimate(flops=20_000_000_000, bytes_accessed=100_000_000, transcendentals=0)
     params = pltpu.CompilerParams(vmem_limit_bytes=20 * 1024 * 1024)
 
     def struct(*dims):
@@ -760,46 +779,45 @@
     fields_far = lax.ppermute(fields, axes, far)
 
     coarse = planes // 4
-    share, cshare = (6, planes, WIN, width), (6, coarse, WIN, width)
-    plane, cplane = (planes, WIN, width), (coarse, WIN, width)
-    padded = [vmem(planes + 2, WIN + 2 * ROWS, width)] * 2
-    cpadded = [vmem(coarse + 2, WIN + 2 * ROWS, width)] * 2
-
-    def hbm(*shapes):
+    face, plane = (6, planes, WIN, width), (planes, WIN, width)
+    cface, cplane = (6, coarse, WIN, width), (coarse, WIN, width)
+    height = INNER[1] - INNER[0]
+    iplane = (planes, height, width)
+    letter = (coarse, 2 * ROWS, width)
+
+    def in_hbm(*arrays):
+        return [pltpu.with_memory_space_constraint(x, pltpu.HBM) for x in arrays]
+
+    def far_outs(*shapes):
         return [pltpu.HBM(dims, f32) for dims in shapes], [pl.BlockSpec(memory_space=pltpu.HBM)] * len(shapes)
 
-    def near_core(*shapes):
+    def near_outs(*shapes):
         return [struct(*dims) for dims in shapes], [pl.BlockSpec(memory_space=pltpu.VMEM)] * len(shapes)
 
-    first = near_core(share, share, plane, plane, plane, cshare, cshare, cplane, cplane, cplane, (coarse, width))
-    second = hbm(share, share, plane, cshare, cshare)
-    *made, share0, share1, diagonal0, cshare0, cshare1 = pl.pallas_call(
+    made = pl.pallas_call(
         functools.partial(weights_kernel, columns),
-        out_shape=first[0] + second[0],
-        out_specs=first[1] + second[1],
-        scratch_shapes=padded + cpadded + [vmem(WIN, width), pltpu.SemaphoreType.DMA((5,))],
+        out_shape=near_outs(face, plane, plane, cface, cplane, cplane, (coarse, width))[0],
+        scratch_shapes=[vmem(*plane)] * 2 + [vmem(*cplane)] * 2 + [vmem(WIN, width)],
         compiler_params=params,
-        cost_estimate=pl.CostEstimate(flops=20_000_000_000, bytes_accessed=100_000_000, transcendentals=0),
+        cost_estimate=cost,
         name="weights",
     )(own, own_near, mobility_far)
 
-    first = hbm(plane, plane, cplane, cplane, plane, cplane, (coarse, 2 * ROWS, width))
-    second = near_core((count, 2 * coarse, width))
-    scaled0, scaled1, cscaled0, cscaled1, field1, cfield1, message, packed = pl.pallas_call(
+    first = near_outs((11, planes, height, width))
+    second = far_outs((11, coarse, WIN, width), letter, (count, 2 * coarse, width))
+    state, cstate, message, packed = pl.pallas_call(
         functools.partial(down_kernel, columns),
         out_shape=first[0] + second[0],
         out_specs=first[1] + second[1],
-        scratch_shapes=[vmem(*plane)] * 2 + [vmem(*cplane)] * 2 + padded + cpadded + [
+        scratch_shapes=[vmem(*plane)] * 2 + [vmem(*cplane)] * 2 + [vmem(*plane)] * 2 + [vmem(*cplane)] * 2 + [
             vmem(WIN, width),
-            vmem(coarse, 2 * ROWS, width),
-            pltpu.SemaphoreType.DMA((7,)),
+            vmem(*letter),
+            vmem(count, 2 * coarse, width),
+            pltpu.SemaphoreType.DMA((14,)),
         ],
         compiler_params=params,
         name="down",
     )(*made, own, own_near, fields_far)
-    state = (share0, share1, scaled0, scaled1, diagonal0, cshare0, cshare1, cscaled0, cscaled1, field1, cfield1)
-    fine = [vmem(*share)] * 2 + [vmem(*plane)] * 3
-    half = [vmem(*cshare)] * 2 + [vmem(*cplane)] * 2
     gathered = lax.all_to_all(packed, axes, 0, 0)
     message_far = lax.ppermute(message, axes, far)
     message_near = lax.ppermute(message, axes, near)
@@ -807,16 +825,16 @@
     cycle = pl.pallas_call(
         functools.partial(up_kernel, columns),
         out_shape=struct(count, 3 * ROWS, 128),
-        in_specs=[pl.BlockSpec(memory_space=pltpu.VMEM)] + [pl.BlockSpec(memory_space=pltpu.HBM)] * (KEPT + 2),
-        scratch_shapes=fine + half + padded + cpadded + [vmem(coarse, 2 * ROWS, width)] * 2 + [
+        in_specs=[pl.BlockSpec(memory_space=pltpu.VMEM)] * 2 + [pl.BlockSpec(memory_space=pltpu.HBM)] * 3,
+        scratch_shapes=[vmem(11, *cplane)] + [vmem(*iplane)] * 2 + [vmem(*cplane)] + [vmem(*letter)] * 2 + [
             vmem(2, 6, 2 * (2 * REACH + 1), coarse, width),
             vmem(WIN // 2 * coarse, width),
             vmem(WIN, width),
-            pltpu.SemaphoreType.DMA((KEPT + 2,)),
+            pltpu.SemaphoreType.DMA((3,)),
         ],
         compiler_params=params,
         name="up",
-    )(gathered, *(pltpu.with_memory_space_constraint(x, pltpu.HBM) for x in (*state, message_near, message_far)))
+    )(gathered, state, *in_hbm(cstate, message_near, message_far))
     back = lax.all_to_all(cycle, axes, 0, 0)
     return pl.pallas_call(
         functools.partial(unpack_kernel, order),

time: 79.2 us -> 75.9 us (0.958)
  Pallas kernels: 15.9 us -> 9.83 us
  starting transfers between devices: 14.5 us -> 17.3 us
    pallas_call x1, Pallas kernels: 4.72 us -> 1.34 us  [local_slabs(): pl.pallas_call(functools.partial(weights_kernel, columns), out_shape=near...]
    all_to_all x1, starting transfers between devices: 9.16 us -> 12 us  [local_slabs(): gathered = lax.all_to_all(packed, axes, 0, 0)]
    pallas_call x1, Pallas kernels: 4.38 us -> 2.96 us  [local_slabs(): pl.pallas_call(functools.partial(up_kernel, columns), out_shape=struct(co...]
    pallas_call x1, Pallas kernels: 4.45 us -> 3.14 us  [local_slabs(): pl.pallas_call(functools.partial(down_kernel, columns), out_shape=first[0...]
  transfers between devices with their start and end apart: 6 -> 6, of which waited for: 3 -> 3; matrix products, arithmetic and copies ran while one was open for 0% -> 0% of each run, Pallas kernels for 6% -> 2%
where the time goes in v6:
time: 75.9 us; the launch traced here: 75.6 us
  blocking collectives  40.4 us (53%)
  starting transfers between devices  17.3 us (23%)
  Pallas kernels  9.83 us (13%)
  waiting for transfers between devices  7.31 us (10%)
    all_to_all x1, blocking collectives, local_slabs(): own = lax.all_to_all(bricks, axes, 0, 0)  25 us
    all_to_all x1, blocking collectives, local_slabs(): back = lax.all_to_all(cycle, axes, 0, 0)  15.4 us
    all_to_all x1, starting transfers between devices, local_slabs(): gathered = lax.all_to_all(packed, axes, 0, 0)  12 us
    all_to_all x1, waiting for transfers between devices, local_slabs(): gathered = lax.all_to_all(packed, axes, 0, 0)  5.62 us
    ppermute x1, starting transfers between devices, local_slabs(): message_near = lax.ppermute(message, axes, near)  3.19 us
    pallas_call x1, Pallas kernels, local_slabs(): pl.pallas_call(functools.partial(down_kernel, columns), out_shape=first[0...  3.14 us
    pallas_call x1, Pallas kernels, local_slabs(): pl.pallas_call(functools.partial(up_kernel, columns), out_shape=struct(co...  2.96 us
  transfers between devices with their start and end apart: 6, of which 3 were waited for; matrix products, arithmetic and copies ran while one was open for 0% of the time, Pallas kernels for 2%

profile of v6, /device:TPU:0, one launch (start us, length us, event | category | flops | bytes accessed | tf_op | source)
XLA Modules:
  0.0 75.6 jit_solution(9837452631536165069)
XLA Ops:
  0.6 1.4 %pack.1 = f32[32,40,128]{2,1,0:T(8,128)S(1)} custom-call(f32[4,32,512]{2,1,0:T(8,128)} %source_hbm.1, s32[4,32,512]{2,1,0:T(8,128)} %phase_hbm.1, f32[4,32,512]{2,1,0:T(8,128)} %guess_hbm.1), custom_call_target="tpu_custom_call" | custom-call | tf_op jit(solution)/shard_map/pack/pallas_call | solution.py:761
  2.1 25.0 %all_to_all.15.own = f32[32,40,128]{2,1,0:T(8,128)S(1)} all-to-all(f32[32,40,128]{2,1,0:T(8,128)S(1)} %pack.1), channel_id=1, replica_groups=mesh['gx'=8,'yz'=4] {'gx','yz'}, dimensions={0} | all-to-all | bytes 1310720 | tf_op jit(solution)/shard_map/all_to_all | solution.py:775
  27.1 0.1 collective-permute-start
  27.2 0.7 collective-permute-start.1
  27.9 0.7 collective-permute-start.2
  28.6 0.0 collective-permute-done.1.far
  28.6 0.6 collective-permute-done.near
  29.2 1.3 %weights.1 = (f32[6,32,24,128]{3,2,1,0:T(8,128)S(1)}, f32[32,24,128]{2,1,0:T(8,128)S(1)}, f32[32,24,128]{2,1,0:T(8,128)S(1)}, f32[6,8,24,128]{3,2,1,0:T(8,128)S(...) custom-call(f32[32,40,128]{2,1,0:T(8,128)S(1)} %all_to_all.15.own, ...), custom_call_target="tpu_custom_call" | custom-call | flops 20000000000 | bytes 100000000 | tf_op jit(solution)/shard_map/weights/pallas_call | solution.py:797
  30.5 0.0 collective-permute-done.2.far
  30.6 3.1 %down.1 = (f32[11,32,16,128]{3,2,1,0:T(8,128)S(1)}, f32[11,8,24,128]{3,2,1,0:T(8,128)}, f32[8,16,128]{2,1,0:T(8,128)}, f32[32,16,128]{2,1,0:T(8,128)}) custom-call(f32[6,32,24,128]{3,2,1,0:T(8,128)S(1)} %get-tuple-element.13.face, f32[32,24,128]{2,1,0:T(8,128)S(1)} %get-tuple-element.14.inverse0, f32[32,24,128]{2,1,0:T(8,128)S(1)} %get-tuple-element.15.inverse1, ...), custom_call_target="tpu_custom_call" | custom-call | tf_op jit(solution)/shard_map/down/pallas_call | solution.py:808
  33.7 12.0 %all-to-all-start.1 = ((f32[32,16,128]{2,1,0:T(8,128)}), f32[32,16,128]{2,1,0:T(8,128)S(1)}, u32[]{:S(2)}, u32[]{:S(2)}) async-start(f32[32,16,128]{2,1,0:T(8,128)} %get-tuple-element.20), calls=%async_computation.1 | async-start | bytes 524288 | tf_op jit(solution)/shard_map/all_to_all | solution.py:821
  45.7 0.7 collective-permute-start.4
  46.4 3.2 %collective-permute-start.3 = (f32[8,16,128]{2,1,0:T(8,128)}, f32[8,16,128]{2,1,0:T(8,128)S(1)}, u32[]{:S(2)}, u32[]{:S(2)}) collective-permute-start(f32[8,16,128]{2,1,0:T(8,128)} %get-tuple-element.23), channel_id=1, source_target_pairs={{0,1},{1,0},{2,3},{3,2},{7,6},{6,7},{5,4},{4,5},{12,13},{13,12},{1... | collective-permute-start | bytes 196616 | tf_op jit(solution)/shard_map/ppermute | solution.py:823
  49.6 0.0 collective-permute-done.4.far_hbm
  49.6 0.0 copy-start
  49.6 1.1 %collective-permute-done.3.near_hbm = f32[8,16,128]{2,1,0:T(8,128)S(1)} collective-permute-done((f32[8,16,128]{2,1,0:T(8,128)}, f32[8,16,128]{2,1,0:T(8,128)S(1)}, u32[]{:S(2)}, u32[]{:S(2)}) %collective-permute-start.3) | collective-permute-done | bytes 65568 | tf_op jit(solution)/shard_map/ppermute | solution.py:823
  50.7 0.0 copy-start.1
  50.7 5.6 %all-to-all-done.1.gathered = f32[32,16,128]{2,1,0:T(8,128)S(1)} async-done(((f32[32,16,128]{2,1,0:T(8,128)}), f32[32,16,128]{2,1,0:T(8,128)S(1)}, u32[]{:S(2)}, u32[]{:S(2)}) %all-to-all-start.1) | async-done | bytes 262176 | tf_op jit(solution)/shard_map/all_to_all | solution.py:821
  56.3 0.0 copy-done
  56.3 0.0 copy-done.1
  56.3 3.0 %up.1 = f32[32,24,128]{2,1,0:T(8,128)S(1)} custom-call(f32[32,16,128]{2,1,0:T(8,128)S(1)} %all-to-all-done.1.gathered, f32[11,32,16,128]{3,2,1,0:T(8,128)S(1)} %get-tuple-element.21.state, f32[11,8,24,128]{3,2,1,0:T(8,128)} %get-tuple-element.22.cstate_hbm, f32[8,16,128]{2,1,0:T(8,128)} %copy-done.1, f32[8,16,128]{2,1,0:T(8,128)} %copy-done), custom_call_target="tpu_custom_call" | custom-call | tf_op jit(solution)/shard_map/up/pallas_call | solution.py:825
  59.3 15.4 %all_to_all.16.in_ref = f32[32,24,128]{2,1,0:T(8,128)S(1)} all-to-all(f32[32,24,128]{2,1,0:T(8,128)S(1)} %up.1), channel_id=1, replica_groups=mesh['gx'=8,'yz'=4] {'gx','yz'}, dimensions={0} | all-to-all | bytes 786432 | tf_op jit(solution)/shard_map/all_to_all | solution.py:838
  74.7 0.9 %unpack.1 = (f32[4,32,512]{2,1,0:T(8,128)}, f32[4,32,512]{2,1,0:T(8,128)}) custom-call(f32[32,24,128]{2,1,0:T(8,128)S(1)} %all_to_all.16.in_ref), custom_call_target="tpu_custom_call" | custom-call | tf_op jit(solution)/shard_map/unpack/pallas_call | solution.py:839
  (2 shorter events, 0.0 us)
Async XLA Ops:
  27.1 2.1 %collective-permute-start = (f32[32,40,128]{2,1,0:T(8,128)S(1)}, f32[32,40,128]{2,1,0:T(8,128)S(1)}, u32[]{:S(2)}, u32[]{:S(2)}) collective-permute-start(f32[32,40,128]{2,1,0:T(8,128)S(1)} %all_to_all.15.own), channel_id=1, source_target_pairs={{0,1},{1,0},{2,3},{3,2},{7,6},{6,7},{5,4},{4,5},{12,13},{13,12},{1... | collective-permute-start | bytes 1966088 | tf_op jit(solution)/shard_map/ppermute | solution.py:778
  27.2 1.4 %collective-permute-start.1 = (f32[32,16,128]{2,1,0:T(8,128)S(1)}, f32[32,16,128]{2,1,0:T(8,128)S(1)}, u32[]{:S(2)}, u32[]{:S(2)}) collective-permute-start(f32[32,16,128]{2,1,0:T(8,128)S(1)} %slice.8), channel_id=1, source_target_pairs={{1,2},{2,1},{3,7},{7,3},{6,5},{5,6},{4,12},{12,4},{13,14},{14,13},... | collective-permute-start | bytes 786440 | tf_op jit(solution)/shard_map/ppermute | solution.py:777
  27.9 2.6 %collective-permute-start.2 = (f32[32,24,128]{2,1,0:T(8,128)S(1)}, f32[32,24,128]{2,1,0:T(8,128)S(1)}, u32[]{:S(2)}, u32[]{:S(2)}) collective-permute-start(f32[32,24,128]{2,1,0:T(8,128)S(1)} %slice.9), channel_id=1, source_target_pairs={{1,2},{2,1},{3,7},{7,3},{6,5},{5,6},{4,12},{12,4},{13,14},{14,13},... | collective-permute-start | bytes 1179656 | tf_op jit(solution)/shard_map/ppermute | solution.py:779
  33.7 22.6 %all-to-all-start.1 = ((f32[32,16,128]{2,1,0:T(8,128)}), f32[32,16,128]{2,1,0:T(8,128)S(1)}, u32[]{:S(2)}, u32[]{:S(2)}) async-start(f32[32,16,128]{2,1,0:T(8,128)} %get-tuple-element.20), calls=%async_computation.1 | async-start | bytes 524288 | tf_op jit(solution)/shard_map/all_to_all | solution.py:821
  45.7 3.9 %collective-permute-start.4 = (f32[8,16,128]{2,1,0:T(8,128)}, f32[8,16,128]{2,1,0:T(8,128)S(1)}, u32[]{:S(2)}, u32[]{:S(2)}) collective-permute-start(f32[8,16,128]{2,1,0:T(8,128)} %get-tuple-element.23), channel_id=1, source_target_pairs={{1,2},{2,1},{3,7},{7,3},{6,5},{5,6},{4,12},{12,4},{13,14},{14,13},... | collective-permute-start | bytes 196616 | tf_op jit(solution)/shard_map/ppermute | solution.py:822
  46.4 4.3 %collective-permute-start.3 = (f32[8,16,128]{2,1,0:T(8,128)}, f32[8,16,128]{2,1,0:T(8,128)S(1)}, u32[]{:S(2)}, u32[]{:S(2)}) collective-permute-start(f32[8,16,128]{2,1,0:T(8,128)} %get-tuple-element.23), channel_id=1, source_target_pairs={{0,1},{1,0},{2,3},{3,2},{7,6},{6,7},{5,4},{4,5},{12,13},{13,12},{1... | collective-permute-start | bytes 196616 | tf_op jit(solution)/shard_map/ppermute | solution.py:823
  49.6 6.7 %copy-start = (f32[8,16,128]{2,1,0:T(8,128)}, f32[8,16,128]{2,1,0:T(8,128)S(1)}, u32[]{:S(2)}) copy-start(f32[8,16,128]{2,1,0:T(8,128)S(1)} %collective-permute-done.4.far_hbm) | copy-start | bytes 196612
  50.7 5.6 %copy-start.1 = (f32[8,16,128]{2,1,0:T(8,128)}, f32[8,16,128]{2,1,0:T(8,128)S(1)}, u32[]{:S(2)}) copy-start(f32[8,16,128]{2,1,0:T(8,128)S(1)} %collective-permute-done.3.near_hbm) | copy-start | bytes 196612

commit v7 on v6

--- a/solution.py
+++ b/solution.py
@@ -234,12 +234,12 @@
     even = brick_parity((ROWS, 128)) == 0
     for device, slab in enumerate(order):
         base = 2 * ROWS * slab
-        for a, at in ((1, 0), (0, 2 * ROWS), (2, 3 * ROWS)):
+        for a, row in ((1, 0), (2, ROWS), (0, 3 * ROWS)):
             low = turned[a, pl.ds(base, ROWS, stride=2), :]
             high = turned[a, pl.ds(base + 1, ROWS, stride=2), :]
             if a != 2:
-                out_ref[device, at : at + ROWS, :] = jnp.where(even, low, high)
-            out_ref[device, at + ROWS : at + 2 * ROWS, :] = jnp.where(even, high, low)
+                out_ref[device, row : row + ROWS, :] = jnp.where(even, low, high)
+            out_ref[device, row + ROWS : row + 2 * ROWS, :] = jnp.where(even, high, low)
 
 
 def unpack_kernel(order, in_ref, pressure_ref, residual_ref, turned):
@@ -330,13 +330,23 @@
     return (row + lanes(shape) // 2 + colour) % 2 == 0
 
 
-def fine_sides(v, x, low, rows):
-    here = at(v, rows)
-    centre = v[x, here, :]
+def loader(v, rows):
+    seen = {}
+
+    def load(x):
+        if x not in seen:
+            seen[x] = v[x, at(v, rows), :]
+        return seen[x]
+
+    return load
+
+
+def fine_sides(v, load, x, low, rows):
+    centre = load(x)
     width = centre.shape[1]
     return (
-        v[x - 1, here, :] if x > 0 else None,
-        v[x + 1, here, :] if x + 1 < v.shape[0] else None,
+        load(x - 1) if x > 0 else None,
+        load(x + 1) if x + 1 < v.shape[0] else None,
         pltpu.roll(centre, 1, 1),
         pltpu.roll(centre, width - 1, 1),
         centre,
@@ -344,17 +354,19 @@
     )
 
 
-def fine_flow(colour, face, v, x, rows):
+def fine_flow(colour, face, v, x, rows, load=None):
     planes, width = face.shape[1], face.shape[3]
     part = at(face, rows)
     low = fine_low(x, colour, width, rows)
+    if v is not None and load is None:
+        load = loader(v, rows)
     if colour == 0:
-        sides = fine_sides(v, x, low, rows)
+        sides = fine_sides(v, load, x, low, rows)
         return add_up([face[a, x, part, :] * side for a, side in enumerate(sides) if side is not None])
 
     def carried(a, plane):
         values = face[a, plane, part, :]
-        return values if v is None else values * v[plane, at(v, rows), :]
+        return values if v is None else values * load(plane)
 
     away = beyond(face, x, low, rows, 5)
     terms = [
@@ -386,7 +398,7 @@
     )
 
 
-def coarse_flow(colour, face, v, i, rows):
+def coarse_flow(colour, face, v, i, rows, load=None):
     planes, width = face.shape[1], face.shape[3]
     low = coarse_low(colour, width, rows)
     if colour == 0:
@@ -413,8 +425,9 @@
 
 
 def renew(flow, colour, target, other, face, inverse, scaled, rows):
+    load = loader(other, rows)
     for x in range(face.shape[1]):
-        moved = inverse[x, at(inverse, rows), :] * flow(colour, face, other, x, rows)
+        moved = inverse[x, at(inverse, rows), :] * flow(colour, face, other, x, rows, load)
         target[x, at(target, rows), :] = scaled[x, at(scaled, rows), :] + moved
 
 
@@ -433,10 +446,11 @@
     rows = FACE_ROWS
     here = at(face, rows)
     lane = lanes((rows[1] - rows[0], width))
+    load = loader(m1, rows)
     for x in range(planes):
         low = fine_low(x, 0, width, rows)
         u = m0[x, here, :]
-        sides = walls(fine_sides(m1, x, low, rows), lane == 0, lane == width - 1)
+        sides = walls(fine_sides(m1, load, x, low, rows), lane == 0, lane == width - 1)
         terms = []
         for a, side in enumerate(sides):
             value = jnp.zeros_like(u) if side is None else mean_fine(u, side)
@@ -516,14 +530,19 @@
 def weights_kernel(
     columns,
     own, near, far,
-    face, inverse0, inverse1, cface, cinverse0, cinverse1, coarsest,
-    m0, m1, cm0, cm1, rest,
+    face, inverse0, inverse1, cface, cinverse0, cinverse1, coarsest, flow0,
+    m0, m1, guess, cm0, cm1, rest,
 ):
     planes, width = face.shape[1], face.shape[3]
     near_at, far_at = neighbour_rows(columns)
     places = ((own, 0, ROWS), (near, 0, near_at), (far, 0, far_at))
-    unfold_slabs(places, ((0, plain_store(m0)), (ROWS, plain_store(m1))), planes)
+    arrays = ((0, plain_store(m0)), (ROWS, plain_store(m1)), (2 * ROWS, plain_store(guess)))
+    unfold_slabs(places, arrays, planes)
     fine_faces(m0, m1, face, inverse0, inverse1)
+    flow0[...] = jnp.zeros(flow0.shape, jnp.float32)
+    load = loader(guess, FACE_ROWS)
+    for x in range(planes):
+        flow0[x, slice(*FACE_ROWS), :] = fine_flow(0, face, guess, x, FACE_ROWS, load)
     even = coarse_low(0, width, (0, WIN))
     for i in range(planes // 4):
         mobilities = []
@@ -543,7 +562,7 @@
 
 def down_kernel(
     columns,
-    face, inverse0, inverse1, cface, cinverse0, cinverse1, coarsest,
+    face, inverse0, inverse1, cface, cinverse0, cinverse1, coarsest, flow0,
     own, near, far,
     *refs,
 ):
@@ -561,17 +580,20 @@
     for copy in copies[:3] + copies[6:9]:
         copy.start()
     near_at, far_at = neighbour_rows(columns)
-    places = ((own, 2 * ROWS, ROWS), (near, 2 * ROWS, near_at), (far, 0, far_at))
-    arrays = (
-        (0, scaled_store(scaled0, inverse0)),
-        (ROWS, scaled_store(scaled1, inverse1)),
-        (2 * ROWS, plain_store(v1)),
-    )
+    places = ((own, 0, ROWS), (near, 3 * ROWS, near_at), (far, 0, far_at))
+
+    def first_pass(x, row, tile):
+        part = pl.ds(row, ROWS)
+        factor = inverse0[x, part, :]
+        scaled = tile * factor
+        scaled0[x, part, :] = scaled
+        v0[x, part, :] = scaled + flow0[x, part, :] * factor
+
+    arrays = ((0, first_pass), (ROWS, scaled_store(scaled1, inverse1)))
     unfold_slabs(places, arrays, planes)
     for copy in copies[3:5]:
         copy.start()
 
-    renew(fine_flow, 0, v0, v1, face, inverse0, scaled0, (1, WIN - 1))
     renew(fine_flow, 1, v1, v0, face, inverse1, scaled1, (2, WIN - 2))
     renew(fine_flow, 0, v0, v1, face, inverse0, scaled0, (3, WIN - 3))
     renew(fine_flow, 1, v1, v0, face, inverse1, scaled1, (3, WIN - 3))
@@ -773,10 +795,10 @@
         name="pack",
     )(*(pltpu.with_memory_space_constraint(x, pltpu.HBM) for x in (right_side, phase, pressure_guess)))
     own = lax.all_to_all(bricks, axes, 0, 0)
-    mobility, fields = own[:, : 2 * ROWS], own[:, 2 * ROWS :]
-    mobility_far = lax.ppermute(mobility, axes, far)
+    first_part, second_part = own[:, : 3 * ROWS], own[:, 3 * ROWS :]
+    first_far = lax.ppermute(first_part, axes, far)
     own_near = lax.ppermute(own, axes, near)
-    fields_far = lax.ppermute(fields, axes, far)
+    second_far = lax.ppermute(second_part, axes, far)
 
     coarse = planes // 4
     face, plane = (6, planes, WIN, width), (planes, WIN, width)
@@ -796,12 +818,12 @@
 
     made = pl.pallas_call(
         functools.partial(weights_kernel, columns),
-        out_shape=near_outs(face, plane, plane, cface, cplane, cplane, (coarse, width))[0],
-        scratch_shapes=[vmem(*plane)] * 2 + [vmem(*cplane)] * 2 + [vmem(WIN, width)],
+        out_shape=near_outs(face, plane, plane, cface, cplane, cplane, (coarse, width), plane)[0],
+        scratch_shapes=[vmem(*plane)] * 3 + [vmem(*cplane)] * 2 + [vmem(WIN, width)],
         compiler_params=params,
         cost_estimate=cost,
         name="weights",
-    )(own, own_near, mobility_far)
+    )(first_part, own_near, first_far)
 
     first = near_outs((11, planes, height, width))
     second = far_outs((11, coarse, WIN, width), letter, (count, 2 * coarse, width))
@@ -817,7 +839,7 @@
         ],
         compiler_params=params,
         name="down",
-    )(*made, own, own_near, fields_far)
+    )(*made, second_part, own_near, second_far)
     gathered = lax.all_to_all(packed, axes, 0, 0)
     message_far = lax.ppermute(message, axes, far)
     message_near = lax.ppermute(message, axes, near)

time: 75.9 us -> 75.6 us (level)
  no operation moved by 1% of the time
where the time goes in v7:
time: 75.6 us; the launch traced here: 75.3 us
  blocking collectives  40.4 us (53%)
  starting transfers between devices  17.1 us (23%)
  Pallas kernels  9.74 us (13%)
  waiting for transfers between devices  7.31 us (10%)
    all_to_all x1, blocking collectives, local_slabs(): own = lax.all_to_all(bricks, axes, 0, 0)  25 us
    all_to_all x1, blocking collectives, local_slabs(): back = lax.all_to_all(cycle, axes, 0, 0)  15.4 us
    all_to_all x1, starting transfers between devices, local_slabs(): gathered = lax.all_to_all(packed, axes, 0, 0)  11.8 us
    all_to_all x1, waiting for transfers between devices, local_slabs(): gathered = lax.all_to_all(packed, axes, 0, 0)  5.62 us
    ppermute x1, starting transfers between devices, local_slabs(): message_near = lax.ppermute(message, axes, near)  3.19 us
    pallas_call x1, Pallas kernels, local_slabs(): pl.pallas_call(functools.partial(up_kernel, columns), out_shape=struct(co...  2.97 us
    pallas_call x1, Pallas kernels, local_slabs(): pl.pallas_call(functools.partial(down_kernel, columns), out_shape=first[0...  2.82 us
    pallas_call x1, Pallas kernels, local_slabs(): pl.pallas_call(functools.partial(weights_kernel, columns), out_shape=near...  1.55 us
  transfers between devices with their start and end apart: 6, of which 3 were waited for; matrix products, arithmetic and copies ran while one was open for 0% of the time, Pallas kernels for 2%

profile of v7, /device:TPU:0, one launch (start us, length us, event | category | flops | bytes accessed | tf_op | source)
XLA Modules:
  0.0 75.3 jit_solution(10495261032767641136)
XLA Ops:
  0.6 1.4 %pack.1 = f32[32,40,128]{2,1,0:T(8,128)S(1)} custom-call(f32[4,32,512]{2,1,0:T(8,128)} %source_hbm.1, s32[4,32,512]{2,1,0:T(8,128)} %phase_hbm.1, f32[4,32,512]{2,1,0:T(8,128)} %guess_hbm.1), custom_call_target="tpu_custom_call" | custom-call | tf_op jit(solution)/shard_map/pack/pallas_call | solution.py:783
  2.1 25.0 %all_to_all.15 = f32[32,40,128]{2,1,0:T(8,128)S(1)} all-to-all(f32[32,40,128]{2,1,0:T(8,128)S(1)} %pack.1), channel_id=1, replica_groups=mesh['gx'=8,'yz'=4] {'gx','yz'}, dimensions={0} | all-to-all | bytes 1310720 | tf_op jit(solution)/shard_map/all_to_all | solution.py:797
  27.1 0.1 collective-permute-start
  27.2 0.7 collective-permute-start.1
  27.9 0.7 collective-permute-start.2
  28.6 0.0 collective-permute-done.1.far
  28.6 0.6 collective-permute-done.near
  29.2 1.6 %weights.1 = (f32[6,32,24,128]{3,2,1,0:T(8,128)S(1)}, f32[32,24,128]{2,1,0:T(8,128)S(1)}, f32[32,24,128]{2,1,0:T(8,128)S(1)}, f32[6,8,24,128]{3,2,1,0:T(8,128)S(...) custom-call(f32[32,24,128]{2,1,0:T(8,128)S(1)} %slice.8.own, ...), custom_call_target="tpu_custom_call" | custom-call | flops 20000000000 | bytes 100000000 | tf_op jit(solution)/shard_map/weights/pallas_call | solution.py:819
  30.8 0.0 collective-permute-done.2.far
  30.8 2.8 %down.1 = (f32[11,32,16,128]{3,2,1,0:T(8,128)S(1)}, f32[11,8,24,128]{3,2,1,0:T(8,128)}, f32[8,16,128]{2,1,0:T(8,128)}, f32[32,16,128]{2,1,0:T(8,128)}) custom-call(f32[6,32,24,128]{3,2,1,0:T(8,128)S(1)} %get-tuple-element.14.face, f32[32,24,128]{2,1,0:T(8,128)S(1)} %get-tuple-element.15.inverse0, f32[32,24,128]{2,1,0:T(8,128)S(1)} %get-tuple-element.16.inverse1, ...), custom_call_target="tpu_custom_call" | custom-call | tf_op jit(solution)/shard_map/down/pallas_call | solution.py:830
  33.6 11.8 %all-to-all-start.1 = ((f32[32,16,128]{2,1,0:T(8,128)}), f32[32,16,128]{2,1,0:T(8,128)S(1)}, u32[]{:S(2)}, u32[]{:S(2)}) async-start(f32[32,16,128]{2,1,0:T(8,128)} %get-tuple-element.22), calls=%async_computation.1 | async-start | bytes 524288 | tf_op jit(solution)/shard_map/all_to_all | solution.py:843
  45.4 0.7 collective-permute-start.4
  46.1 3.2 %collective-permute-start.3 = (f32[8,16,128]{2,1,0:T(8,128)}, f32[8,16,128]{2,1,0:T(8,128)S(1)}, u32[]{:S(2)}, u32[]{:S(2)}) collective-permute-start(f32[8,16,128]{2,1,0:T(8,128)} %get-tuple-element.25), channel_id=1, source_target_pairs={{0,1},{1,0},{2,3},{3,2},{7,6},{6,7},{5,4},{4,5},{12,13},{13,12},{1... | collective-permute-start | bytes 196616 | tf_op jit(solution)/shard_map/ppermute | solution.py:845
  49.3 0.0 collective-permute-done.4.far_hbm
  49.3 0.0 copy-start
  49.3 1.1 %collective-permute-done.3.near_hbm = f32[8,16,128]{2,1,0:T(8,128)S(1)} collective-permute-done((f32[8,16,128]{2,1,0:T(8,128)}, f32[8,16,128]{2,1,0:T(8,128)S(1)}, u32[]{:S(2)}, u32[]{:S(2)}) %collective-permute-start.3) | collective-permute-done | bytes 65568 | tf_op jit(solution)/shard_map/ppermute | solution.py:845
  50.4 0.0 copy-start.1
  50.4 5.6 %all-to-all-done.1.gathered = f32[32,16,128]{2,1,0:T(8,128)S(1)} async-done(((f32[32,16,128]{2,1,0:T(8,128)}), f32[32,16,128]{2,1,0:T(8,128)S(1)}, u32[]{:S(2)}, u32[]{:S(2)}) %all-to-all-start.1) | async-done | bytes 262176 | tf_op jit(solution)/shard_map/all_to_all | solution.py:843
  56.0 0.0 copy-done
  56.0 0.0 copy-done.1
  56.0 3.0 %up.1 = f32[32,24,128]{2,1,0:T(8,128)S(1)} custom-call(f32[32,16,128]{2,1,0:T(8,128)S(1)} %all-to-all-done.1.gathered, f32[11,32,16,128]{3,2,1,0:T(8,128)S(1)} %get-tuple-element.23.state, f32[11,8,24,128]{3,2,1,0:T(8,128)} %get-tuple-element.24.cstate_hbm, f32[8,16,128]{2,1,0:T(8,128)} %copy-done.1, f32[8,16,128]{2,1,0:T(8,128)} %copy-done), custom_call_target="tpu_custom_call" | custom-call | tf_op jit(solution)/shard_map/up/pallas_call | solution.py:847
  59.0 15.4 %all_to_all.16.in_ref = f32[32,24,128]{2,1,0:T(8,128)S(1)} all-to-all(f32[32,24,128]{2,1,0:T(8,128)S(1)} %up.1), channel_id=1, replica_groups=mesh['gx'=8,'yz'=4] {'gx','yz'}, dimensions={0} | all-to-all | bytes 786432 | tf_op jit(solution)/shard_map/all_to_all | solution.py:860
  74.4 0.9 %unpack.1 = (f32[4,32,512]{2,1,0:T(8,128)}, f32[4,32,512]{2,1,0:T(8,128)}) custom-call(f32[32,24,128]{2,1,0:T(8,128)S(1)} %all_to_all.16.in_ref), custom_call_target="tpu_custom_call" | custom-call | tf_op jit(solution)/shard_map/unpack/pallas_call | solution.py:861
  (2 shorter events, 0.0 us)
Async XLA Ops:
  27.1 2.1 %collective-permute-start = (f32[32,40,128]{2,1,0:T(8,128)S(1)}, f32[32,40,128]{2,1,0:T(8,128)S(1)}, u32[]{:S(2)}, u32[]{:S(2)}) collective-permute-start(f32[32,40,128]{2,1,0:T(8,128)S(1)} %all_to_all.15), channel_id=1, source_target_pairs={{0,1},{1,0},{2,3},{3,2},{7,6},{6,7},{5,4},{4,5},{12,13},{13,12},{1... | collective-permute-start | bytes 1966088 | tf_op jit(solution)/shard_map/ppermute | solution.py:800
  27.2 1.4 %collective-permute-start.1 = (f32[32,24,128]{2,1,0:T(8,128)S(1)}, f32[32,24,128]{2,1,0:T(8,128)S(1)}, u32[]{:S(2)}, u32[]{:S(2)}) collective-permute-start(f32[32,24,128]{2,1,0:T(8,128)S(1)} %slice.8.own), channel_id=1, source_target_pairs={{1,2},{2,1},{3,7},{7,3},{6,5},{5,6},{4,12},{12,4},{13,14},{14,13},... | collective-permute-start | bytes 1179656 | tf_op jit(solution)/shard_map/ppermute | solution.py:799
  27.9 2.8 %collective-permute-start.2 = (f32[32,16,128]{2,1,0:T(8,128)S(1)}, f32[32,16,128]{2,1,0:T(8,128)S(1)}, u32[]{:S(2)}, u32[]{:S(2)}) collective-permute-start(f32[32,16,128]{2,1,0:T(8,128)S(1)} %slice.9.own), channel_id=1, source_target_pairs={{1,2},{2,1},{3,7},{7,3},{6,5},{5,6},{4,12},{12,4},{13,14},{14,13},... | collective-permute-start | bytes 786440 | tf_op jit(solution)/shard_map/ppermute | solution.py:801
  33.6 22.4 %all-to-all-start.1 = ((f32[32,16,128]{2,1,0:T(8,128)}), f32[32,16,128]{2,1,0:T(8,128)S(1)}, u32[]{:S(2)}, u32[]{:S(2)}) async-start(f32[32,16,128]{2,1,0:T(8,128)} %get-tuple-element.22), calls=%async_computation.1 | async-start | bytes 524288 | tf_op jit(solution)/shard_map/all_to_all | solution.py:843
  45.4 3.9 %collective-permute-start.4 = (f32[8,16,128]{2,1,0:T(8,128)}, f32[8,16,128]{2,1,0:T(8,128)S(1)}, u32[]{:S(2)}, u32[]{:S(2)}) collective-permute-start(f32[8,16,128]{2,1,0:T(8,128)} %get-tuple-element.25), channel_id=1, source_target_pairs={{1,2},{2,1},{3,7},{7,3},{6,5},{5,6},{4,12},{12,4},{13,14},{14,13},... | collective-permute-start | bytes 196616 | tf_op jit(solution)/shard_map/ppermute | solution.py:844
  46.1 4.3 %collective-permute-start.3 = (f32[8,16,128]{2,1,0:T(8,128)}, f32[8,16,128]{2,1,0:T(8,128)S(1)}, u32[]{:S(2)}, u32[]{:S(2)}) collective-permute-start(f32[8,16,128]{2,1,0:T(8,128)} %get-tuple-element.25), channel_id=1, source_target_pairs={{0,1},{1,0},{2,3},{3,2},{7,6},{6,7},{5,4},{4,5},{12,13},{13,12},{1... | collective-permute-start | bytes 196616 | tf_op jit(solution)/shard_map/ppermute | solution.py:845
  49.3 6.7 %copy-start = (f32[8,16,128]{2,1,0:T(8,128)}, f32[8,16,128]{2,1,0:T(8,128)S(1)}, u32[]{:S(2)}) copy-start(f32[8,16,128]{2,1,0:T(8,128)S(1)} %collective-permute-done.4.far_hbm) | copy-start | bytes 196612
  50.4 5.6 %copy-start.1 = (f32[8,16,128]{2,1,0:T(8,128)}, f32[8,16,128]{2,1,0:T(8,128)S(1)}, u32[]{:S(2)}) copy-start(f32[8,16,128]{2,1,0:T(8,128)S(1)} %collective-permute-done.3.near_hbm) | copy-start | bytes 196612

commit v8 on v7

--- a/solution.py
+++ b/solution.py
@@ -566,18 +566,21 @@
     own, near, far,
     *refs,
 ):
-    state, cstate, message_hbm, packed_hbm = refs[:4]
-    scaled0, scaled1, cscaled0, cscaled1, v0, v1, e0, e1, rest, message, packed, done = refs[4:]
+    state, cstate, late, message_hbm, packed_hbm = refs[:5]
+    scaled0, scaled1, cscaled0, cscaled1, v0, v1, e0, e1, rest, message, packed, done = refs[5:]
     planes, width = face.shape[1], face.shape[3]
     coarse = planes // 4
     middle = slice(*INNER)
     held = [(face.at[:, :, middle, :], state.at[0:6])]
-    held += [(ref.at[:, middle, :], state.at[6 + k]) for k, ref in enumerate((inverse0, inverse1, scaled0, scaled1, v1))]
-    held += [(cface, cstate.at[0:6])]
-    held += [(ref, cstate.at[6 + k]) for k, ref in enumerate((cinverse0, cinverse1, cscaled0, cscaled1, e1))]
+    held += [
+        (inverse0.at[:, middle, :], state.at[6]),
+        (inverse1.at[:, middle, :], late.at[0]),
+        (scaled1.at[:, middle, :], late.at[1]),
+        (v1.at[:, middle, :], late.at[2]),
+    ]
     held += [(message, message_hbm)]
     copies = [pltpu.make_async_copy(ref, out, done.at[k]) for k, (ref, out) in enumerate(held)]
-    for copy in copies[:3] + copies[6:9]:
+    for copy in copies[:3]:
         copy.start()
     near_at, far_at = neighbour_rows(columns)
     places = ((own, 0, ROWS), (near, 3 * ROWS, near_at), (far, 0, far_at))
@@ -591,13 +594,19 @@
 
     arrays = ((0, first_pass), (ROWS, scaled_store(scaled1, inverse1)))
     unfold_slabs(places, arrays, planes)
-    for copy in copies[3:5]:
-        copy.start()
+    copies[3].start()
+    for x in range(planes):
+        state[7, x] = scaled0[x, middle, :]
+    for i in range(coarse):
+        for a in range(6):
+            cstate[a, i] = cface[a, i]
+        cstate[6, i] = cinverse0[i]
+        cstate[7, i] = cinverse1[i]
 
     renew(fine_flow, 1, v1, v0, face, inverse1, scaled1, (2, WIN - 2))
     renew(fine_flow, 0, v0, v1, face, inverse0, scaled0, (3, WIN - 3))
     renew(fine_flow, 1, v1, v0, face, inverse1, scaled1, (3, WIN - 3))
-    copies[5].start()
+    copies[4].start()
 
     even = coarse_low(0, width, INNER)
     for i in range(coarse):
@@ -610,13 +619,15 @@
         cscaled0[i, middle, :] = first
         e0[i, middle, :] = first
         cscaled1[i, middle, :] = jnp.where(even, fields[1], fields[0]) * cinverse1[i, middle, :]
-    for copy in copies[9:11]:
-        copy.start()
+    for i in range(coarse):
+        cstate[8, i] = cscaled0[i]
+        cstate[9, i] = cscaled1[i]
 
     renew(coarse_flow, 1, e1, e0, cface, cinverse1, cscaled1, wider(INNER, -1))
     renew(coarse_flow, 0, e0, e1, cface, cinverse0, cscaled0, wider(INNER, -2))
     renew(coarse_flow, 1, e1, e0, cface, cinverse1, cscaled1, wider(OWN, 1))
-    copies[11].start()
+    for i in range(coarse):
+        cstate[10, i] = e1[i]
 
     pick = picked(width)
     for i in range(coarse):
@@ -636,7 +647,7 @@
     for i in range(coarse):
         message[i, 0:ROWS, :] = jnp.where(first, e1[i, here, :], cscaled0[i, here, :])
         message[i, ROWS : 2 * ROWS, :] = cscaled1[i, here, :]
-    copies[12].start()
+    copies[5].start()
     for copy in copies:
         copy.wait()
     sent.wait()
@@ -644,16 +655,17 @@
 
 def up_kernel(
     columns,
-    gathered, state, cstate_hbm, near_hbm, far_hbm,
+    gathered, state, cstate, near_hbm, far_hbm, late_hbm,
     out,
-    cstate, v0, v1, e0, near, far, bshare, coarsest, spread, done,
+    late, cscaled0, cscaled1, e1, v0, v1, e0, near, far, bshare, coarsest, spread, done,
 ):
     planes, width = state.shape[1], state.shape[3]
     count = gathered.shape[0]
     rows = planes // 4
-    face, (inverse0, inverse1, scaled0, scaled1, field1) = state, [state.at[k] for k in range(6, 11)]
-    cface, (cinverse0, cinverse1, cscaled0, cscaled1, e1) = cstate, [cstate.at[k] for k in range(6, 11)]
-    held = ((cstate_hbm, cstate), (near_hbm, near), (far_hbm, far))
+    face, inverse0, scaled0 = state, state.at[6], state.at[7]
+    inverse1, scaled1, field1 = [late.at[k] for k in range(3)]
+    cface, (cinverse0, cinverse1, kept0, kept1, field) = cstate, [cstate.at[k] for k in range(6, 11)]
+    held = ((near_hbm, near), (far_hbm, far), (late_hbm, late))
     copies = [pltpu.make_async_copy(hbm, ref, done.at[k]) for k, (hbm, ref) in enumerate(held)]
     for copy in copies:
         copy.start()
@@ -698,14 +710,14 @@
                 bshare[colour, a, k] = shares[a]
             scaled[colour].append(source[colour][k + 1] * inverse)
 
-    fields = [[zero] + scaled[0] + [zero], None]
+    fields = [[zero] + scaled[0] + [zero], [zero] * (pairs + 2)]
     for step in range(1, 2 * BOTTOM_SWEEPS):
-        colour = step % 2
-        new = []
-        for k in range(pairs):
+        colour, skip = step % 2, (step + 1) // 2
+        new = list(fields[colour])
+        for k in range(skip, pairs - skip):
             sides = around_coarsest(fields[1 - colour], k, low[colour])
-            new.append(relax(scaled[colour][k], [bshare[colour, a, k] for a in range(6)], sides))
-        fields[colour] = [zero] + new + [zero]
+            new[k + 1] = relax(scaled[colour][k], [bshare[colour, a, k] for a in range(6)], sides)
+        fields[colour] = new
 
     start = 4 * REACH - ROWS // 2
     for k in range(WIN // 4):
@@ -713,7 +725,7 @@
         coarsest[2 * k * rows : (2 * k + 1) * rows, :] = jnp.where(low[0], a, b)
         coarsest[(2 * k + 1) * rows : (2 * k + 2) * rows, :] = jnp.where(low[0], b, a)
 
-    for copy in copies:
+    for copy in copies[:2]:
         copy.wait()
     near_at, far_at = neighbour_rows(columns)
     here = slice(*OWN)
@@ -722,7 +734,9 @@
         half = coarsest[pl.ds(i, WIN // 2, stride=rows), :]
         spread[pl.ds(0, WIN // 2, stride=2), :] = half
         spread[pl.ds(1, WIN // 2, stride=2), :] = half
-        e1[i, here, :] = e1[i, here, :] + spread[here, :]
+        e1[i, here, :] = field[i, here, :] + spread[here, :]
+        cscaled0[i, here, :] = kept0[i, here, :]
+        cscaled1[i, here, :] = kept1[i, here, :]
         for row, ref in ((near_at, near), (far_at, far)):
             mixed = ref[i, 0:ROWS, :]
             other = swap_lanes(mixed, 1)
@@ -736,6 +750,7 @@
     renew(coarse_flow, 0, e0, e1, cface, cinverse0, cscaled0, (3, WIN - 3))
     renew(coarse_flow, 1, e1, e0, cface, cinverse1, cscaled1, INNER)
 
+    copies[2].wait()
     even = coarse_low(0, width, INNER)
     for i in range(rows):
         a, b = e0[i, at(e0, INNER), :], e1[i, at(e1, INNER), :]
@@ -825,9 +840,9 @@
         name="weights",
     )(first_part, own_near, first_far)
 
-    first = near_outs((11, planes, height, width))
-    second = far_outs((11, coarse, WIN, width), letter, (count, 2 * coarse, width))
-    state, cstate, message, packed = pl.pallas_call(
+    first = near_outs((8, planes, height, width), (11, coarse, WIN, width))
+    second = far_outs((3, planes, height, width), letter, (count, 2 * coarse, width))
+    state, cstate, late, message, packed = pl.pallas_call(
         functools.partial(down_kernel, columns),
         out_shape=first[0] + second[0],
         out_specs=first[1] + second[1],
@@ -847,8 +862,8 @@
     cycle = pl.pallas_call(
         functools.partial(up_kernel, columns),
         out_shape=struct(count, 3 * ROWS, 128),
-        in_specs=[pl.BlockSpec(memory_space=pltpu.VMEM)] * 2 + [pl.BlockSpec(memory_space=pltpu.HBM)] * 3,
-        scratch_shapes=[vmem(11, *cplane)] + [vmem(*iplane)] * 2 + [vmem(*cplane)] + [vmem(*letter)] * 2 + [
+        in_specs=[pl.BlockSpec(memory_space=pltpu.VMEM)] * 3 + [pl.BlockSpec(memory_space=pltpu.HBM)] * 3,
+        scratch_shapes=[vmem(3, *iplane)] + [vmem(*cplane)] * 3 + [vmem(*iplane)] * 2 + [vmem(*cplane)] + [vmem(*letter)] * 2 + [
             vmem(2, 6, 2 * (2 * REACH + 1), coarse, width),
             vmem(WIN // 2 * coarse, width),
             vmem(WIN, width),
@@ -856,7 +871,7 @@
         ],
         compiler_params=params,
         name="up",
-    )(gathered, state, *in_hbm(cstate, message_near, message_far))
+    )(gathered, state, cstate, *in_hbm(message_near, message_far, late))
     back = lax.all_to_all(cycle, axes, 0, 0)
     return pl.pallas_call(
         functools.partial(unpack_kernel, order),

time: 75.6 us -> 75 us (level)
  no operation moved by 1% of the time
where the time goes in v8:
time: 75 us; the launch traced here: 74.8 us
  blocking collectives  40.4 us (54%)
  starting transfers between devices  17.1 us (23%)
  Pallas kernels  9.17 us (12%)
  waiting for transfers between devices  7.31 us (10%)
    all_to_all x1, blocking collectives, local_slabs(): own = lax.all_to_all(bricks, axes, 0, 0)  25 us
    all_to_all x1, blocking collectives, local_slabs(): back = lax.all_to_all(cycle, axes, 0, 0)  15.4 us
    all_to_all x1, starting transfers between devices, local_slabs(): gathered = lax.all_to_all(packed, axes, 0, 0)  11.8 us
    all_to_all x1, waiting for transfers between devices, local_slabs(): gathered = lax.all_to_all(packed, axes, 0, 0)  5.49 us
    ppermute x1, starting transfers between devices, local_slabs(): message_near = lax.ppermute(message, axes, near)  3.19 us
    pallas_call x1, Pallas kernels, local_slabs(): pl.pallas_call(functools.partial(down_kernel, columns), out_shape=first[0...  2.66 us
    pallas_call x1, Pallas kernels, local_slabs(): pl.pallas_call(functools.partial(up_kernel, columns), out_shape=struct(co...  2.57 us
    pallas_call x1, Pallas kernels, local_slabs(): pl.pallas_call(functools.partial(weights_kernel, columns), out_shape=near...  1.55 us
  transfers between devices with their start and end apart: 6, of which 3 were waited for; matrix products, arithmetic and copies ran while one was open for 0% of the time, Pallas kernels for 2%

profile of v8, /device:TPU:0, one launch (start us, length us, event | category | flops | bytes accessed | tf_op | source)
XLA Modules:
  0.0 74.8 jit_solution(13770583330387399956)
XLA Ops:
  0.6 1.4 %pack.1 = f32[32,40,128]{2,1,0:T(8,128)S(1)} custom-call(f32[4,32,512]{2,1,0:T(8,128)} %source_hbm.1, s32[4,32,512]{2,1,0:T(8,128)} %phase_hbm.1, f32[4,32,512]{2,1,0:T(8,128)} %guess_hbm.1), custom_call_target="tpu_custom_call" | custom-call | tf_op jit(solution)/shard_map/pack/pallas_call | solution.py:798
  2.1 25.0 %all_to_all.15 = f32[32,40,128]{2,1,0:T(8,128)S(1)} all-to-all(f32[32,40,128]{2,1,0:T(8,128)S(1)} %pack.1), channel_id=1, replica_groups=mesh['gx'=8,'yz'=4] {'gx','yz'}, dimensions={0} | all-to-all | bytes 1310720 | tf_op jit(solution)/shard_map/all_to_all | solution.py:812
  27.1 0.1 collective-permute-start
  27.2 0.7 collective-permute-start.1
  27.9 0.7 collective-permute-start.2
  28.6 0.0 collective-permute-done.1.far
  28.6 0.6 collective-permute-done.near
  29.2 1.6 %weights.1 = (f32[6,32,24,128]{3,2,1,0:T(8,128)S(1)}, f32[32,24,128]{2,1,0:T(8,128)S(1)}, f32[32,24,128]{2,1,0:T(8,128)S(1)}, f32[6,8,24,128]{3,2,1,0:T(8,128)S(...) custom-call(f32[32,24,128]{2,1,0:T(8,128)S(1)} %slice.8.own, ...), custom_call_target="tpu_custom_call" | custom-call | flops 20000000000 | bytes 100000000 | tf_op jit(solution)/shard_map/weights/pallas_call | solution.py:834
  30.8 0.0 collective-permute-done.2.far
  30.8 2.7 %down.1 = (f32[8,32,16,128]{3,2,1,0:T(8,128)S(1)}, f32[11,8,24,128]{3,2,1,0:T(8,128)S(1)}, f32[3,32,16,128]{3,2,1,0:T(8,128)}, f32[8,16,128]{2,1,0:T(8,128)}, f32[32,16,128]{2,1,0:T(8,128)}) custom-call(f32[6,32,24,128]{3,2,1,0:T(8,128)S(1)} %get-tuple-element.15.face, f32[32,24,128]{2,1,0:T(8,128)S(1)} %get-tuple-element.16.inverse0, ...), custom_call_target="tpu_custom_call" | custom-call | tf_op jit(solution)/shard_map/down/pallas_call | solution.py:845
  33.4 11.8 %all-to-all-start.1 = ((f32[32,16,128]{2,1,0:T(8,128)}), f32[32,16,128]{2,1,0:T(8,128)S(1)}, u32[]{:S(2)}, u32[]{:S(2)}) async-start(f32[32,16,128]{2,1,0:T(8,128)} %get-tuple-element.23), calls=%async_computation.1 | async-start | bytes 524288 | tf_op jit(solution)/shard_map/all_to_all | solution.py:858
  45.2 0.7 collective-permute-start.4
  45.9 3.2 %collective-permute-start.3 = (f32[8,16,128]{2,1,0:T(8,128)}, f32[8,16,128]{2,1,0:T(8,128)}, u32[]{:S(2)}, u32[]{:S(2)}) collective-permute-start(f32[8,16,128]{2,1,0:T(8,128)} %get-tuple-element.26), channel_id=1, source_target_pairs={{0,1},{1,0},{2,3},{3,2},{7,6},{6,7},{5,4},{4,5},{12,13},{13,12},{1... | collective-permute-start | bytes 196616 | tf_op jit(solution)/shard_map/ppermute | solution.py:860
  49.1 0.0 collective-permute-done.4.far_hbm
  49.1 0.0 copy-start
  49.1 1.2 %collective-permute-done.3.near_hbm = f32[8,16,128]{2,1,0:T(8,128)} collective-permute-done((f32[8,16,128]{2,1,0:T(8,128)}, f32[8,16,128]{2,1,0:T(8,128)}, u32[]{:S(2)}, u32[]{:S(2)}) %collective-permute-start.3) | collective-permute-done | bytes 65568 | tf_op jit(solution)/shard_map/ppermute | solution.py:860
  50.3 5.5 %all-to-all-done.1.gathered = f32[32,16,128]{2,1,0:T(8,128)S(1)} async-done(((f32[32,16,128]{2,1,0:T(8,128)}), f32[32,16,128]{2,1,0:T(8,128)S(1)}, u32[]{:S(2)}, u32[]{:S(2)}) %all-to-all-start.1) | async-done | bytes 262176 | tf_op jit(solution)/shard_map/all_to_all | solution.py:858
  55.8 0.0 copy-done
  55.8 2.6 %up.1 = f32[32,24,128]{2,1,0:T(8,128)S(1)} custom-call(f32[32,16,128]{2,1,0:T(8,128)S(1)} %all-to-all-done.1.gathered, f32[8,32,16,128]{3,2,1,0:T(8,128)S(1)} %get-tuple-element.24.state, f32[11,8,24,128]{3,2,1,0:T(8,128)S(1)} %get-tuple-element.25.cstate, f32[8,16,128]{2,1,0:T(8,128)} %collective-permute-done.3.near_hbm, f32[8,16,128]{2,1,0:T(8,128)} %copy-done, ...), custom_call_target="tpu_custom_call" | custom-call | tf_op jit(solution)/shard_map/up/pallas_call | solution.py:862
  58.4 15.4 %all_to_all.16.in_ref = f32[32,24,128]{2,1,0:T(8,128)S(1)} all-to-all(f32[32,24,128]{2,1,0:T(8,128)S(1)} %up.1), channel_id=1, replica_groups=mesh['gx'=8,'yz'=4] {'gx','yz'}, dimensions={0} | all-to-all | bytes 786432 | tf_op jit(solution)/shard_map/all_to_all | solution.py:875
  73.8 0.9 %unpack.1 = (f32[4,32,512]{2,1,0:T(8,128)}, f32[4,32,512]{2,1,0:T(8,128)}) custom-call(f32[32,24,128]{2,1,0:T(8,128)S(1)} %all_to_all.16.in_ref), custom_call_target="tpu_custom_call" | custom-call | tf_op jit(solution)/shard_map/unpack/pallas_call | solution.py:876
  (2 shorter events, 0.0 us)
Async XLA Ops:
  27.1 2.1 %collective-permute-start = (f32[32,40,128]{2,1,0:T(8,128)S(1)}, f32[32,40,128]{2,1,0:T(8,128)S(1)}, u32[]{:S(2)}, u32[]{:S(2)}) collective-permute-start(f32[32,40,128]{2,1,0:T(8,128)S(1)} %all_to_all.15), channel_id=1, source_target_pairs={{0,1},{1,0},{2,3},{3,2},{7,6},{6,7},{5,4},{4,5},{12,13},{13,12},{1... | collective-permute-start | bytes 1966088 | tf_op jit(solution)/shard_map/ppermute | solution.py:815
  27.2 1.4 %collective-permute-start.1 = (f32[32,24,128]{2,1,0:T(8,128)S(1)}, f32[32,24,128]{2,1,0:T(8,128)S(1)}, u32[]{:S(2)}, u32[]{:S(2)}) collective-permute-start(f32[32,24,128]{2,1,0:T(8,128)S(1)} %slice.8.own), channel_id=1, source_target_pairs={{1,2},{2,1},{3,7},{7,3},{6,5},{5,6},{4,12},{12,4},{13,14},{14,13},... | collective-permute-start | bytes 1179656 | tf_op jit(solution)/shard_map/ppermute | solution.py:814
  27.9 2.8 %collective-permute-start.2 = (f32[32,16,128]{2,1,0:T(8,128)S(1)}, f32[32,16,128]{2,1,0:T(8,128)S(1)}, u32[]{:S(2)}, u32[]{:S(2)}) collective-permute-start(f32[32,16,128]{2,1,0:T(8,128)S(1)} %slice.9.own), channel_id=1, source_target_pairs={{1,2},{2,1},{3,7},{7,3},{6,5},{5,6},{4,12},{12,4},{13,14},{14,13},... | collective-permute-start | bytes 786440 | tf_op jit(solution)/shard_map/ppermute | solution.py:816
  33.4 22.4 %all-to-all-start.1 = ((f32[32,16,128]{2,1,0:T(8,128)}), f32[32,16,128]{2,1,0:T(8,128)S(1)}, u32[]{:S(2)}, u32[]{:S(2)}) async-start(f32[32,16,128]{2,1,0:T(8,128)} %get-tuple-element.23), calls=%async_computation.1 | async-start | bytes 524288 | tf_op jit(solution)/shard_map/all_to_all | solution.py:858
  45.2 3.9 %collective-permute-start.4 = (f32[8,16,128]{2,1,0:T(8,128)}, f32[8,16,128]{2,1,0:T(8,128)S(1)}, u32[]{:S(2)}, u32[]{:S(2)}) collective-permute-start(f32[8,16,128]{2,1,0:T(8,128)} %get-tuple-element.26), channel_id=1, source_target_pairs={{1,2},{2,1},{3,7},{7,3},{6,5},{5,6},{4,12},{12,4},{13,14},{14,13},... | collective-permute-start | bytes 196616 | tf_op jit(solution)/shard_map/ppermute | solution.py:859
  45.9 4.4 %collective-permute-start.3 = (f32[8,16,128]{2,1,0:T(8,128)}, f32[8,16,128]{2,1,0:T(8,128)}, u32[]{:S(2)}, u32[]{:S(2)}) collective-permute-start(f32[8,16,128]{2,1,0:T(8,128)} %get-tuple-element.26), channel_id=1, source_target_pairs={{0,1},{1,0},{2,3},{3,2},{7,6},{6,7},{5,4},{4,5},{12,13},{13,12},{1... | collective-permute-start | bytes 196616 | tf_op jit(solution)/shard_map/ppermute | solution.py:860
  49.1 6.7 %copy-start = (f32[8,16,128]{2,1,0:T(8,128)}, f32[8,16,128]{2,1,0:T(8,128)S(1)}, u32[]{:S(2)}) copy-start(f32[8,16,128]{2,1,0:T(8,128)S(1)} %collective-permute-done.4.far_hbm) | copy-start | bytes 196612

commit v9 on v8

--- a/solution.py
+++ b/solution.py
@@ -247,11 +247,11 @@
     for device, slab in enumerate(order):
         base = 2 * ROWS * slab
         p0, p1 = in_ref[device, 0:ROWS, :], in_ref[device, ROWS : 2 * ROWS, :]
-        r0 = in_ref[device, 2 * ROWS : 3 * ROWS, :]
+        r0, r1 = in_ref[device, 2 * ROWS : 3 * ROWS, :], in_ref[device, 3 * ROWS : 4 * ROWS, :]
         turned[0, pl.ds(base, ROWS, stride=2), :] = jnp.where(even, p0, p1)
         turned[0, pl.ds(base + 1, ROWS, stride=2), :] = jnp.where(even, p1, p0)
-        turned[1, pl.ds(base, ROWS, stride=2), :] = jnp.where(even, r0, 0.0)
-        turned[1, pl.ds(base + 1, ROWS, stride=2), :] = jnp.where(even, 0.0, r0)
+        turned[1, pl.ds(base, ROWS, stride=2), :] = jnp.where(even, r0, r1)
+        turned[1, pl.ds(base + 1, ROWS, stride=2), :] = jnp.where(even, r1, r0)
     for a, ref in enumerate((pressure_ref, residual_ref)):
         ref[...] = turned[a].T.reshape(ref.shape)
 
@@ -431,10 +431,11 @@
         target[x, at(target, rows), :] = scaled[x, at(scaled, rows), :] + moved
 
 
-def rest_of(flow, v0, v1, face, inverse0, scaled0, x, rows):
-    factor = inverse0[x, at(inverse0, rows), :]
-    updated = scaled0[x, at(scaled0, rows), :] + factor * flow(0, face, v1, x, rows)
-    return (updated - v0[x, at(v0, rows), :]) / factor
+def rest_of(flow, colour, fields, face, inverses, sources, x, rows):
+    inverse, scaled, v = inverses[colour], sources[colour], fields[colour]
+    factor = inverse[x, at(inverse, rows), :]
+    updated = scaled[x, at(scaled, rows), :] + factor * flow(colour, face, fields[1 - colour], x, rows)
+    return (updated - v[x, at(v, rows), :]) / factor
 
 
 def one_over(diagonal):
@@ -612,8 +613,11 @@
     for i in range(coarse):
         fields = []
         for x in (4 * i, 4 * i + 2):
-            total = rest_of(fine_flow, v0, v1, face, inverse0, scaled0, x, INNER)
-            total = total + rest_of(fine_flow, v0, v1, face, inverse0, scaled0, x + 1, INNER)
+            total = 0.0
+            for plane in (x, x + 1):
+                for colour in (0, 1):
+                    level = ((v0, v1), face, (inverse0, inverse1), (scaled0, scaled1))
+                    total = total + rest_of(fine_flow, colour, *level, plane, INNER)
             fields.append(0.5 * (total + swap_lanes(total, 1)))
         first = jnp.where(even, fields[0], fields[1]) * cinverse0[i, middle, :]
         cscaled0[i, middle, :] = first
@@ -631,7 +635,8 @@
 
     pick = picked(width)
     for i in range(coarse):
-        rest[slice(*OWN), :] = rest_of(coarse_flow, e0, e1, cface, cinverse0, cscaled0, i, OWN)
+        level = ((e0, e1), cface, (cinverse0, cinverse1), (cscaled0, cscaled1))
+        rest[slice(*OWN), :] = rest_of(coarse_flow, 0, *level, i, OWN) + rest_of(coarse_flow, 1, *level, i, OWN)
         pair = pair_sum(rest)
         pair = 0.5 * (pair + swap_lanes(pair, 2))
         packed[0, i : i + 1, :] = jnp.sum(jnp.where(pick, pair, 0.0), axis=0, keepdims=True)
@@ -765,11 +770,13 @@
 
     for i in range(rows):
         planes_of = range(4 * i, 4 * i + 4)
-        rest = [rest_of(fine_flow, v0, v1, face, inverse0, scaled0, x, OWN) for x in planes_of]
+        level = ((v0, v1), face, (inverse0, inverse1), (scaled0, scaled1))
+        rest = [[rest_of(fine_flow, colour, *level, x, OWN) for x in planes_of] for colour in (0, 1)]
         for a, tiles in (
             (0, [v0[x, at(v0, OWN), :] for x in planes_of]),
             (1, [v1[x, at(v1, OWN), :] for x in planes_of]),
-            (2, rest),
+            (2, rest[0]),
+            (3, rest[1]),
         ):
             for j, tile in enumerate(swap_blocks(tiles)):
                 out[4 * i + j, a * ROWS : (a + 1) * ROWS, :] = tile
@@ -861,7 +868,7 @@
 
     cycle = pl.pallas_call(
         functools.partial(up_kernel, columns),
-        out_shape=struct(count, 3 * ROWS, 128),
+        out_shape=struct(count, 4 * ROWS, 128),
         in_specs=[pl.BlockSpec(memory_space=pltpu.VMEM)] * 3 + [pl.BlockSpec(memory_space=pltpu.HBM)] * 3,
         scratch_shapes=[vmem(3, *iplane)] + [vmem(*cplane)] * 3 + [vmem(*iplane)] * 2 + [vmem(*cplane)] + [vmem(*letter)] * 2 + [
             vmem(2, 6, 2 * (2 * REACH + 1), coarse, width),

time: 75 us -> 78.3 us (1.044)
  blocking collectives: 40.4 us -> 42.8 us
  Pallas kernels: 9.17 us -> 10.1 us
    all_to_all x1, blocking collectives: 15.4 us -> 17.8 us  [local_slabs(): back = lax.all_to_all(cycle, axes, 0, 0)]
where the time goes in v9:
time: 78.3 us; the launch traced here: 78 us
  blocking collectives  42.8 us (55%)
  starting transfers between devices  17.1 us (22%)
  Pallas kernels  10.1 us (13%)
  waiting for transfers between devices  7.31 us (9%)
    all_to_all x1, blocking collectives, local_slabs(): own = lax.all_to_all(bricks, axes, 0, 0)  25 us
    all_to_all x1, blocking collectives, local_slabs(): back = lax.all_to_all(cycle, axes, 0, 0)  17.8 us
    all_to_all x1, starting transfers between devices, local_slabs(): gathered = lax.all_to_all(packed, axes, 0, 0)  11.8 us
    all_to_all x1, waiting for transfers between devices, local_slabs(): gathered = lax.all_to_all(packed, axes, 0, 0)  5.49 us
    pallas_call x1, Pallas kernels, local_slabs(): pl.pallas_call(functools.partial(down_kernel, columns), out_shape=first[0...  3.33 us
    ppermute x1, starting transfers between devices, local_slabs(): message_near = lax.ppermute(message, axes, near)  3.19 us
    pallas_call x1, Pallas kernels, local_slabs(): pl.pallas_call(functools.partial(up_kernel, columns), out_shape=struct(co...  2.8 us
  transfers between devices with their start and end apart: 6, of which 3 were waited for; matrix products, arithmetic and copies ran while one was open for 0% of the time, Pallas kernels for 2%

profile of v9, /device:TPU:0, one launch (start us, length us, event | category | flops | bytes accessed | tf_op | source)
XLA Modules:
  0.0 78.0 jit_solution(7120362531484117287)
XLA Ops:
  0.6 1.4 %pack.1 = f32[32,40,128]{2,1,0:T(8,128)S(1)} custom-call(f32[4,32,512]{2,1,0:T(8,128)} %source_hbm.1, s32[4,32,512]{2,1,0:T(8,128)} %phase_hbm.1, f32[4,32,512]{2,1,0:T(8,128)} %guess_hbm.1), custom_call_target="tpu_custom_call" | custom-call | tf_op jit(solution)/shard_map/pack/pallas_call | solution.py:805
  2.1 25.0 %all_to_all.15 = f32[32,40,128]{2,1,0:T(8,128)S(1)} all-to-all(f32[32,40,128]{2,1,0:T(8,128)S(1)} %pack.1), channel_id=1, replica_groups=mesh['gx'=8,'yz'=4] {'gx','yz'}, dimensions={0} | all-to-all | bytes 1310720 | tf_op jit(solution)/shard_map/all_to_all | solution.py:819
  27.1 0.1 collective-permute-start
  27.2 0.7 collective-permute-start.1
  27.9 0.7 collective-permute-start.2
  28.6 0.0 collective-permute-done.1.far
  28.6 0.6 collective-permute-done.near
  29.2 1.6 %weights.1 = (f32[6,32,24,128]{3,2,1,0:T(8,128)S(1)}, f32[32,24,128]{2,1,0:T(8,128)S(1)}, f32[32,24,128]{2,1,0:T(8,128)S(1)}, f32[6,8,24,128]{3,2,1,0:T(8,128)S(...) custom-call(f32[32,24,128]{2,1,0:T(8,128)S(1)} %slice.8.own, ...), custom_call_target="tpu_custom_call" | custom-call | flops 20000000000 | bytes 100000000 | tf_op jit(solution)/shard_map/weights/pallas_call | solution.py:841
  30.8 0.0 collective-permute-done.2.far
  30.8 3.3 %down.1 = (f32[8,32,16,128]{3,2,1,0:T(8,128)S(1)}, f32[11,8,24,128]{3,2,1,0:T(8,128)S(1)}, f32[3,32,16,128]{3,2,1,0:T(8,128)}, f32[8,16,128]{2,1,0:T(8,128)}, f32[32,16,128]{2,1,0:T(8,128)}) custom-call(f32[6,32,24,128]{3,2,1,0:T(8,128)S(1)} %get-tuple-element.15.face, f32[32,24,128]{2,1,0:T(8,128)S(1)} %get-tuple-element.16.inverse0, ...), custom_call_target="tpu_custom_call" | custom-call | tf_op jit(solution)/shard_map/down/pallas_call | solution.py:852
  34.1 11.8 %all-to-all-start.1 = ((f32[32,16,128]{2,1,0:T(8,128)}), f32[32,16,128]{2,1,0:T(8,128)S(1)}, u32[]{:S(2)}, u32[]{:S(2)}) async-start(f32[32,16,128]{2,1,0:T(8,128)} %get-tuple-element.23), calls=%async_computation.1 | async-start | bytes 524288 | tf_op jit(solution)/shard_map/all_to_all | solution.py:865
  45.9 0.7 collective-permute-start.4
  46.6 3.2 %collective-permute-start.3 = (f32[8,16,128]{2,1,0:T(8,128)}, f32[8,16,128]{2,1,0:T(8,128)}, u32[]{:S(2)}, u32[]{:S(2)}) collective-permute-start(f32[8,16,128]{2,1,0:T(8,128)} %get-tuple-element.26), channel_id=1, source_target_pairs={{0,1},{1,0},{2,3},{3,2},{7,6},{6,7},{5,4},{4,5},{12,13},{13,12},{1... | collective-permute-start | bytes 196616 | tf_op jit(solution)/shard_map/ppermute | solution.py:867
  49.8 0.0 collective-permute-done.4.far_hbm
  49.8 0.0 copy-start
  49.8 1.2 %collective-permute-done.3.near_hbm = f32[8,16,128]{2,1,0:T(8,128)} collective-permute-done((f32[8,16,128]{2,1,0:T(8,128)}, f32[8,16,128]{2,1,0:T(8,128)}, u32[]{:S(2)}, u32[]{:S(2)}) %collective-permute-start.3) | collective-permute-done | bytes 65568 | tf_op jit(solution)/shard_map/ppermute | solution.py:867
  51.0 5.5 %all-to-all-done.1.gathered = f32[32,16,128]{2,1,0:T(8,128)S(1)} async-done(((f32[32,16,128]{2,1,0:T(8,128)}), f32[32,16,128]{2,1,0:T(8,128)S(1)}, u32[]{:S(2)}, u32[]{:S(2)}) %all-to-all-start.1) | async-done | bytes 262176 | tf_op jit(solution)/shard_map/all_to_all | solution.py:865
  56.5 0.0 copy-done
  56.5 2.8 %up.1 = f32[32,32,128]{2,1,0:T(8,128)S(1)} custom-call(f32[32,16,128]{2,1,0:T(8,128)S(1)} %all-to-all-done.1.gathered, f32[8,32,16,128]{3,2,1,0:T(8,128)S(1)} %get-tuple-element.24.state, f32[11,8,24,128]{3,2,1,0:T(8,128)S(1)} %get-tuple-element.25.cstate, f32[8,16,128]{2,1,0:T(8,128)} %collective-permute-done.3.near_hbm, f32[8,16,128]{2,1,0:T(8,128)} %copy-done, ...), custom_call_target="tpu_custom_call" | custom-call | tf_op jit(solution)/shard_map/up/pallas_call | solution.py:869
  59.3 17.8 %all_to_all.16.in_ref = f32[32,32,128]{2,1,0:T(8,128)S(1)} all-to-all(f32[32,32,128]{2,1,0:T(8,128)S(1)} %up.1), channel_id=1, replica_groups=mesh['gx'=8,'yz'=4] {'gx','yz'}, dimensions={0} | all-to-all | bytes 1048576 | tf_op jit(solution)/shard_map/all_to_all | solution.py:882
  77.1 0.9 %unpack.1 = (f32[4,32,512]{2,1,0:T(8,128)}, f32[4,32,512]{2,1,0:T(8,128)}) custom-call(f32[32,32,128]{2,1,0:T(8,128)S(1)} %all_to_all.16.in_ref), custom_call_target="tpu_custom_call" | custom-call | tf_op jit(solution)/shard_map/unpack/pallas_call | solution.py:883
  (2 shorter events, 0.0 us)
Async XLA Ops:
  27.1 2.1 %collective-permute-start = (f32[32,40,128]{2,1,0:T(8,128)S(1)}, f32[32,40,128]{2,1,0:T(8,128)S(1)}, u32[]{:S(2)}, u32[]{:S(2)}) collective-permute-start(f32[32,40,128]{2,1,0:T(8,128)S(1)} %all_to_all.15), channel_id=1, source_target_pairs={{0,1},{1,0},{2,3},{3,2},{7,6},{6,7},{5,4},{4,5},{12,13},{13,12},{1... | collective-permute-start | bytes 1966088 | tf_op jit(solution)/shard_map/ppermute | solution.py:822
  27.2 1.4 %collective-permute-start.1 = (f32[32,24,128]{2,1,0:T(8,128)S(1)}, f32[32,24,128]{2,1,0:T(8,128)S(1)}, u32[]{:S(2)}, u32[]{:S(2)}) collective-permute-start(f32[32,24,128]{2,1,0:T(8,128)S(1)} %slice.8.own), channel_id=1, source_target_pairs={{1,2},{2,1},{3,7},{7,3},{6,5},{5,6},{4,12},{12,4},{13,14},{14,13},... | collective-permute-start | bytes 1179656 | tf_op jit(solution)/shard_map/ppermute | solution.py:821
  27.9 2.8 %collective-permute-start.2 = (f32[32,16,128]{2,1,0:T(8,128)S(1)}, f32[32,16,128]{2,1,0:T(8,128)S(1)}, u32[]{:S(2)}, u32[]{:S(2)}) collective-permute-start(f32[32,16,128]{2,1,0:T(8,128)S(1)} %slice.9.own), channel_id=1, source_target_pairs={{1,2},{2,1},{3,7},{7,3},{6,5},{5,6},{4,12},{12,4},{13,14},{14,13},... | collective-permute-start | bytes 786440 | tf_op jit(solution)/shard_map/ppermute | solution.py:823
  34.1 22.4 %all-to-all-start.1 = ((f32[32,16,128]{2,1,0:T(8,128)}), f32[32,16,128]{2,1,0:T(8,128)S(1)}, u32[]{:S(2)}, u32[]{:S(2)}) async-start(f32[32,16,128]{2,1,0:T(8,128)} %get-tuple-element.23), calls=%async_computation.1 | async-start | bytes 524288 | tf_op jit(solution)/shard_map/all_to_all | solution.py:865
  45.9 3.9 %collective-permute-start.4 = (f32[8,16,128]{2,1,0:T(8,128)}, f32[8,16,128]{2,1,0:T(8,128)S(1)}, u32[]{:S(2)}, u32[]{:S(2)}) collective-permute-start(f32[8,16,128]{2,1,0:T(8,128)} %get-tuple-element.26), channel_id=1, source_target_pairs={{1,2},{2,1},{3,7},{7,3},{6,5},{5,6},{4,12},{12,4},{13,14},{14,13},... | collective-permute-start | bytes 196616 | tf_op jit(solution)/shard_map/ppermute | solution.py:866
  46.6 4.4 %collective-permute-start.3 = (f32[8,16,128]{2,1,0:T(8,128)}, f32[8,16,128]{2,1,0:T(8,128)}, u32[]{:S(2)}, u32[]{:S(2)}) collective-permute-start(f32[8,16,128]{2,1,0:T(8,128)} %get-tuple-element.26), channel_id=1, source_target_pairs={{0,1},{1,0},{2,3},{3,2},{7,6},{6,7},{5,4},{4,5},{12,13},{13,12},{1... | collective-permute-start | bytes 196616 | tf_op jit(solution)/shard_map/ppermute | solution.py:867
  49.8 6.7 %copy-start = (f32[8,16,128]{2,1,0:T(8,128)}, f32[8,16,128]{2,1,0:T(8,128)S(1)}, u32[]{:S(2)}) copy-start(f32[8,16,128]{2,1,0:T(8,128)S(1)} %collective-permute-done.4.far_hbm) | copy-start | bytes 196612

commit v10 on v8

--- a/solution.py
+++ b/solution.py
@@ -597,11 +597,6 @@
     copies[3].start()
     for x in range(planes):
         state[7, x] = scaled0[x, middle, :]
-    for i in range(coarse):
-        for a in range(6):
-            cstate[a, i] = cface[a, i]
-        cstate[6, i] = cinverse0[i]
-        cstate[7, i] = cinverse1[i]
 
     renew(fine_flow, 1, v1, v0, face, inverse1, scaled1, (2, WIN - 2))
     renew(fine_flow, 0, v0, v1, face, inverse0, scaled0, (3, WIN - 3))
@@ -619,15 +614,10 @@
         cscaled0[i, middle, :] = first
         e0[i, middle, :] = first
         cscaled1[i, middle, :] = jnp.where(even, fields[1], fields[0]) * cinverse1[i, middle, :]
-    for i in range(coarse):
-        cstate[8, i] = cscaled0[i]
-        cstate[9, i] = cscaled1[i]
 
     renew(coarse_flow, 1, e1, e0, cface, cinverse1, cscaled1, wider(INNER, -1))
     renew(coarse_flow, 0, e0, e1, cface, cinverse0, cscaled0, wider(INNER, -2))
     renew(coarse_flow, 1, e1, e0, cface, cinverse1, cscaled1, wider(OWN, 1))
-    for i in range(coarse):
-        cstate[10, i] = e1[i]
 
     pick = picked(width)
     for i in range(coarse):
@@ -648,6 +638,14 @@
         message[i, 0:ROWS, :] = jnp.where(first, e1[i, here, :], cscaled0[i, here, :])
         message[i, ROWS : 2 * ROWS, :] = cscaled1[i, here, :]
     copies[5].start()
+    for i in range(coarse):
+        for a in range(6):
+            cstate[a, i] = cface[a, i]
+        cstate[6, i] = cinverse0[i]
+        cstate[7, i] = cinverse1[i]
+        cstate[8, i] = cscaled0[i]
+        cstate[9, i] = cscaled1[i]
+        cstate[10, i] = e1[i]
     for copy in copies:
         copy.wait()
     sent.wait()

time: 75 us -> 75.1 us (level)
  no operation moved by 1% of the time
where the time goes in v10:
time: 75.1 us; the launch traced here: 74.8 us
  blocking collectives  40.4 us (54%)
  starting transfers between devices  17.1 us (23%)
  Pallas kernels  9.25 us (12%)
  waiting for transfers between devices  7.31 us (10%)
    all_to_all x1, blocking collectives, local_slabs(): own = lax.all_to_all(bricks, axes, 0, 0)  25 us
    all_to_all x1, blocking collectives, local_slabs(): back = lax.all_to_all(cycle, axes, 0, 0)  15.4 us
    all_to_all x1, starting transfers between devices, local_slabs(): gathered = lax.all_to_all(packed, axes, 0, 0)  11.8 us
    all_to_all x1, waiting for transfers between devices, local_slabs(): gathered = lax.all_to_all(packed, axes, 0, 0)  5.49 us
    ppermute x1, starting transfers between devices, local_slabs(): message_near = lax.ppermute(message, axes, near)  3.19 us
    pallas_call x1, Pallas kernels, local_slabs(): pl.pallas_call(functools.partial(down_kernel, columns), out_shape=first[0...  2.74 us
    pallas_call x1, Pallas kernels, local_slabs(): pl.pallas_call(functools.partial(up_kernel, columns), out_shape=struct(co...  2.57 us
    pallas_call x1, Pallas kernels, local_slabs(): pl.pallas_call(functools.partial(weights_kernel, columns), out_shape=near...  1.55 us
  transfers between devices with their start and end apart: 6, of which 3 were waited for; matrix products, arithmetic and copies ran while one was open for 0% of the time, Pallas kernels for 2%

profile of v10, /device:TPU:0, one launch (start us, length us, event | category | flops | bytes accessed | tf_op | source)
XLA Modules:
  0.0 74.8 jit_solution(7905071041098728366)
XLA Ops:
  0.6 1.4 %pack.1 = f32[32,40,128]{2,1,0:T(8,128)S(1)} custom-call(f32[4,32,512]{2,1,0:T(8,128)} %source_hbm.1, s32[4,32,512]{2,1,0:T(8,128)} %phase_hbm.1, f32[4,32,512]{2,1,0:T(8,128)} %guess_hbm.1), custom_call_target="tpu_custom_call" | custom-call | tf_op jit(solution)/shard_map/pack/pallas_call | solution.py:796
  2.1 25.0 %all_to_all.15 = f32[32,40,128]{2,1,0:T(8,128)S(1)} all-to-all(f32[32,40,128]{2,1,0:T(8,128)S(1)} %pack.1), channel_id=1, replica_groups=mesh['gx'=8,'yz'=4] {'gx','yz'}, dimensions={0} | all-to-all | bytes 1310720 | tf_op jit(solution)/shard_map/all_to_all | solution.py:810
  27.1 0.1 collective-permute-start
  27.2 0.7 collective-permute-start.1
  27.9 0.7 collective-permute-start.2
  28.6 0.0 collective-permute-done.1.far
  28.6 0.6 collective-permute-done.near
  29.2 1.6 %weights.1 = (f32[6,32,24,128]{3,2,1,0:T(8,128)S(1)}, f32[32,24,128]{2,1,0:T(8,128)S(1)}, f32[32,24,128]{2,1,0:T(8,128)S(1)}, f32[6,8,24,128]{3,2,1,0:T(8,128)S(...) custom-call(f32[32,24,128]{2,1,0:T(8,128)S(1)} %slice.8.own, ...), custom_call_target="tpu_custom_call" | custom-call | flops 20000000000 | bytes 100000000 | tf_op jit(solution)/shard_map/weights/pallas_call | solution.py:832
  30.8 0.0 collective-permute-done.2.far
  30.8 2.7 %down.1 = (f32[8,32,16,128]{3,2,1,0:T(8,128)S(1)}, f32[11,8,24,128]{3,2,1,0:T(8,128)S(1)}, f32[3,32,16,128]{3,2,1,0:T(8,128)}, f32[8,16,128]{2,1,0:T(8,128)}, f32[32,16,128]{2,1,0:T(8,128)}) custom-call(f32[6,32,24,128]{3,2,1,0:T(8,128)S(1)} %get-tuple-element.15.face, f32[32,24,128]{2,1,0:T(8,128)S(1)} %get-tuple-element.16.inverse0, ...), custom_call_target="tpu_custom_call" | custom-call | tf_op jit(solution)/shard_map/down/pallas_call | solution.py:843
  33.5 11.8 %all-to-all-start.1 = ((f32[32,16,128]{2,1,0:T(8,128)}), f32[32,16,128]{2,1,0:T(8,128)S(1)}, u32[]{:S(2)}, u32[]{:S(2)}) async-start(f32[32,16,128]{2,1,0:T(8,128)} %get-tuple-element.23), calls=%async_computation.1 | async-start | bytes 524288 | tf_op jit(solution)/shard_map/all_to_all | solution.py:856
  45.3 0.7 collective-permute-start.4
  46.0 3.2 %collective-permute-start.3 = (f32[8,16,128]{2,1,0:T(8,128)}, f32[8,16,128]{2,1,0:T(8,128)}, u32[]{:S(2)}, u32[]{:S(2)}) collective-permute-start(f32[8,16,128]{2,1,0:T(8,128)} %get-tuple-element.26), channel_id=1, source_target_pairs={{0,1},{1,0},{2,3},{3,2},{7,6},{6,7},{5,4},{4,5},{12,13},{13,12},{1... | collective-permute-start | bytes 196616 | tf_op jit(solution)/shard_map/ppermute | solution.py:858
  49.2 0.0 collective-permute-done.4.far_hbm
  49.2 0.0 copy-start
  49.2 1.2 %collective-permute-done.3.near_hbm = f32[8,16,128]{2,1,0:T(8,128)} collective-permute-done((f32[8,16,128]{2,1,0:T(8,128)}, f32[8,16,128]{2,1,0:T(8,128)}, u32[]{:S(2)}, u32[]{:S(2)}) %collective-permute-start.3) | collective-permute-done | bytes 65568 | tf_op jit(solution)/shard_map/ppermute | solution.py:858
  50.4 5.5 %all-to-all-done.1.gathered = f32[32,16,128]{2,1,0:T(8,128)S(1)} async-done(((f32[32,16,128]{2,1,0:T(8,128)}), f32[32,16,128]{2,1,0:T(8,128)S(1)}, u32[]{:S(2)}, u32[]{:S(2)}) %all-to-all-start.1) | async-done | bytes 262176 | tf_op jit(solution)/shard_map/all_to_all | solution.py:856
  55.9 0.0 copy-done
  55.9 2.6 %up.1 = f32[32,24,128]{2,1,0:T(8,128)S(1)} custom-call(f32[32,16,128]{2,1,0:T(8,128)S(1)} %all-to-all-done.1.gathered, f32[8,32,16,128]{3,2,1,0:T(8,128)S(1)} %get-tuple-element.24.state, f32[11,8,24,128]{3,2,1,0:T(8,128)S(1)} %get-tuple-element.25.cstate, f32[8,16,128]{2,1,0:T(8,128)} %collective-permute-done.3.near_hbm, f32[8,16,128]{2,1,0:T(8,128)} %copy-done, ...), custom_call_target="tpu_custom_call" | custom-call | tf_op jit(solution)/shard_map/up/pallas_call | solution.py:860
  58.5 15.4 %all_to_all.16.in_ref = f32[32,24,128]{2,1,0:T(8,128)S(1)} all-to-all(f32[32,24,128]{2,1,0:T(8,128)S(1)} %up.1), channel_id=1, replica_groups=mesh['gx'=8,'yz'=4] {'gx','yz'}, dimensions={0} | all-to-all | bytes 786432 | tf_op jit(solution)/shard_map/all_to_all | solution.py:873
  73.9 0.9 %unpack.1 = (f32[4,32,512]{2,1,0:T(8,128)}, f32[4,32,512]{2,1,0:T(8,128)}) custom-call(f32[32,24,128]{2,1,0:T(8,128)S(1)} %all_to_all.16.in_ref), custom_call_target="tpu_custom_call" | custom-call | tf_op jit(solution)/shard_map/unpack/pallas_call | solution.py:874
  (2 shorter events, 0.0 us)
Async XLA Ops:
  27.1 2.1 %collective-permute-start = (f32[32,40,128]{2,1,0:T(8,128)S(1)}, f32[32,40,128]{2,1,0:T(8,128)S(1)}, u32[]{:S(2)}, u32[]{:S(2)}) collective-permute-start(f32[32,40,128]{2,1,0:T(8,128)S(1)} %all_to_all.15), channel_id=1, source_target_pairs={{0,1},{1,0},{2,3},{3,2},{7,6},{6,7},{5,4},{4,5},{12,13},{13,12},{1... | collective-permute-start | bytes 1966088 | tf_op jit(solution)/shard_map/ppermute | solution.py:813
  27.2 1.4 %collective-permute-start.1 = (f32[32,24,128]{2,1,0:T(8,128)S(1)}, f32[32,24,128]{2,1,0:T(8,128)S(1)}, u32[]{:S(2)}, u32[]{:S(2)}) collective-permute-start(f32[32,24,128]{2,1,0:T(8,128)S(1)} %slice.8.own), channel_id=1, source_target_pairs={{1,2},{2,1},{3,7},{7,3},{6,5},{5,6},{4,12},{12,4},{13,14},{14,13},... | collective-permute-start | bytes 1179656 | tf_op jit(solution)/shard_map/ppermute | solution.py:812
  27.9 2.8 %collective-permute-start.2 = (f32[32,16,128]{2,1,0:T(8,128)S(1)}, f32[32,16,128]{2,1,0:T(8,128)S(1)}, u32[]{:S(2)}, u32[]{:S(2)}) collective-permute-start(f32[32,16,128]{2,1,0:T(8,128)S(1)} %slice.9.own), channel_id=1, source_target_pairs={{1,2},{2,1},{3,7},{7,3},{6,5},{5,6},{4,12},{12,4},{13,14},{14,13},... | collective-permute-start | bytes 786440 | tf_op jit(solution)/shard_map/ppermute | solution.py:814
  33.5 22.4 %all-to-all-start.1 = ((f32[32,16,128]{2,1,0:T(8,128)}), f32[32,16,128]{2,1,0:T(8,128)S(1)}, u32[]{:S(2)}, u32[]{:S(2)}) async-start(f32[32,16,128]{2,1,0:T(8,128)} %get-tuple-element.23), calls=%async_computation.1 | async-start | bytes 524288 | tf_op jit(solution)/shard_map/all_to_all | solution.py:856
  45.3 3.9 %collective-permute-start.4 = (f32[8,16,128]{2,1,0:T(8,128)}, f32[8,16,128]{2,1,0:T(8,128)S(1)}, u32[]{:S(2)}, u32[]{:S(2)}) collective-permute-start(f32[8,16,128]{2,1,0:T(8,128)} %get-tuple-element.26), channel_id=1, source_target_pairs={{1,2},{2,1},{3,7},{7,3},{6,5},{5,6},{4,12},{12,4},{13,14},{14,13},... | collective-permute-start | bytes 196616 | tf_op jit(solution)/shard_map/ppermute | solution.py:857
  46.0 4.4 %collective-permute-start.3 = (f32[8,16,128]{2,1,0:T(8,128)}, f32[8,16,128]{2,1,0:T(8,128)}, u32[]{:S(2)}, u32[]{:S(2)}) collective-permute-start(f32[8,16,128]{2,1,0:T(8,128)} %get-tuple-element.26), channel_id=1, source_target_pairs={{0,1},{1,0},{2,3},{3,2},{7,6},{6,7},{5,4},{4,5},{12,13},{13,12},{1... | collective-permute-start | bytes 196616 | tf_op jit(solution)/shard_map/ppermute | solution.py:858
  49.2 6.7 %copy-start = (f32[8,16,128]{2,1,0:T(8,128)}, f32[8,16,128]{2,1,0:T(8,128)S(1)}, u32[]{:S(2)}) copy-start(f32[8,16,128]{2,1,0:T(8,128)S(1)} %collective-permute-done.4.far_hbm) | copy-start | bytes 196612
